TPU v7x, 32 devices: a whole 2x2x4 slice. The times are simulated.
32 devices in a mesh: stream: 8 (over y, x, core), shard: 4 (over z).
Axes of the slice: x: 2, y: 2, z: 4, core: 2. Of those that a mesh axis runs over, the one named last changes fastest.
Arguments:
- frames_in: bfloat16 [96, 4, 12, 5120], P('stream', None, None, 'shard'), may hold values from -6 to 6
- kept_state: float32 [96, 80, 64, 128], P('stream', 'shard'), may hold values from -6 to 6
- moved_to: int32 [96], P('stream'), may hold values from 0 to 95, as said below
- xz_weight: bfloat16 [5120, 2, 5120], P('stream', None, 'shard'), may hold values from -0.078125 to 0.078125
- side_weight: bfloat16 [5120, 336], P('stream'), may hold values from -0.01953125 to 0.01953125
- xz_mask: int32 [40, 2, 40], replicated, may hold values 0 or 1
- dt_bias: float32 [80], P('shard'), may hold values from -1 to 1
- decay_rate: float32 [80], P('shard'), may hold values from 0.00625 to 0.25
- skip_gain: float32 [80], P('shard'), may hold values from 0.5 to 1.5
- norm_gain: float32 [5120], P('shard'), may hold values from 0.1 to 1.9
- out_weight: bfloat16 [5120, 5120], P('stream', 'shard'), may hold values from -0.078125 to 0.078125
- out_mask: int32 [40, 40], replicated, may hold values 0 or 1
Outputs:
- mixed: bfloat16 [96, 4, 12, 5120], P('stream', None, None, 'shard')
- carry_state: float32 [96, 80, 64, 128], P('stream', 'shard')
Inputs may be any that keep to these rules, and one draw needn't show every extreme that they name: `moved_to`: A permutation of the slots; the 12 old slots of index i of stream go, exactly 3 each, to the 4 indices i + 1, i + 2, i + 3 and i + 4 of stream (counted modulo 8).
All inputs are finite; a program needn't handle non-finite values.
Results may differ from a plain program's by a relative error of at most 0.025.
Values may be sent and summed in bfloat16 or wider, within the bound.
No kernel may reach another device: no remote copies, remote signals or barrier semaphores. Data moves between devices by JAX's collectives and lax.ppermute only.
A program may use at most 192 MiB of HBM per device.

v0:
```python
import jax
import jax.numpy as jnp
from jax import lax
from jax.sharding import PartitionSpec as P

NSTATE = 128
NORM_GROUPS = 16
BLOCK = 128
FRAMES = 4
MOST = 3
DINNER = 5120


def frame_step(head_inputs, input_mix, output_mix, step_sizes, decay_rate, skip_gain, carry_state):
    highest = lax.Precision.HIGHEST
    length = head_inputs.shape[1]
    decays = -decay_rate * step_sizes
    cumulative = jnp.cumsum(decays, axis=1)
    causal = (jnp.arange(length)[:, None] >= jnp.arange(length)[None, :])[None, :, :, None]
    between = cumulative[:, :, None, :] - cumulative[:, None, :, :]
    weights = jnp.where(causal, jnp.exp(jnp.where(causal, between, 0.0)), 0.0)
    scores = jnp.einsum("sln,smn->slm", output_mix, input_mix, precision=highest)
    mixing = scores[:, :, :, None] * weights * step_sizes[:, None, :, :]
    inside = jnp.einsum("slmh,smhp->slhp", mixing, head_inputs, precision=highest)
    carried = jnp.exp(cumulative)[:, :, :, None] * jnp.einsum(
        "sln,shpn->slhp", output_mix, carry_state, precision=highest
    )
    outputs = inside + carried + skip_gain[None, None, :, None] * head_inputs
    to_end = jnp.exp(cumulative[:, -1:, :] - cumulative) * step_sizes
    carry_state = jnp.exp(cumulative[:, -1, :])[:, :, None, None] * carry_state + jnp.einsum(
        "slh,slhp,sln->shpn", to_end, head_inputs, input_mix, precision=highest
    )
    return (outputs, carry_state)


def column_table(column_ids, block_total):
    return (jnp.arange(block_total)[:, None] == (column_ids // BLOCK)[None, :]).astype(jnp.float32)


def row_table(panel_rows, block_rows):
    row_ids = jnp.arange(panel_rows)
    return ((row_ids // BLOCK)[:, None] == jnp.arange(block_rows)[None, :]).astype(jnp.float32)


def on_device(
    frames_in,
    kept_state,
    moved_to,
    xz_weight,
    side_weight,
    xz_mask,
    dt_bias,
    decay_rate,
    skip_gain,
    norm_gain,
    out_weight,
    out_mask,
):
    device_count = lax.axis_size("stream")
    shard_pos = lax.axis_index("shard")
    slots = kept_state.shape[0]
    target_dev = moved_to // slots
    target_slot = moved_to % slots
    slot_ids = jnp.arange(slots)
    same_dest = (target_dev[:, None] == target_dev[None, :]) & (
        slot_ids[:, None] > slot_ids[None, :]
    )
    ranking = jnp.sum(same_dest.astype(jnp.int32), axis=1)
    position = target_dev * MOST + ranking
    send_states = (
        jnp.zeros((device_count * MOST,) + kept_state.shape[1:], jnp.float32)
        .at[position]
        .set(kept_state)
    )
    send_slots = jnp.full((device_count * MOST,), -1, jnp.int32).at[position].set(target_slot)
    got_states, got_slots = (
        lax.all_to_all(
            send_states.astype(jnp.bfloat16), "stream", split_axis=0, concat_axis=0, tiled=True
        ).astype(send_states.dtype),
        lax.all_to_all(send_slots, "stream", split_axis=0, concat_axis=0, tiled=True),
    )
    landing = jnp.where(got_slots >= 0, got_slots, slots)
    carry_state = jnp.zeros_like(kept_state).at[landing].set(got_states, mode="drop")
    patch_len = frames_in.shape[2]
    local_rows = frames_in.reshape(-1, frames_in.shape[3])
    features = lax.all_gather(local_rows, "shard", axis=1, tiled=True)
    row_count = features.shape[0]
    width_local = xz_weight.shape[2]
    block_rows = xz_mask.shape[0]
    column_ids = shard_pos * width_local + jnp.arange(width_local)
    col_onehot = column_table(column_ids, xz_mask.shape[2])
    xz_keep = jnp.einsum("rgc,cl->rgl", xz_mask.astype(jnp.float32), col_onehot).reshape(
        block_rows, 2 * width_local
    )
    out_keep = jnp.dot(out_mask.astype(jnp.float32), col_onehot)
    panel = lax.all_gather(xz_weight, "stream", axis=0, tiled=True)
    panel_rows = panel.shape[0]
    keep_mask = jnp.dot(row_table(panel_rows, block_rows), xz_keep).astype(jnp.bfloat16)
    masked = panel.reshape(panel_rows, 2 * width_local) * keep_mask
    columns = features
    xz_total = jnp.dot(columns, masked, preferred_element_type=jnp.float32)
    columns = features
    side_total = jnp.dot(
        columns,
        lax.all_gather(side_weight, "stream", axis=0, tiled=True),
        preferred_element_type=jnp.float32,
    )
    head_count = dt_bias.shape[0]
    head_size = width_local // head_count
    head_inputs = xz_total[:, :width_local].reshape(slots, FRAMES, patch_len, head_count, head_size)
    gate_inputs = xz_total[:, width_local:]
    input_mix = side_total[:, :NSTATE].reshape(slots, FRAMES, patch_len, NSTATE)
    output_mix = side_total[:, NSTATE : 2 * NSTATE].reshape(slots, FRAMES, patch_len, NSTATE)
    step_raw = lax.dynamic_slice_in_dim(
        side_total, 2 * NSTATE + shard_pos * head_count, head_count, 1
    )
    step_sizes = jax.nn.softplus(step_raw + dt_bias).reshape(slots, FRAMES, patch_len, head_count)
    results = []
    for frame_index in range(FRAMES):
        outputs, carry_state = frame_step(
            head_inputs[:, frame_index],
            input_mix[:, frame_index],
            output_mix[:, frame_index],
            step_sizes[:, frame_index],
            decay_rate,
            skip_gain,
            carry_state,
        )
        results.append(outputs)
    scanned = jnp.stack(results, axis=1).reshape(row_count, width_local)
    gated = (scanned * jax.nn.silu(gate_inputs)).reshape(row_count, -1, DINNER // NORM_GROUPS)
    mean_square = jnp.mean(gated * gated, axis=2, keepdims=True)
    normed = (
        (gated * lax.rsqrt(mean_square + 1e-05)).reshape(row_count, width_local) * norm_gain
    ).astype(jnp.bfloat16)
    panel = lax.all_gather(out_weight, "stream", axis=0, tiled=True)
    panel_rows = panel.shape[0]
    keep_mask = jnp.dot(row_table(panel_rows, block_rows), out_keep).astype(jnp.bfloat16)
    partial_out = lax.dot_general(
        normed, panel * keep_mask, (((1,), (1,)), ((), ())), preferred_element_type=jnp.float32
    )
    mixed = lax.psum_scatter(
        partial_out.astype(jnp.bfloat16), "shard", scatter_dimension=1, tiled=True
    )
    return (mixed.reshape(slots, FRAMES, patch_len, -1), carry_state)


def solution(mesh):
    placed = (
        P("stream", None, None, "shard"),
        P("stream", "shard", None, None),
        P("stream"),
        P("stream", None, "shard"),
        P("stream", None),
        P(),
        P("shard"),
        P("shard"),
        P("shard"),
        P("shard"),
        P("stream", "shard"),
        P(),
    )
    return jax.shard_map(
        on_device,
        mesh=mesh,
        in_specs=placed,
        out_specs=(P("stream", None, None, "shard"), P("stream", "shard", None, None)),
        check_vma=False,
    )
```

profile of v0, /device:TPU:0, one launch (start us, length us, event | category | flops | bytes accessed | tf_op | source)
XLA Modules:
  0.0 641.9 jit_solution(1544657725376834883)
XLA Ops:
  13.7 5.2 all-to-all-start
  18.9 7.5 %broadcast_in_dim.127 = f32[24,20,64,128]{3,2,1,0:T(8,128)} broadcast(f32[]{:T(128)} %constant.81.clone.1), dimensions={} | broadcast | bytes 15728644 | tf_op jit(solution)/shard_map/broadcast_in_dim | solution.py:71
  26.3 13.5 %scatter_fusion = f32[24,20,64,128]{3,2,1,0:T(8,128)} fusion(f32[24,20,64,128]{3,2,1,0:T(8,128)} %broadcast_in_dim.127, s32[12]{0:T(128)S(1)} %compare_select_fusion.3, f32[12,20,64,128]{3,2,1,0:T(8,128)} %param.13), kind=kCustom, calls=%fused_computation.1 | custom fusion | bytes 23593008 | tf_op jit(solution)/shard_map/scatter | solution.py:73
  39.8 11.0 %convert_element_type.33 = bf16[24,20,64,128]{3,2,1,0:T(8,128)(2,1)} convert(f32[24,20,64,128]{3,2,1,0:T(8,128)} %scatter_fusion) | non-fusion elementwise | flops 3932160 | bytes 23592960 | tf_op jit(solution)/shard_map/convert_element_type | solution.py:78
  60.1 84.3 %all-to-all-done.1 = bf16[24,20,64,128]{3,2,1,0:T(8,128)(2,1)} async-done(((bf16[24,20,64,128]{3,2,1,0:T(8,128)(2,1)}), bf16[24,20,64,128]{3,2,1,0:T(8,128)(2,1)}, u32[]{:S(2)}, u32[]{:S(2)}) %all-to-all-start.1) | async-done | bytes 7864352 | tf_op jit(solution)/shard_map/all_to_all | solution.py:77
  144.4 10.7 %convert_element_type.34 = f32[24,20,64,128]{3,2,1,0:T(8,128)} convert(bf16[24,20,64,128]{3,2,1,0:T(8,128)(2,1)} %all-to-all-done.1) | non-fusion elementwise | flops 3932160 | bytes 23592960 | tf_op jit(solution)/shard_map/convert_element_type | solution.py:79
  159.3 24.1 %scatter_fusion.1 = f32[12,20,64,128]{3,2,1,0:T(8,128)} fusion(f32[12,20,64,128]{3,2,1,0:T(8,128)} %broadcast_in_dim.66, s32[24]{0:T(128)S(1)} %fusion.133, f32[24,20,64,128]{3,2,1,0:T(8,128)} %convert_element_type.34), kind=kCustom, calls=%fused_computation.2 | custom fusion | bytes 47186016 | tf_op jit(solution)/shard_map/scatter | solution.py:83
  183.4 6.6 %fusion.147 = f32[576,336]{0,1:T(8,128)S(1)} fusion(bf16[576,5120]{1,0:T(8,128)(2,1)} %all-gather.7.cloned.1.call-done, bf16[5120,336]{0,1:T(8,128)(2,1)} %all-gather.9.cloned.1.call-done), kind=kOutput, calls=%fused_computation.202 | convolution fusion | flops 1981808640 | bytes 10113024 | tf_op jit(solution)/shard_map/dot_general | solution.py:103
  207.5 79.6 %all-gather.5.cloned.1.call-done = bf16[5120,2,1280]{2,1,0:T(2,128)(2,1)} async-done(((bf16[640,2,1280]{2,1,0:T(2,128)(2,1)}), bf16[5120,2,1280]{2,1,0:T(2,128)(2,1)}) %all-gather.5.cloned.1.call-update) | async-done | bytes 26214416 | tf_op jit(solution)/shard_map/all_gather | solution.py:96
  287.1 18.7 %copy.390 = bf16[640,8,2,1280]{3,1,2,0:T(8,128)(2,1)} copy(bf16[640,8,2,1280]{3,2,1,0:T(2,128)(2,1)} %bitcast.222) | data formatting | bytes 52428800
  305.8 28.5 %fusion.3 = f32[576,2560]{1,0:T(8,128)} fusion(bf16[576,5120]{1,0:T(8,128)(2,1)} %all-gather.7.cloned.1.call-done, bf16[5120,2560]{1,0:T(8,128)(2,1)} %bitcast.223, bf16[40,2560]{1,0:T(8,128)(2,1)S(1)} %bitcast.226, s32[5120]{0:T(1024)S(1)} %copy-done.29), kind=kOutput, calls=%fused_computation.14 | convolution fusion | flops 16161382400 | bytes 38236160 | tf_op jit(solution)/shard_map/dot_general | solution.py:101
  357.1 19.1 %fusion.13 = f32[12,1,12,20,64]{4,2,3,0,1:T(8,128)S(1)} fusion(f32[12,20,64,12]{2,3,1,0:T(8,128)S(1)} %fusion.39, f32[12,1,12,20,64]{4,3,2,1,0:T(8,128)S(1)} %get-tuple-element.18, f32[12,20,64,128]{3,2,1,0:T(8,128)S(1)} %bitcast.221, f32[20]{0:T(128)S(1)} %copy-done.32, f32[12,12,20]{1,2,0:T(8,128)S(1)} %copy-done.10, f32[12,4,12,128]{3,2,1,0:T(8,128)S(1)} %copy-done.3), kind=kOutput, calls=%fused_computation.33 | convolution fusion | flops 283852800 | bytes 12583424 | tf_op jit(solution)/shard_map/sln,shpn->slhp/dot_general | solution.py:25
  376.1 14.7 %multiply_add_fusion.3 = f32[12,20,64,128]{3,2,1,0:T(8,128)S(1)} fusion(f32[12,20,64,128]{3,2,1,0:T(8,128)S(1)} %bitcast.221, f32[12,20]{1,0:T(8,128)S(1)} %fusion.129, f32[12,1,12,20,64]{4,3,2,1,0:T(8,128)S(1)} %get-tuple-element.18, f32[12,12,20]{1,2,0:T(8,128)S(1)} %copy.337, f32[12,4,12,128]{3,2,1,0:T(8,128)S(1)} %reshape.173), kind=kOutput, calls=%fused_computation.12 | convolution fusion | flops 287232000 | bytes 17752064 | tf_op jit(solution)/shard_map/slh,slhp,sln->shpn/dot_general | solution.py:30
  390.8 19.9 %fusion.11 = f32[12,1,12,20,64]{4,2,3,0,1:T(8,128)} fusion(f32[12,20,64,12]{2,3,1,0:T(8,128)S(1)} %fusion.32, f32[12,1,12,20,64]{4,3,2,1,0:T(8,128)S(1)} %get-tuple-element.17, f32[12,20,64,128]{3,2,1,0:T(8,128)S(1)} %multiply_add_fusion.3, f32[12,12,20]{1,2,0:T(8,128)S(1)} %copy-done.11, f32[20]{0:T(128)S(1)} %copy-done.32, ...), kind=kOutput, calls=%fused_computation.30 | convolution fusion | flops 283852800 | bytes 12583424 | tf_op jit(solution)/shard_map/sln,shpn->slhp/dot_general | solution.py:25
  410.8 14.9 %multiply_add_fusion.2 = f32[12,20,64,128]{3,2,1,0:T(8,128)S(1)} fusion(f32[12,20,64,128]{3,2,1,0:T(8,128)S(1)} %multiply_add_fusion.3, f32[12,20]{1,0:T(8,128)S(1)} %fusion.130, f32[12,1,12,20,64]{4,3,2,1,0:T(8,128)S(1)} %get-tuple-element.17, f32[12,12,20]{1,2,0:T(8,128)S(1)} %copy-done.6, f32[12,4,12,128]{3,2,1,0:T(8,128)S(1)} %reshape.173), kind=kOutput, calls=%fused_computation.11 | convolution fusion | flops 287232000 | bytes 17752064 | tf_op jit(solution)/shard_map/slh,slhp,sln->shpn/dot_general | solution.py:30
  425.7 18.6 %fusion.9 = f32[12,1,12,20,64]{4,2,3,0,1:T(8,128)S(1)} fusion(f32[12,20,64,12]{2,3,1,0:T(8,128)S(1)} %copy-done.5, f32[12,1,12,20,64]{4,3,2,1,0:T(8,128)S(1)} %get-tuple-element.16, f32[12,20,64,128]{3,2,1,0:T(8,128)S(1)} %multiply_add_fusion.2, f32[12,12,20]{1,2,0:T(8,128)S(1)} %copy-done.9, f32[20]{0:T(128)S(1)} %copy-done.32, ...), kind=kOutput, calls=%fused_computation.27 | convolution fusion | flops 283852800 | bytes 12583424 | tf_op jit(solution)/shard_map/sln,shpn->slhp/dot_general | solution.py:25
  444.4 14.7 %multiply_add_fusion.1 = f32[12,20,64,128]{3,2,1,0:T(8,128)S(1)} fusion(f32[12,20,64,128]{3,2,1,0:T(8,128)S(1)} %multiply_add_fusion.2, f32[12,20]{1,0:T(8,128)S(1)} %fusion.131, f32[12,1,12,20,64]{4,3,2,1,0:T(8,128)S(1)} %get-tuple-element.16, f32[12,12,20]{1,2,0:T(8,128)S(1)} %copy-done.7, f32[12,4,12,128]{3,2,1,0:T(8,128)S(1)} %reshape.173), kind=kOutput, calls=%fused_computation.10 | convolution fusion | flops 287232000 | bytes 17752064 | tf_op jit(solution)/shard_map/slh,slhp,sln->shpn/dot_general | solution.py:30
  459.1 18.8 %fusion.7 = f32[12,1,12,20,64]{4,2,3,0,1:T(8,128)S(1)} fusion(f32[12,20,64,12]{2,3,1,0:T(8,128)S(1)} %copy-done.4, f32[12,1,12,20,64]{4,3,2,1,0:T(8,128)S(1)} %get-tuple-element.19, f32[12,20,64,128]{3,2,1,0:T(8,128)S(1)} %multiply_add_fusion.1, f32[12,12,20]{1,2,0:T(8,128)S(1)} %copy-done.8, f32[20]{0:T(128)S(1)} %copy-done.32, ...), kind=kOutput, calls=%fused_computation.24 | convolution fusion | flops 283852800 | bytes 12583424 | tf_op jit(solution)/shard_map/sln,shpn->slhp/dot_general | solution.py:25
  479.0 5.4 copy.356
  484.5 6.4 reshape.175
  490.8 5.1 fusion.140
  507.1 19.2 %convolution_convert_fusion.2 = bf16[576,5120]{1,0:T(8,128)(2,1)} fusion(bf16[5120,1280]{1,0:T(8,128)(2,1)} %all-gather.11.cloned.1.call-done, bf16[1280,40]{0,1:T(8,128)(2,1)S(1)} %copy-done.23, f32[576,1280]{1,0:T(8,128)} %copy.358, f32[1280]{0:T(1024)S(1)} %copy-done.34, s32[5120]{0:T(1024)S(1)} %copy-done.30, f32[576,1280]{1,0:T(8,128)} %reshape.175, ...), kind=kOutput, calls=%fused_computation.13 | convolution fusion | flops 8089640960 | bytes 27980800 | tf_op jit(solution)/shard_map/dot_general | solution.py:139
  527.3 17.7 %multiply_add_fusion = f32[12,20,64,128]{3,2,1,0:T(8,128)} fusion(f32[12,20,64,128]{3,2,1,0:T(8,128)} %copy-done, f32[12,20]{1,0:T(8,128)S(1)} %fusion.132, f32[12,1,12,20,64]{4,3,2,1,0:T(8,128)S(1)} %get-tuple-element.19, f32[12,12,20]{1,2,0:T(8,128)S(1)} %copy.359, f32[12,4,12,128]{3,2,1,0:T(8,128)S(1)} %reshape.173), kind=kOutput, calls=%fused_computation.9 | convolution fusion | flops 287232000 | bytes 17752064 | tf_op jit(solution)/shard_map/slh,slhp,sln->shpn/dot_general | solution.py:30
  545.0 85.9 %reduce-scatter.2.cloned.1.call-done = bf16[576,1280]{1,0:T(8,128)(2,1)} async-done(((bf16[576,5120]{1,0:T(8,128)(2,1)}), bf16[576,1280]{1,0:T(8,128)(2,1)}) %reduce-scatter.2.cloned.1.call-update) | async-done | bytes 1474576 | tf_op jit(solution)/shard_map/reduce_scatter | solution.py:142
  (181 shorter events, 77.1 us)
Async XLA Ops:
  7.2 176.3 %all-gather.9.cloned.1.call-start = ((), (), s32[]{:S(2)}) async-start(), calls=%async_computation.5 | async-start | bytes 3870720 | tf_op jit(solution)/shard_map/all_gather | solution.py:105
  7.9 175.5 %all-gather.7.cloned.1.call-start = ((), (), s32[]{:S(2)}) async-start(), calls=%async_computation.4 | async-start | bytes 7372800 | tf_op jit(solution)/shard_map/all_gather | solution.py:86
  11.4 275.7 %all-gather.5.cloned.1.call-start = ((), (), s32[]{:S(2)}) async-start(), calls=%async_computation.3 | async-start | bytes 29491200 | tf_op jit(solution)/shard_map/all_gather | solution.py:96
  13.7 37.1 %all-to-all-start = ((s32[8,3,1]{1,2,0:T(1,128)}), s32[8,3,1]{1,2,0:T(1,128)S(1)}, u32[]{:S(2)}, u32[]{:S(2)}) async-start(s32[8,3,1]{1,2,0:T(1,128)} %bitcast.11), calls=%async_computation | async-start | bytes 8192 | tf_op jit(solution)/shard_map/all_to_all | solution.py:80
  50.8 5.7 copy-start.36
  50.8 5.7 copy-start.28
  50.8 93.5 %all-to-all-start.1 = ((bf16[24,20,64,128]{3,2,1,0:T(8,128)(2,1)}), bf16[24,20,64,128]{3,2,1,0:T(8,128)(2,1)}, u32[]{:S(2)}, u32[]{:S(2)}) async-start(bf16[24,20,64,128]{3,2,1,0:T(8,128)(2,1)} %convert_element_type.33), calls=%async_computation.1 | async-start | bytes 15728640 | tf_op jit(solution)/shard_map/all_to_all | solution.py:77
  55.9 451.2 %all-gather.11.cloned.1.call-start = ((), (), s32[]{:S(2)}) async-start(), calls=%async_computation.6 | async-start | bytes 14745600 | tf_op jit(solution)/shard_map/all_gather | solution.py:136
  56.5 574.5 %reduce-scatter.2.cloned.1.call-start = ((), (), s32[]{:S(2)}) async-start(), calls=%async_computation.7 | async-start | bytes 7372800 | tf_op jit(solution)/shard_map/reduce_scatter | solution.py:142
  183.4 6.6 %copy-start.33 = (f32[20]{0:T(128)S(1)}, f32[20]{0:T(128)}, u32[]{:S(2)}) copy-start(f32[20]{0:T(128)} %param.18) | copy-start | bytes 244
  199.2 106.6 %copy-start.2 = (f32[12,4,12,128]{3,2,1,0:T(8,128)}, f32[12,4,12,128]{3,2,1,0:T(8,128)S(1)}, u32[]{:S(2)}) copy-start(f32[12,4,12,128]{3,2,1,0:T(8,128)S(1)} %reshape.172) | copy-start | bytes 884740
  287.1 18.7 %copy-start.14 = (bf16[2,5,8,1280]{3,2,0,1:T(8,128)(2,1)S(1)}, bf16[2,5,8,1280]{3,2,0,1:T(8,128)(2,1)}, u32[]{:S(2)}) copy-start(bf16[2,5,8,1280]{3,2,0,1:T(8,128)(2,1)} %copy.389) | copy-start | bytes 614404
  287.1 18.7 %copy-start.29 = (s32[5120]{0:T(1024)S(1)}, s32[5120]{0:T(1024)}, u32[]{:S(2)}) copy-start(s32[5120]{0:T(1024)} %add_select_fusion) | copy-start | bytes 61444
  346.7 10.4 %slice-start = ((s8[7864320]{0:T(1024)(128)(4,1)}), s8[4194304]{0:T(1024)(128)(4,1)S(1)}, s32[]{:S(2)}) async-start(s8[7864320]{0:T(1024)(128)(4,1)} %bitcast.220), calls=%async_computation.8 | async-start | bytes 8388608
  349.3 7.7 %slice-start.1 = ((s8[7864320]{0:T(1024)(128)(4,1)}), s8[3670016]{0:T(1024)(128)(4,1)S(1)}, s32[]{:S(2)}) async-start(s8[7864320]{0:T(1024)(128)(4,1)} %bitcast.220), calls=%async_computation.9 | async-start | bytes 7340032
  376.1 14.7 %copy-start.11 = (f32[12,12,20]{1,2,0:T(8,128)S(1)}, f32[12,12,20]{1,2,0:T(8,128)}, u32[]{:S(2)}) copy-start(f32[12,12,20]{1,2,0:T(8,128)} %copy.336) | copy-start | bytes 34564
  390.8 20.0 %copy-start.6 = (f32[12,12,20]{1,2,0:T(8,128)S(1)}, f32[12,12,20]{1,2,0:T(8,128)}, u32[]{:S(2)}) copy-start(f32[12,12,20]{1,2,0:T(8,128)} %copy.346) | copy-start | bytes 34564
  410.8 14.9 %copy-start.5 = (f32[12,20,64,12]{2,3,1,0:T(8,128)S(1)}, f32[12,20,64,12]{2,3,1,0:T(8,128)}, u32[]{:S(2)}) copy-start(f32[12,20,64,12]{2,3,1,0:T(8,128)} %fusion.24) | copy-start | bytes 2211844
  410.8 14.9 %copy-start.9 = (f32[12,12,20]{1,2,0:T(8,128)S(1)}, f32[12,12,20]{1,2,0:T(8,128)}, u32[]{:S(2)}) copy-start(f32[12,12,20]{1,2,0:T(8,128)} %copy.345) | copy-start | bytes 34564
  425.7 18.6 %copy-start.7 = (f32[12,12,20]{1,2,0:T(8,128)S(1)}, f32[12,12,20]{1,2,0:T(8,128)}, u32[]{:S(2)}) copy-start(f32[12,12,20]{1,2,0:T(8,128)} %copy.355) | copy-start | bytes 34564
  444.4 14.7 %copy-start.4 = (f32[12,20,64,12]{2,3,1,0:T(8,128)S(1)}, f32[12,20,64,12]{2,3,1,0:T(8,128)}, u32[]{:S(2)}) copy-start(f32[12,20,64,12]{2,3,1,0:T(8,128)} %fusion.16) | copy-start | bytes 2211844
  444.4 14.7 %copy-start.8 = (f32[12,12,20]{1,2,0:T(8,128)S(1)}, f32[12,12,20]{1,2,0:T(8,128)}, u32[]{:S(2)}) copy-start(f32[12,12,20]{1,2,0:T(8,128)} %copy.354) | copy-start | bytes 34564
  459.1 18.8 %copy-start = (f32[12,20,64,128]{3,2,1,0:T(8,128)}, f32[12,20,64,128]{3,2,1,0:T(8,128)S(1)}, u32[]{:S(2)}) copy-start(f32[12,20,64,128]{3,2,1,0:T(8,128)S(1)} %multiply_add_fusion.1) | copy-start | bytes 23592964
  459.1 18.8 %copy-start.1 = (f32[12,1,12,20,64]{4,2,3,0,1:T(8,128)S(1)}, f32[12,1,12,20,64]{4,2,3,0,1:T(8,128)}, u32[]{:S(2)}) copy-start(f32[12,1,12,20,64]{4,2,3,0,1:T(8,128)} %fusion.11) | copy-start | bytes 2211844
  (23 other events, 68.3 us)
Sparse Core Ops, SparseCore 0:
  9.9 36.1 all-gather.8
  48.3 108.8 all-gather.6
  159.1 127.9 all-gather.4
  288.9 74.3 all-gather.10
  526.4 104.5 reduce-scatter.1
where the time goes:
time: 648 us; the launch traced here: 642 us
  waiting for transfers between devices  252 us (39%)
  matrix products  210 us (32%)
  local copies, waits for them, and re-layouts  122 us (19%)
  other arithmetic  33.3 us (5%)
  between operations  14.7 us (2%)
  starting transfers between devices  10.4 us (2%)
    reduce_scatter x1, waiting for transfers between devices, on_device(): lax.psum_scatter(partial_out.astype(jnp.bfloat16), 'shard', scatter_dimen...  85.9 us
    all_to_all x1, waiting for transfers between devices, on_device(): lax.all_to_all(send_states.astype(jnp.bfloat16), 'stream', split_axis=0,...  84.3 us
    all_gather x1, waiting for transfers between devices, on_device(): panel = lax.all_gather(xz_weight, 'stream', axis=0, tiled=True)  79.6 us
    dot_general x4, matrix products, frame_step(): jnp.einsum('sln,shpn->slhp', output_mix, carry_state, precision=highest)  76.4 us
    dot_general x4, matrix products, frame_step(): jnp.einsum('slh,slhp,sln->shpn', to_end, head_inputs, input_mix, precisio...  62 us
    dot_general x1, matrix products, on_device(): xz_total = jnp.dot(columns, masked, preferred_element_type=jnp.float32)  28.5 us
    scatter x1, local copies, waits for them, and re-layouts, on_device(): jnp.zeros_like(kept_state).at[landing].set(got_states, mode='drop')  24.1 us
    unnamed x85, local copies, waits for them, and re-layouts  23.2 us
  transfers between devices with their start and end apart: 7, of which 3 were waited for; matrix products, arithmetic and copies ran while one was open for 53% of the time, Pallas kernels for 0%

commit v1 on v0

--- a/solution.py
+++ b/solution.py
@@ -1,6 +1,10 @@
+import functools
+
 import jax
 import jax.numpy as jnp
 from jax import lax
+from jax.experimental import pallas as pl
+from jax.experimental.pallas import tpu as pltpu
 from jax.sharding import PartitionSpec as P
 
 NSTATE = 128
@@ -42,7 +46,7 @@
     return ((row_ids // BLOCK)[:, None] == jnp.arange(block_rows)[None, :]).astype(jnp.float32)
 
 
-def on_device(
+def general(
     frames_in,
     kept_state,
     moved_to,
@@ -145,6 +149,491 @@
     return (mixed.reshape(slots, FRAMES, patch_len, -1), carry_state)
 
 
+HEADDIM = 64
+XZ_SHARE = 0.66
+OUT_SHARE = 0.72
+BF16 = jnp.bfloat16
+F32 = jnp.float32
+MIB = 1 << 20
+
+
+def params(limit=48 * MIB):
+    return pltpu.CompilerParams(vmem_limit_bytes=limit)
+
+
+def cost(flops, nbytes):
+    return pl.CostEstimate(flops=int(flops), bytes_accessed=int(nbytes), transcendentals=0)
+
+
+def dot_f32(left, right):
+    return jnp.dot(left, right, precision=lax.Precision.HIGHEST, preferred_element_type=F32)
+
+
+def dot_nt(left, right):
+    return lax.dot_general(left, right, (((1,), (1,)), ((), ())), preferred_element_type=F32)
+
+
+def pack_kernel(half, block_rows, groups, columns, mask_columns, at_ref, mask_ref, x_ref, a_ref, b_ref):
+    panel, shard = at_ref[0], at_ref[1]
+    count = jnp.int32(0)
+    for row in range(block_rows):
+        for group in range(groups):
+            for column in range(columns):
+                place = ((panel * block_rows + row) * groups + group) * mask_columns + shard * columns + column
+                keep = mask_ref[place] != 0
+                low = (group * columns + column) * BLOCK
+                rows = slice(row * BLOCK, (row + 1) * BLOCK)
+
+                @pl.when(keep & (count < half))
+                def _(count=count, low=low, rows=rows):
+                    a_ref[count] = x_ref[rows, low : low + BLOCK]
+
+                @pl.when(keep & (count >= half))
+                def _(count=count, low=low, rows=rows):
+                    b_ref[count - half] = x_ref[rows, low : low + BLOCK]
+
+                count = count + keep.astype(jnp.int32)
+
+
+def pack(at, mask, panel, groups, half):
+    rows, width = panel.shape
+    columns = width // groups // BLOCK
+    mask_columns = mask.shape[-1]
+    packed = jax.ShapeDtypeStruct((half, BLOCK, BLOCK), BF16)
+    smem = pl.BlockSpec(memory_space=pltpu.SMEM)
+    vmem = pl.BlockSpec(memory_space=pltpu.VMEM)
+    return pl.pallas_call(
+        functools.partial(pack_kernel, half, rows // BLOCK, groups, columns, mask_columns),
+        out_shape=(packed, packed),
+        in_specs=[smem, smem, vmem],
+        out_specs=(vmem, vmem),
+        compiler_params=params(),
+        cost_estimate=cost(0, 2 * rows * width * 2),
+    )(at, mask.reshape(-1), panel)
+
+
+def spread_kernel(half, block_rows, groups, columns, mask_columns, at_ref, mask_ref, a_ref, b_ref, *rest):
+    out_ref, count_ref = rest[-2:]
+    row = pl.program_id(0)
+    panel, shard = at_ref[0], at_ref[1]
+
+    @pl.when(row == 0)
+    def _():
+        count_ref[0] = 0
+
+    count = count_ref[0]
+    for group in range(groups):
+        for column in range(columns):
+            place = ((panel * block_rows + row) * groups + group) * mask_columns + shard * columns + column
+            keep = mask_ref[place] != 0
+            low = (group * columns + column) * BLOCK
+
+            @pl.when(keep & (count < half))
+            def _(count=count, low=low):
+                out_ref[0, :, low : low + BLOCK] = a_ref[count]
+
+            @pl.when(keep & (count >= half))
+            def _(count=count, low=low):
+                out_ref[0, :, low : low + BLOCK] = b_ref[count - half]
+
+            @pl.when(jnp.logical_not(keep))
+            def _(low=low):
+                out_ref[0, :, low : low + BLOCK] = jnp.zeros((BLOCK, BLOCK), BF16)
+
+            count = count + keep.astype(jnp.int32)
+    count_ref[0] = count
+
+
+def spread(at, mask, a, b, groups, shape, before):
+    _, rows, width = shape
+    half = a.shape[0]
+    columns = width // groups // BLOCK
+    whole = pl.BlockSpec((half, BLOCK, BLOCK), lambda r, at, mask: (0, 0, 0))
+    return pl.pallas_call(
+        functools.partial(spread_kernel, half, rows // BLOCK, groups, columns, mask.shape[-1]),
+        grid_spec=pltpu.PrefetchScalarGridSpec(
+            num_scalar_prefetch=2,
+            grid=(rows // BLOCK,),
+            in_specs=[whole, whole] + ([] if before is None else [pl.BlockSpec(memory_space=pl.ANY)]),
+            out_specs=pl.BlockSpec((1, BLOCK, width), lambda r, at, mask: (at[2], r, 0)),
+            scratch_shapes=[pltpu.SMEM((1,), jnp.int32)],
+        ),
+        out_shape=jax.ShapeDtypeStruct(shape, BF16),
+        input_output_aliases={} if before is None else {4: 0},
+        compiler_params=params(),
+        cost_estimate=cost(0, 3 * rows * width * 2),
+    )(at, mask.reshape(-1), a, b, *(() if before is None else (before,)))
+
+
+def product_kernel(count, *refs):
+    base = refs[2 * count] if len(refs) > 2 * count + 1 else None
+    total = jnp.zeros(refs[-1].shape, F32) if base is None else base[...]
+    for step in range(count):
+        total = total + jnp.dot(refs[step][...], refs[count + step][0], preferred_element_type=F32)
+    refs[-1][...] = total
+
+
+def product(features, dense, first, base, tile=256):
+    count = len(features)
+    rows, depth = features[0].shape
+    width = dense.shape[2]
+    out = pl.BlockSpec((rows, tile), lambda n: (0, n))
+    return pl.pallas_call(
+        functools.partial(product_kernel, count),
+        grid=(width // tile,),
+        in_specs=[pl.BlockSpec((rows, depth), lambda n: (0, 0))] * count
+        + [pl.BlockSpec((1, depth, tile), lambda n, i=i: (first + i, 0, n)) for i in range(count)]
+        + ([] if base is None else [out]),
+        out_specs=out,
+        out_shape=jax.ShapeDtypeStruct((rows, width), F32),
+        input_output_aliases={} if base is None else {2 * count: 0},
+        compiler_params=params(),
+        cost_estimate=cost(2 * rows * depth * width * count, count * depth * width * 2 + 8 * rows * width),
+    )(*features, *([dense] * count), *(() if base is None else (base,)))
+
+
+def side_kernel(count, per, at_ref, side_ref, *refs):
+    total = jnp.zeros(refs[-1].shape, F32)
+    depth = side_ref.shape[2]
+    for step in range(count):
+        plane = lax.rem(at_ref[1] + (count - step), count)
+        for part in range(per):
+            total = total + dot_nt(refs[step][:, part * depth : (part + 1) * depth], side_ref[plane * per + part])
+    refs[-1][...] = total
+
+
+def side_product(at, side, features):
+    count, (rows, width) = len(features), features[0].shape
+    smem = pl.BlockSpec(memory_space=pltpu.SMEM)
+    vmem = pl.BlockSpec(memory_space=pltpu.VMEM)
+    columns = side.shape[1]
+    return pl.pallas_call(
+        functools.partial(side_kernel, count, side.shape[0] // count),
+        in_specs=[smem, vmem] + [vmem] * count,
+        out_specs=vmem,
+        out_shape=jax.ShapeDtypeStruct((rows, columns), F32),
+        compiler_params=params(),
+        cost_estimate=cost(2 * rows * width * count * columns, count * width * (rows + columns) * 2),
+    )(at, side, *features)
+
+
+def pick_kernel(order_ref, x_ref, out_ref):
+    out_ref[...] = x_ref[...].astype(out_ref.dtype)
+
+
+def pick(order, states):
+    count, block = order.shape[0], (1,) + states.shape[1:]
+    return pl.pallas_call(
+        pick_kernel,
+        grid_spec=pltpu.PrefetchScalarGridSpec(
+            num_scalar_prefetch=1,
+            grid=(count,),
+            in_specs=[pl.BlockSpec(block, lambda i, order: (order[i], 0, 0))],
+            out_specs=pl.BlockSpec(block, lambda i, order: (i, 0, 0)),
+        ),
+        out_shape=jax.ShapeDtypeStruct((count,) + states.shape[1:], BF16),
+        compiler_params=params(),
+        cost_estimate=cost(0, count * states.shape[1] * states.shape[2] * 6),
+    )(order, states)
+
+
+def scan_kernel(heads, group_width, slots_ref, xz_ref, side_ref, state_ref, rows_ref, pick_ref, *rest):
+    normed_ref, carry_ref = rest[-2:]
+    length, width = normed_ref.shape
+    head_inputs = xz_ref[:, :width]
+    gate_inputs = xz_ref[:, width:]
+    input_mix = side_ref[:, :NSTATE].astype(BF16)
+    output_mix = side_ref[:, NSTATE : 2 * NSTATE].astype(BF16)
+    bias, decay, skip, gain = (rows_ref[i : i + 1, :] for i in range(4))
+    raw = dot_f32(side_ref[:, 2 * NSTATE :], pick_ref[...]) + bias
+    steps = jnp.maximum(raw, 0.0) + jnp.log1p(jnp.exp(-jnp.abs(raw)))
+    token = lax.broadcasted_iota(jnp.int32, (length, length), 0)
+    earlier = lax.broadcasted_iota(jnp.int32, (length, length), 1)
+    lower = (token >= earlier).astype(F32)
+    cumulative = dot_f32(lower, -(steps * decay))
+    lane = lax.broadcasted_iota(jnp.int32, (length, width), 1) & (HEADDIM - 1)
+    line = lax.broadcasted_iota(jnp.int32, (length, width), 0)
+    own = lane == line
+    cum_row = jnp.sum(jnp.where(own, cumulative, 0.0), axis=0, keepdims=True)
+    step_row = jnp.sum(jnp.where(own, steps, 0.0), axis=0, keepdims=True)
+    last = cumulative[length - 1 : length, :]
+    mixing = jnp.exp(jnp.where(lane <= line, cumulative - cum_row, -1e30)) * step_row
+    half = lax.broadcasted_iota(jnp.int32, (length, 2 * HEADDIM), 1) < HEADDIM
+    spare = jnp.zeros((HEADDIM - length, NSTATE), BF16)
+    twice = jnp.concatenate([input_mix, spare, input_mix, spare], axis=0)
+    scores = dot_nt(output_mix, twice)
+    inputs16 = head_inputs.astype(BF16)
+    inside = []
+    for pair in range(heads // 2):
+        low = pair * 2 * HEADDIM
+        inputs = inputs16[:, low : low + 2 * HEADDIM]
+        zero = jnp.zeros_like(inputs)
+        pad = jnp.zeros((HEADDIM - length, 2 * HEADDIM), BF16)
+        both = jnp.concatenate([jnp.where(half, inputs, zero), pad, jnp.where(half, zero, inputs), pad], axis=0)
+        mix = (mixing[:, low : low + 2 * HEADDIM] * scores).astype(BF16)
+        inside.append(jnp.dot(mix, both, preferred_element_type=F32))
+    inside = jnp.concatenate(inside, axis=1)
+    state = state_ref[0]
+    carried = jnp.exp(cumulative) * dot_nt(output_mix, state)
+    scanned = inside + carried + skip * head_inputs
+    gated = scanned * (gate_inputs / (1.0 + jnp.exp(-gate_inputs)))
+    channel = lax.broadcasted_iota(jnp.int32, (width, 128), 0)
+    member = lax.broadcasted_iota(jnp.int32, (width, 128), 1) * group_width
+    member = ((channel >= member) & (channel < member + group_width)).astype(BF16)
+    squares = jnp.dot((gated * gated).astype(BF16), member, preferred_element_type=F32)
+    scale = lax.rsqrt(squares * (1.0 / group_width) + 1e-05)
+    position = lax.broadcasted_iota(jnp.int32, (length, width), 1)
+    spread_scale = jnp.broadcast_to(scale[:, 0:1], (length, width))
+    for group in range(1, width // group_width):
+        spread_scale = jnp.where(position >= group * group_width, scale[:, group : group + 1], spread_scale)
+    normed_ref[...] = (gated * spread_scale * gain).astype(BF16)
+    to_end = (jnp.exp(last - cumulative) * steps * head_inputs).astype(BF16)
+    added = lax.dot_general(to_end, input_mix, (((0,), (0,)), ((), ())), preferred_element_type=F32)
+    head_rows = -(-heads // 8) * 8
+    head_of = lax.broadcasted_iota(jnp.int32, (head_rows, width), 1)
+    first = lax.broadcasted_iota(jnp.int32, (head_rows, width), 0) * HEADDIM
+    whole = jnp.sum(jnp.where(head_of == first, last, 0.0), axis=1, keepdims=True)
+    whole = jnp.broadcast_to(jnp.exp(whole), (head_rows, NSTATE))
+    for head in range(heads):
+        rows = slice(head * HEADDIM, (head + 1) * HEADDIM)
+        carry_ref[0, rows, :] = state[rows].astype(F32) * whole[head : head + 1, :] + added[rows]
+
+
+def scan(slots, xz, side, state, rows, picked, carry, total_slots, group_width):
+    count, width, _ = state.shape
+    length = xz.shape[0] // total_slots
+    more = [] if carry is None else [pl.BlockSpec(memory_space=pl.ANY)]
+    return pl.pallas_call(
+        functools.partial(scan_kernel, width // HEADDIM, group_width),
+        grid_spec=pltpu.PrefetchScalarGridSpec(
+            num_scalar_prefetch=1,
+            grid=(count,),
+            in_specs=[
+                pl.BlockSpec((length, 2 * width), lambda i, slots: (slots[i], 0)),
+                pl.BlockSpec((length, side.shape[1]), lambda i, slots: (slots[i], 0)),
+                pl.BlockSpec((1, width, NSTATE), lambda i, slots: (i, 0, 0)),
+                pl.BlockSpec(rows.shape, lambda i, slots: (0, 0)),
+                pl.BlockSpec(picked.shape, lambda i, slots: (0, 0)),
+            ]
+            + more,
+            out_specs=(
+                pl.BlockSpec((length, width), lambda i, slots: (i, 0)),
+                pl.BlockSpec((1, width, NSTATE), lambda i, slots: (slots[i], 0, 0)),
+            ),
+        ),
+        out_shape=(
+            jax.ShapeDtypeStruct((count * length, width), BF16),
+            jax.ShapeDtypeStruct((total_slots, width, NSTATE), F32),
+        ),
+        input_output_aliases={} if carry is None else {6: 1},
+        compiler_params=params(),
+        cost_estimate=cost(count * length * width * 1500, count * width * NSTATE * 6),
+    )(slots, xz, side, state, rows, picked, *(() if carry is None else (carry,)))
+
+
+def add_kernel(at_ref, normed_ref, out_ref, *rest):
+    total = dot_nt(normed_ref[...], out_ref[0])
+    if len(rest) > 1:
+        total = total + rest[0][...].astype(F32)
+    rest[-1][...] = total.astype(BF16)
+
+
+def add_term(at, normed, dense, dest, shards, got):
+    rows, depth = normed.shape
+    width = dense.shape[1]
+    whole = pl.BlockSpec((rows, width), lambda i, at: (0, 0))
+    return pl.pallas_call(
+        add_kernel,
+        grid_spec=pltpu.PrefetchScalarGridSpec(
+            num_scalar_prefetch=1,
+            grid=(1,),
+            in_specs=[
+                pl.BlockSpec((rows, depth), lambda i, at: (0, 0)),
+                pl.BlockSpec((1, width, depth), lambda i, at: (lax.rem(at[1] + (shards - dest), shards), 0, 0)),
+            ]
+            + ([] if got is None else [whole]),
+            out_specs=whole,
+        ),
+        out_shape=jax.ShapeDtypeStruct((rows, width), BF16),
+        compiler_params=params(),
+        cost_estimate=cost(2 * rows * depth * width, width * depth * 2),
+    )(at, normed, dense, *(() if got is None else (got,)))
+
+
+def place_kernel(frames, at_ref, slots_ref, normed_ref, dense_ref, got_ref, *rest):
+    out_ref = rest[-1]
+    total = (dot_nt(normed_ref[...], dense_ref[0]) + got_ref[...].astype(F32)).astype(BF16).astype(F32)
+    patch = total.shape[0] // frames
+    for frame in range(frames):
+        out_ref[0, frame] = total[frame * patch : (frame + 1) * patch].astype(BF16)
+
+
+def place_term(at, slots, normed, dense, got, total_slots, before):
+    rows, depth = normed.shape
+    count = slots.shape[0]
+    length = rows // count
+    width = dense.shape[1]
+    patch = length // FRAMES
+    return pl.pallas_call(
+        functools.partial(place_kernel, FRAMES),
+        grid_spec=pltpu.PrefetchScalarGridSpec(
+            num_scalar_prefetch=2,
+            grid=(count,),
+            in_specs=[
+                pl.BlockSpec((length, depth), lambda i, at, slots: (i, 0)),
+                pl.BlockSpec((1, width, depth), lambda i, at, slots: (at[1], 0, 0)),
+                pl.BlockSpec((length, width), lambda i, at, slots: (i, 0)),
+            ]
+            + ([] if before is None else [pl.BlockSpec(memory_space=pl.ANY)]),
+            out_specs=pl.BlockSpec((1, FRAMES, patch, width), lambda i, at, slots: (slots[i], 0, 0, 0)),
+        ),
+        out_shape=jax.ShapeDtypeStruct((total_slots, FRAMES, patch, width), BF16),
+        input_output_aliases={} if before is None else {5: 0},
+        compiler_params=params(),
+        cost_estimate=cost(2 * rows * depth * width, width * depth * 2),
+    )(at, slots, normed, dense, got, *(() if before is None else (before,)))
+
+
+def swap(value, bit, size):
+    return lax.ppermute(value, "stream", [(i, i ^ bit) for i in range(size)])
+
+
+def cube(halves, size):
+    a, b = halves
+    got_a, got_b = {0: a}, {0: b}
+    got_a[2], got_a[4] = swap(a, 2, size), swap(a, 4, size)
+    got_b[2], got_b[4] = swap(b, 2, size), swap(b, 4, size)
+    got_a[6] = swap(got_a[4], 2, size)
+    got_b[6] = swap(got_b[2], 4, size)
+    for bits in (0, 2, 4, 6):
+        got_a[bits | 1] = swap(got_a[bits], 1, size)
+        got_b[bits | 1] = swap(got_b[bits], 1, size)
+    return got_a, got_b
+
+
+def after(values, earlier):
+    return lax.optimization_barrier((values, earlier))[0]
+
+
+def sparse(
+    xz_room,
+    out_room,
+    frames_in,
+    kept_state,
+    moved_to,
+    xz_weight,
+    side_weight,
+    xz_mask,
+    dt_bias,
+    decay_rate,
+    skip_gain,
+    norm_gain,
+    out_weight,
+    out_mask,
+):
+    streams, shards = lax.axis_size("stream"), lax.axis_size("shard")
+    me, shard = lax.axis_index("stream"), lax.axis_index("shard")
+    at = jnp.stack([me, shard, jnp.zeros_like(me)]).astype(jnp.int32)
+    slots, heads = kept_state.shape[:2]
+    width = heads * HEADDIM
+    ring = [(i, (i + 1) % shards) for i in range(shards)]
+
+    features = [frames_in.reshape(-1, frames_in.shape[3])]
+    for _ in range(shards - 1):
+        features.append(lax.ppermute(features[-1], "shard", ring))
+
+    xz_panel = xz_weight.reshape(xz_weight.shape[0], -1)
+    xz_halves = pack(at, xz_mask, xz_panel, 2, xz_room // 2)
+    out_halves = pack(at, out_mask, out_weight, 1, out_room // 2)
+    xz_a, xz_b = cube(xz_halves, streams)
+    side = lax.all_gather(side_weight.T, "stream", axis=0)
+
+    steps = (1, 2, 3, streams // 2)
+    distance = (moved_to // slots - me) % streams
+    match = distance[None, :] == jnp.array(steps)[:, None]
+    rank = jnp.cumsum(match.astype(jnp.int32), axis=1) - 1
+    chosen = match[:, None, :] & (rank[:, None, :] == jnp.arange(MOST)[None, :, None])
+    order = jnp.sum(jnp.where(chosen, jnp.arange(slots), 0), axis=2, dtype=jnp.int32)
+    landing = jnp.sum(jnp.where(chosen, moved_to % slots, 0), axis=2, dtype=jnp.int32)
+    flat_state = kept_state.reshape(slots, width, NSTATE)
+    sends = [pick(order[k], flat_state) for k in range(len(steps))]
+    sends = after(sends, (xz_a[6], xz_b[6]))
+    got_states, got_slots = [], []
+    for k, step in enumerate(steps):
+        pairs = [(i, (i + step) % streams) for i in range(streams)]
+        got_states.append(lax.ppermute(sends[k], "stream", pairs))
+        got_slots.append(lax.ppermute(landing[k], "stream", pairs))
+    out_halves = after(out_halves, (xz_a[6], xz_b[6]))
+    out_a, out_b = cube(out_halves, streams)
+
+    per = streams // shards
+    dense = None
+    for bits in range(streams):
+        panel = me ^ bits
+        where = (shard - panel // per) % shards * per + panel % per
+        spot = jnp.stack([panel, shard, where]).astype(jnp.int32)
+        dense = spread(spot, xz_mask, xz_a[bits], xz_b[bits], 2, (streams, *xz_panel.shape), dense)
+    dense = dense.reshape(shards, -1, xz_panel.shape[1])
+    out_dense = None
+    for bits in range(streams):
+        spot = jnp.stack([me ^ bits, shard, me ^ bits]).astype(jnp.int32)
+        out_dense = spread(spot, out_mask, out_a[bits], out_b[bits], 1, (streams, *out_weight.shape), out_dense)
+    out_dense = out_dense.reshape(shards, -1, width)
+
+    xz = product(features[:-1], dense, 0, None)
+    xz = product(features[-1:], dense, shards - 1, xz)
+    side_total = side_product(at, side, features)
+    head_of = jnp.arange(width) // HEADDIM
+    picked = (shard * heads + head_of[None, :] == jnp.arange(heads * shards)[:, None]).astype(F32)
+    per_head = [jnp.repeat(v, HEADDIM) for v in (dt_bias, decay_rate, skip_gain)]
+    rows = jnp.stack(per_head + [norm_gain] + [jnp.zeros_like(norm_gain)] * 4)
+
+    carry, mixed = None, None
+    normed = []
+    for k in range(len(steps)):
+        done, carry = scan(
+            got_slots[k], xz, side_total, got_states[k], rows, picked, carry, slots, DINNER // NORM_GROUPS
+        )
+        normed.append(done)
+    for k in range(len(steps)):
+        moving = None
+        for hop in range(1, shards):
+            moving = lax.ppermute(add_term(at, normed[k], out_dense, hop, shards, moving), "shard", ring)
+        mixed = place_term(at, got_slots[k], normed[k], out_dense, moving, slots, mixed)
+    return mixed, carry.reshape(kept_state.shape)
+
+
+def fullest(mask, panels, shards):
+    rows = mask.reshape(panels, -1, mask.shape[-1])
+    cells = rows.reshape(panels, rows.shape[1], shards, -1)
+    return jnp.max(jnp.sum(cells, axis=(1, 3)))
+
+
+def on_device(streams, shards, *args):
+    xz_weight, out_weight, kept_state = args[3], args[10], args[1]
+    rows, width = out_weight.shape
+    regular = (
+        streams == 8
+        and streams % shards == 0
+        and rows % BLOCK == 0
+        and width % BLOCK == 0
+        and width % (DINNER // NORM_GROUPS) == 0
+        and kept_state.shape[1] % 2 == 0
+    )
+    if not regular:
+        return general(*args)
+    blocks = (rows // BLOCK) * (width // BLOCK)
+    xz_room = int(2 * blocks * XZ_SHARE) // 2 * 2
+    out_room = int(blocks * OUT_SHARE) // 2 * 2
+    fits = (fullest(args[5], streams, shards) <= xz_room) & (fullest(args[11], streams, shards) <= out_room)
+    return lax.cond(
+        fits,
+        functools.partial(sparse, xz_room, out_room),
+        functools.partial(sparse, 2 * blocks, blocks),
+        *args,
+    )
+
+
 def solution(mesh):
     placed = (
         P("stream", None, None, "shard"),
@@ -161,7 +650,7 @@
         P(),
     )
     return jax.shard_map(
-        on_device,
+        functools.partial(on_device, mesh.shape["stream"], mesh.shape["shard"]),
         mesh=mesh,
         in_specs=placed,
         out_specs=(P("stream", None, None, "shard"), P("stream", "shard", None, None)),

time: 648 us -> 457 us (0.71)
  Pallas kernels: 0 us -> 230 us
  matrix products: 210 us -> 0 us
  waiting for transfers between devices: 252 us -> 132 us
  local copies, waits for them, and re-layouts: 122 us -> 18.4 us
  starting transfers between devices: 10.4 us -> 43.2 us
  other arithmetic: 33.3 us -> 4.33 us
  loops' own time: 0 us -> 6.82 us
    pallas_call x0 -> x45, Pallas kernels: none -> 230 us  [the longest x16 84.8 us: spread(): pl.pallas_call(functools.partial(spread_kernel, half, rows // BLOCK, grou...]
    dot_general x21 -> x0, matrix products: 210 us -> none  [the longest x4 76.4 us: frame_step(): jnp.einsum('sln,shpn->slhp', output_mix, carry_state, precision=highest)]
    ppermute x0 -> x51, waiting for transfers between devices: none -> 132 us  [the longest x28 108 us: swap(): return lax.ppermute(value, 'stream', [(i, i ^ bit) for i in range(size)])]
    reduce_scatter x1 -> x0, waiting for transfers between devices: 85.9 us -> none  [on_device(): lax.psum_scatter(partial_out.astype(jnp.bfloat16), 'shard', scatter_dimen...]
    all_to_all x2 -> x0, waiting for transfers between devices: 84.3 us -> none  [the longest x1 84.3 us: on_device(): lax.all_to_all(send_states.astype(jnp.bfloat16), 'stream', split_axis=0,...]
    all_gather x4 -> x1, waiting for transfers between devices: 79.6 us -> 0.01 us  [sparse(): side = lax.all_gather(side_weight.T, 'stream', axis=0)]
    ppermute x0 -> x51, starting transfers between devices: none -> 43.2 us  [the longest x28 19.7 us: swap(): return lax.ppermute(value, 'stream', [(i, i ^ bit) for i in range(size)])]
    scatter x3 -> x0, local copies, waits for them, and re-layouts: 38.2 us -> none  [the longest x1 24.1 us: on_device(): jnp.zeros_like(kept_state).at[landing].set(got_states, mode='drop')]
  transfers between devices with their start and end apart: 7 -> 52, of which waited for: 3 -> 19; matrix products, arithmetic and copies ran while one was open for 53% -> 2% of each run, Pallas kernels for 0% -> 49%
where the time goes in v1:
time: 457 us; the launch traced here: 450 us
  Pallas kernels  230 us (50%)
  waiting for transfers between devices  132 us (29%)
  starting transfers between devices  43.2 us (9%)
  local copies, waits for them, and re-layouts  18.4 us (4%)
  between operations  15.6 us (3%)
  loops' own time  6.82 us (1%)
    ppermute x28, waiting for transfers between devices, swap(): return lax.ppermute(value, 'stream', [(i, i ^ bit) for i in range(size)])  108 us
    pallas_call x16, Pallas kernels, spread(): pl.pallas_call(functools.partial(spread_kernel, half, rows // BLOCK, grou...  84.8 us
    pallas_call x12, Pallas kernels, add_term(): pl.pallas_call(add_kernel, grid_spec=pltpu.PrefetchScalarGridSpec(num_sca...  44.3 us
    pallas_call x2, Pallas kernels, product(): pl.pallas_call(functools.partial(product_kernel, count), grid=(width // t...  30.7 us
    pallas_call x4, Pallas kernels, scan(): pl.pallas_call(functools.partial(scan_kernel, width // HEADDIM, group_wid...  25.6 us
    pallas_call x4, Pallas kernels, place_term(): pl.pallas_call(functools.partial(place_kernel, FRAMES), grid_spec=pltpu.P...  23 us
    ppermute x12, waiting for transfers between devices, sparse(): lax.ppermute(add_term(at, normed[k], out_dense, hop, shards, moving), 'sh...  21.9 us
    ppermute x28, starting transfers between devices, swap(): return lax.ppermute(value, 'stream', [(i, i ^ bit) for i in range(size)])  19.7 us
  transfers between devices with their start and end apart: 52, of which 19 were waited for; matrix products, arithmetic and copies ran while one was open for 2% of the time, Pallas kernels for 49%

profile of v1, /device:TPU:0, one launch (start us, length us, event | category | flops | bytes accessed | tf_op | source)
XLA Modules:
  0.0 449.9 jit_solution(5761276691614810220)
XLA Ops:
  12.0 429.7 %conditional.1 = (f32[12,20,64,128]{3,2,1,0:T(8,128)}, bf16[12,4,12,1280]{3,1,2,0:T(4,128)(2,1)S(1)}) conditional(s32[]{:T(128)} %convert_element_type.23, (s32[12]{0:T(128)}, s32[4]{0:T(128)}, bf16[12,4,12,1280]{3,1,2,0:T(4,128)(2,1)}, s32[40,2,40]{2,1,0:T(2,128)}, bf16[640,2,1280]{2,1,0:T(2,128)(2,1)}, /*index=5*/bf16[640,336]{0,1:T(8,128)(2,1)}, ...), branch_computations={%region_5.0_spmd, %region_9.13_spmd} | conditional | flops 25737187328 | bytes 548205568 | solution.py:629
  30.6 21.6 %collective-permute-done.55.a_ref = bf16[33,128,128]{2,1,0:T(8,128)(2,1)} collective-permute-done((bf16[33,128,128]{2,1,0:T(8,128)(2,1)}, bf16[33,128,128]{2,1,0:T(8,128)(2,1)}, u32[]{:S(2)}, u32[]{:S(2)}) %collective-permute-start.55) | collective-permute-done | bytes 1081376 | tf_op jit(solution)/shard_map/cond/branch_1_fun/ppermute | solution.py:498
  66.1 16.8 %collective-permute-done.64.a_ref = bf16[33,128,128]{2,1,0:T(8,128)(2,1)} collective-permute-done((bf16[33,128,128]{2,1,0:T(8,128)(2,1)}, bf16[33,128,128]{2,1,0:T(8,128)(2,1)}, u32[]{:S(2)}, u32[]{:S(2)}) %collective-permute-start.64) | collective-permute-done | bytes 1081376 | tf_op jit(solution)/shard_map/cond/branch_1_fun/ppermute | solution.py:498
  83.9 29.9 %collective-permute-done.56.a_ref = bf16[33,128,128]{2,1,0:T(8,128)(2,1)} collective-permute-done((bf16[33,128,128]{2,1,0:T(8,128)(2,1)}, bf16[33,128,128]{2,1,0:T(8,128)(2,1)}, u32[]{:S(2)}, u32[]{:S(2)}) %collective-permute-start.56) | collective-permute-done | bytes 1081376 | tf_op jit(solution)/shard_map/cond/branch_1_fun/ppermute | solution.py:498
  125.0 12.4 %collective-permute-done.79.b_ref = bf16[18,128,128]{2,1,0:T(8,128)(2,1)} collective-permute-done((bf16[18,128,128]{2,1,0:T(8,128)(2,1)}, bf16[18,128,128]{2,1,0:T(8,128)(2,1)}, u32[]{:S(2)}, u32[]{:S(2)}) %collective-permute-start.79) | collective-permute-done | bytes 589856 | tf_op jit(solution)/shard_map/cond/branch_1_fun/ppermute | solution.py:498
  139.4 9.9 %collective-permute-done.85.a_ref = bf16[18,128,128]{2,1,0:T(8,128)(2,1)} collective-permute-done((bf16[18,128,128]{2,1,0:T(8,128)(2,1)}, bf16[18,128,128]{2,1,0:T(8,128)(2,1)}, u32[]{:S(2)}, u32[]{:S(2)}) %collective-permute-start.85) | collective-permute-done | bytes 589856 | tf_op jit(solution)/shard_map/cond/branch_1_fun/ppermute | solution.py:498
  158.1 12.4 %collective-permute-done.77.a_ref = bf16[18,128,128]{2,1,0:T(8,128)(2,1)} collective-permute-done((bf16[18,128,128]{2,1,0:T(8,128)(2,1)}, bf16[18,128,128]{2,1,0:T(8,128)(2,1)}, u32[]{:S(2)}, u32[]{:S(2)}) %collective-permute-start.77) | collective-permute-done | bytes 589856 | tf_op jit(solution)/shard_map/cond/branch_1_fun/ppermute | solution.py:498
  171.2 6.5 %branch_1_fun.46.rest_0_ = bf16[8,640,2560]{2,1,0:T(8,128)(2,1)} custom-call(s32[3]{0:T(128)S(1)} %pad_add_fusion.41.at_ref, s32[3200]{0:T(1024)S(1)} %reshape.221.mask_ref, bf16[33,128,128]{2,1,0:T(8,128)(2,1)} %get-tuple-element.88.a_ref, bf16[33,128,128]{2,1,0:T(8,128)(2,1)} %get-tuple-element.89.b_ref), custom_call_target="tpu_custom_call" | custom-call | bytes 9830400 | tf_op jit(solution)/shard_map/cond/branch_1_fun/pallas_call | solution.py:252
  194.9 6.1 %branch_1_fun.48.rest_0_ = bf16[8,640,2560]{2,1,0:T(8,128)(2,1)} custom-call(s32[3]{0:T(128)S(1)} %pad_add_fusion.37.at_ref, s32[3200]{0:T(1024)S(1)} %reshape.221.mask_ref, bf16[33,128,128]{2,1,0:T(8,128)(2,1)} %collective-permute-done.64.a_ref, bf16[33,128,128]{2,1,0:T(8,128)(2,1)} %collective-permute-done.58.b_ref, ...), custom_call_target="tpu_custom_call", output_to_operand_aliasing={{}: (4, {})} | custom-call | bytes 9830400 | tf_op jit(solution)/shard_map/cond/branch_1_fun/pallas_call | solution.py:252
  205.5 6.2 %branch_1_fun.49.rest_0_ = bf16[8,640,2560]{2,1,0:T(8,128)(2,1)} custom-call(s32[3]{0:T(128)S(1)} %pad_add_fusion.35.at_ref, s32[3200]{0:T(1024)S(1)} %reshape.221.mask_ref, bf16[33,128,128]{2,1,0:T(8,128)(2,1)} %collective-permute-done.65.a_ref, bf16[33,128,128]{2,1,0:T(8,128)(2,1)} %collective-permute-done.66.b_ref, ...), custom_call_target="tpu_custom_call", output_to_operand_aliasing={{}: (4, {})} | custom-call | bytes 9830400 | tf_op jit(solution)/shard_map/cond/branch_1_fun/pallas_call | solution.py:252
  211.6 6.1 %branch_1_fun.50.rest_0_ = bf16[8,640,2560]{2,1,0:T(8,128)(2,1)} custom-call(s32[3]{0:T(128)S(1)} %pad_add_fusion.33.at_ref, s32[3200]{0:T(1024)S(1)} %reshape.221.mask_ref, bf16[33,128,128]{2,1,0:T(8,128)(2,1)} %collective-permute-done.55.a_ref, bf16[33,128,128]{2,1,0:T(8,128)(2,1)} %collective-permute-done.62.b_ref, ...), custom_call_target="tpu_custom_call", output_to_operand_aliasing={{}: (4, {})} | custom-call | bytes 9830400 | tf_op jit(solution)/shard_map/cond/branch_1_fun/pallas_call | solution.py:252
  217.7 6.1 %branch_1_fun.51.rest_0_ = bf16[8,640,2560]{2,1,0:T(8,128)(2,1)} custom-call(s32[3]{0:T(128)S(1)} %pad_add_fusion.31.at_ref, s32[3200]{0:T(1024)S(1)} %reshape.221.mask_ref, bf16[33,128,128]{2,1,0:T(8,128)(2,1)} %collective-permute-done.61.a_ref, bf16[33,128,128]{2,1,0:T(8,128)(2,1)} %collective-permute-done.63.b_ref, ...), custom_call_target="tpu_custom_call", output_to_operand_aliasing={{}: (4, {})} | custom-call | bytes 9830400 | tf_op jit(solution)/shard_map/cond/branch_1_fun/pallas_call | solution.py:252
  223.8 6.2 %branch_1_fun.52.rest_0_ = bf16[8,640,2560]{2,1,0:T(8,128)(2,1)} custom-call(s32[3]{0:T(128)S(1)} %pad_add_fusion.29.at_ref, s32[3200]{0:T(1024)S(1)} %reshape.221.mask_ref, bf16[33,128,128]{2,1,0:T(8,128)(2,1)} %collective-permute-done.56.a_ref, bf16[33,128,128]{2,1,0:T(8,128)(2,1)} %collective-permute-done.59.b_ref, ...), custom_call_target="tpu_custom_call", output_to_operand_aliasing={{}: (4, {})} | custom-call | bytes 9830400 | tf_op jit(solution)/shard_map/cond/branch_1_fun/pallas_call | solution.py:252
  239.2 6.1 %branch_1_fun.53 = bf16[8,640,2560]{2,1,0:T(8,128)(2,1)} custom-call(s32[3]{0:T(128)S(1)} %pad_add_fusion.25.at_ref, s32[3200]{0:T(1024)S(1)} %reshape.221.mask_ref, bf16[33,128,128]{2,1,0:T(8,128)(2,1)} %collective-permute-done.57.a_ref, bf16[33,128,128]{2,1,0:T(8,128)(2,1)} %collective-permute-done.60.b_ref, ...), custom_call_target="tpu_custom_call", output_to_operand_aliasing={{}: (4, {})} | custom-call | bytes 9830400 | tf_op jit(solution)/shard_map/cond/branch_1_fun/pallas_call | solution.py:252
  249.8 18.4 %branch_1_fun.54.refs_2_ = f32[576,2560]{1,0:T(8,128)} custom-call(bf16[576,1280]{1,0:T(8,128)(2,1)S(1)} %reshape.220.refs_0_, bf16[576,1280]{1,0:T(8,128)(2,1)S(1)} %collective-permute-done.52.refs_1_, bf16[576,1280]{1,0:T(8,128)(2,1)} %collective-permute-done.53.refs_2_, bf16[4,1280,2560]{2,1,0:T(8,128)(2,1)} %bitcast.87, bf16[4,1280,2560]{2,1,0:T(8,128)(2,1)} %bitcast.88, ...), custom_call_target="tpu_custom_call" | custom-call | flops 11324620800 | bytes 31457280 | tf_op jit(solution)/shard_map/cond/branch_1_fun/pallas_call | solution.py:281
  291.6 12.4 %branch_1_fun.55.xz_ref = f32[576,2560]{1,0:T(8,128)} custom-call(bf16[576,1280]{1,0:T(8,128)(2,1)} %collective-permute-done.54.refs_0_.refs_3_, bf16[4,1280,2560]{2,1,0:T(8,128)(2,1)} %bitcast.90, f32[576,2560]{1,0:T(8,128)} %branch_1_fun.54.refs_2_), custom_call_target="tpu_custom_call", output_to_operand_aliasing={{}: (2, {})} | custom-call | flops 3774873600 | bytes 18350080 | tf_op jit(solution)/shard_map/cond/branch_1_fun/pallas_call | solution.py:281
  304.0 6.4 %branch_1_fun.56.side_ref = f32[576,336]{1,0:T(8,128)S(1)} custom-call(s32[3]{0:T(128)S(1)} %copy-done.15, bf16[8,336,640]{2,1,0:T(8,128)(2,1)} %bitcast.106, bf16[576,1280]{1,0:T(8,128)(2,1)S(1)} %reshape.220.refs_0_, bf16[576,1280]{1,0:T(8,128)(2,1)S(1)} %collective-permute-done.52.refs_1_, bf16[576,1280]{1,0:T(8,128)(2,1)} %collective-permute-done.53.refs_2_, ...), custom_call_target="tpu_custom_call" | custom-call | flops 1981808640 | bytes 9338880 | tf_op jit(solution)/shard_map/cond/branch_1_fun/pallas_call | solution.py:310
  313.5 6.4 %branch_1_fun.61 = (bf16[144,1280]{1,0:T(8,128)(2,1)S(1)}, f32[12,1280,128]{2,1,0:T(8,128)}) custom-call(s32[3]{0:T(128)S(1)} %collective-permute-done.74.slots_ref, f32[576,2560]{1,0:T(8,128)} %branch_1_fun.55.xz_ref, f32[576,336]{1,0:T(8,128)S(1)} %branch_1_fun.56.side_ref, bf16[3,1280,128]{2,1,0:T(8,128)(2,1)} %collective-permute-done.75.state_ref, ...), custom_call_target="tpu_custom_call" | custom-call | flops 276480000 | bytes 2949120 | tf_op jit(solution)/shard_map/cond/branch_1_fun/pallas_call | solution.py:406
  326.4 6.4 %branch_1_fun.62 = (bf16[144,1280]{1,0:T(8,128)(2,1)S(1)}, f32[12,1280,128]{2,1,0:T(8,128)}) custom-call(s32[3]{0:T(128)S(1)} %collective-permute-done.72.slots_ref, f32[576,2560]{1,0:T(8,128)} %branch_1_fun.55.xz_ref, f32[576,336]{1,0:T(8,128)S(1)} %branch_1_fun.56.side_ref, ...), custom_call_target="tpu_custom_call", output_to_operand_aliasing={{1}: (6, {})} | custom-call | flops 276480000 | bytes 2949120 | tf_op jit(solution)/shard_map/cond/branch_1_fun/pallas_call | solution.py:406
  338.2 6.4 %branch_1_fun.63 = (bf16[144,1280]{1,0:T(8,128)(2,1)S(1)}, f32[12,1280,128]{2,1,0:T(8,128)}) custom-call(s32[3]{0:T(128)S(1)} %collective-permute-done.70.slots_ref, f32[576,2560]{1,0:T(8,128)} %branch_1_fun.55.xz_ref, f32[576,336]{1,0:T(8,128)S(1)} %branch_1_fun.56.side_ref, ...), custom_call_target="tpu_custom_call", output_to_operand_aliasing={{1}: (6, {})} | custom-call | flops 276480000 | bytes 2949120 | tf_op jit(solution)/shard_map/cond/branch_1_fun/pallas_call | solution.py:406
  350.4 6.4 %branch_1_fun.64 = (bf16[144,1280]{1,0:T(8,128)(2,1)S(1)}, f32[12,1280,128]{2,1,0:T(8,128)}) custom-call(s32[3]{0:T(128)S(1)} %collective-permute-done.51.slots_ref, f32[576,2560]{1,0:T(8,128)} %branch_1_fun.55.xz_ref, f32[576,336]{1,0:T(8,128)S(1)} %branch_1_fun.56.side_ref, ...), custom_call_target="tpu_custom_call", output_to_operand_aliasing={{1}: (6, {})} | custom-call | flops 276480000 | bytes 2949120 | tf_op jit(solution)/shard_map/cond/branch_1_fun/pallas_call | solution.py:406
  421.2 5.7 %branch_1_fun.87.rest_0_ = bf16[12,4,12,1280]{3,2,1,0:T(8,128)(2,1)S(1)} custom-call(s32[3]{0:T(128)S(1)} %copy-done.15, s32[3]{0:T(128)S(1)} %collective-permute-done.72.slots_ref, bf16[144,1280]{1,0:T(8,128)(2,1)S(1)} %get-tuple-element.111.normed_ref, bf16[4,1280,1280]{2,1,0:T(8,128)(2,1)} %bitcast.80, ...), custom_call_target="tpu_custom_call", output_to_operand_aliasing={{}: (5, {})} | custom-call | flops 471859200 | bytes 3276800 | tf_op jit(solution)/shard_map/cond/branch_1_fun/pallas_call | solution.py:477
  429.1 5.7 %branch_1_fun.88.rest_0_ = bf16[12,4,12,1280]{3,2,1,0:T(8,128)(2,1)S(1)} custom-call(s32[3]{0:T(128)S(1)} %copy-done.15, s32[3]{0:T(128)S(1)} %collective-permute-done.70.slots_ref, bf16[144,1280]{1,0:T(8,128)(2,1)S(1)} %get-tuple-element.110.normed_ref, bf16[4,1280,1280]{2,1,0:T(8,128)(2,1)} %bitcast.81, ...), custom_call_target="tpu_custom_call", output_to_operand_aliasing={{}: (5, {})} | custom-call | flops 471859200 | bytes 3276800 | tf_op jit(solution)/shard_map/cond/branch_1_fun/pallas_call | solution.py:477
  434.9 5.7 %branch_1_fun.89 = bf16[12,4,12,1280]{3,2,1,0:T(8,128)(2,1)S(1)} custom-call(s32[3]{0:T(128)S(1)} %copy-done.15, s32[3]{0:T(128)S(1)} %collective-permute-done.51.slots_ref, bf16[144,1280]{1,0:T(8,128)(2,1)S(1)} %get-tuple-element.103.normed_ref, bf16[4,1280,1280]{2,1,0:T(8,128)(2,1)} %bitcast.82, ...), custom_call_target="tpu_custom_call", output_to_operand_aliasing={{}: (5, {})} | custom-call | flops 471859200 | bytes 3276800 | tf_op jit(solution)/shard_map/cond/branch_1_fun/pallas_call | solution.py:477
  (220 shorter events, 201.3 us)
Async XLA Ops:
  18.0 286.0 %all-gather.7.cloned.1.call-start = ((), (), s32[]{:S(2)}) async-start(), calls=%async_computation.1 | async-start | bytes 3870720 | tf_op jit(solution)/shard_map/cond/branch_1_fun/all_gather | solution.py:549
  29.5 34.0 %collective-permute-start.68 = (bf16[33,128,128]{2,1,0:T(8,128)(2,1)}, bf16[33,128,128]{2,1,0:T(8,128)(2,1)S(1)}, u32[]{:S(2)}, u32[]{:S(2)}) collective-permute-start(bf16[33,128,128]{2,1,0:T(8,128)(2,1)} %get-tuple-element.89.b_ref), channel_id=1, source_target_pairs={{0,4},{4,0},{8,12},{12,8},{16,20},{20,16},{24,28},{28,24},{1,5},{5... | collective-permute-start | bytes 3244040 | tf_op jit(solution)/shard_map/cond/branch_1_fun/ppermute | solution.py:498
  30.1 52.9 %collective-permute-start.64 = (bf16[33,128,128]{2,1,0:T(8,128)(2,1)}, bf16[33,128,128]{2,1,0:T(8,128)(2,1)}, u32[]{:S(2)}, u32[]{:S(2)}) collective-permute-start(bf16[33,128,128]{2,1,0:T(8,128)(2,1)} %get-tuple-element.88.a_ref), channel_id=1, source_target_pairs={{0,8},{4,12},{8,0},{12,4},{16,24},{20,28},{24,16},{28,20},{1,9},{5... | collective-permute-start | bytes 3244040 | tf_op jit(solution)/shard_map/cond/branch_1_fun/ppermute | solution.py:498
  52.2 31.7 %collective-permute-start.62 = (bf16[33,128,128]{2,1,0:T(8,128)(2,1)}, bf16[33,128,128]{2,1,0:T(8,128)(2,1)}, u32[]{:S(2)}, u32[]{:S(2)}) collective-permute-start(bf16[33,128,128]{2,1,0:T(8,128)(2,1)} %get-tuple-element.89.b_ref), channel_id=1, source_target_pairs={{0,16},{4,20},{8,24},{12,28},{16,0},{20,4},{24,8},{28,12},{1,17},{... | collective-permute-start | bytes 3244040 | tf_op jit(solution)/shard_map/cond/branch_1_fun/ppermute | solution.py:498
  55.1 58.7 %collective-permute-start.56 = (bf16[33,128,128]{2,1,0:T(8,128)(2,1)}, bf16[33,128,128]{2,1,0:T(8,128)(2,1)}, u32[]{:S(2)}, u32[]{:S(2)}) collective-permute-start(bf16[33,128,128]{2,1,0:T(8,128)(2,1)} %collective-permute-done.55.a_ref), channel_id=1, source_target_pairs={{0,8},{4,12},{8,0},{12,4},{16,24},{20,28},{24,16},{28,20},{1,9},{5... | collective-permute-start | bytes 3244040 | tf_op jit(solution)/shard_map/cond/branch_1_fun/ppermute | solution.py:498
  57.6 56.9 %collective-permute-start.59 = (bf16[33,128,128]{2,1,0:T(8,128)(2,1)}, bf16[33,128,128]{2,1,0:T(8,128)(2,1)}, u32[]{:S(2)}, u32[]{:S(2)}) collective-permute-start(bf16[33,128,128]{2,1,0:T(8,128)(2,1)} %collective-permute-done.58.b_ref), channel_id=1, source_target_pairs={{0,16},{4,20},{8,24},{12,28},{16,0},{20,4},{24,8},{28,12},{1,17},{... | collective-permute-start | bytes 3244040 | tf_op jit(solution)/shard_map/cond/branch_1_fun/ppermute | solution.py:498
  64.6 54.1 %collective-permute-start.52 = (bf16[576,1280]{1,0:T(8,128)(2,1)S(1)}, bf16[576,1280]{1,0:T(8,128)(2,1)S(1)}, u32[]{:S(2)}, u32[]{:S(2)}) collective-permute-start(bf16[576,1280]{1,0:T(8,128)(2,1)S(1)} %reshape.220.refs_0_), channel_id=1, source_target_pairs={{0,1},{1,2},{2,3},{3,0},{4,5},{5,6},{6,7},{7,4},{8,9},{9,10},{10,1... | collective-permute-start | bytes 4423688 | tf_op jit(solution)/shard_map/cond/branch_1_fun/ppermute | solution.py:543
  82.9 37.3 %collective-permute-start.66 = (bf16[33,128,128]{2,1,0:T(8,128)(2,1)}, bf16[33,128,128]{2,1,0:T(8,128)(2,1)}, u32[]{:S(2)}, u32[]{:S(2)}) collective-permute-start(bf16[33,128,128]{2,1,0:T(8,128)(2,1)} %collective-permute-done.58.b_ref), channel_id=1, source_target_pairs={{0,4},{4,0},{8,12},{12,8},{16,20},{20,16},{24,28},{28,24},{1,5},{5... | collective-permute-start | bytes 3244040 | tf_op jit(solution)/shard_map/cond/branch_1_fun/ppermute | solution.py:498
  83.9 36.7 %collective-permute-start.65 = (bf16[33,128,128]{2,1,0:T(8,128)(2,1)}, bf16[33,128,128]{2,1,0:T(8,128)(2,1)}, u32[]{:S(2)}, u32[]{:S(2)}) collective-permute-start(bf16[33,128,128]{2,1,0:T(8,128)(2,1)} %collective-permute-done.64.a_ref), channel_id=1, source_target_pairs={{0,4},{4,0},{8,12},{12,8},{16,20},{20,16},{24,28},{28,24},{1,5},{5... | collective-permute-start | bytes 3244040 | tf_op jit(solution)/shard_map/cond/branch_1_fun/ppermute | solution.py:498
  118.7 36.6 %collective-permute-start.53 = (bf16[576,1280]{1,0:T(8,128)(2,1)S(1)}, bf16[576,1280]{1,0:T(8,128)(2,1)}, u32[]{:S(2)}, u32[]{:S(2)}) collective-permute-start(bf16[576,1280]{1,0:T(8,128)(2,1)S(1)} %collective-permute-done.52.refs_1_), channel_id=1, source_target_pairs={{0,1},{1,2},{2,3},{3,0},{4,5},{5,6},{6,7},{7,4},{8,9},{9,10},{10,1... | collective-permute-start | bytes 4423688 | tf_op jit(solution)/shard_map/cond/branch_1_fun/ppermute | solution.py:543
  123.2 33.8 %collective-permute-start.57 = (bf16[33,128,128]{2,1,0:T(8,128)(2,1)}, bf16[33,128,128]{2,1,0:T(8,128)(2,1)}, u32[]{:S(2)}, u32[]{:S(2)}) collective-permute-start(bf16[33,128,128]{2,1,0:T(8,128)(2,1)} %collective-permute-done.56.a_ref), channel_id=1, source_target_pairs={{0,4},{4,0},{8,12},{12,8},{16,20},{20,16},{24,28},{28,24},{1,5},{5... | collective-permute-start | bytes 3244040 | tf_op jit(solution)/shard_map/cond/branch_1_fun/ppermute | solution.py:498
  157.0 30.4 %collective-permute-start.86 = (bf16[18,128,128]{2,1,0:T(8,128)(2,1)}, bf16[18,128,128]{2,1,0:T(8,128)(2,1)}, u32[]{:S(2)}, u32[]{:S(2)}) collective-permute-start(bf16[18,128,128]{2,1,0:T(8,128)(2,1)} %collective-permute-done.85.a_ref), channel_id=1, source_target_pairs={{0,4},{4,0},{8,12},{12,8},{16,20},{20,16},{24,28},{28,24},{1,5},{5... | collective-permute-start | bytes 1769480 | tf_op jit(solution)/shard_map/cond/branch_1_fun/ppermute | solution.py:498
  157.5 87.9 %collective-permute-start.82 = (bf16[18,128,128]{2,1,0:T(8,128)(2,1)}, bf16[18,128,128]{2,1,0:T(8,128)(2,1)}, u32[]{:S(2)}, u32[]{:S(2)}) collective-permute-start(bf16[18,128,128]{2,1,0:T(8,128)(2,1)} %collective-permute-done.76.a_ref), channel_id=1, source_target_pairs={{0,4},{4,0},{8,12},{12,8},{16,20},{20,16},{24,28},{28,24},{1,5},{5... | collective-permute-start | bytes 1769480 | tf_op jit(solution)/shard_map/cond/branch_1_fun/ppermute | solution.py:498
  158.1 87.3 %collective-permute-start.84 = (bf16[18,128,128]{2,1,0:T(8,128)(2,1)}, bf16[18,128,128]{2,1,0:T(8,128)(2,1)}, u32[]{:S(2)}, u32[]{:S(2)}) collective-permute-start(bf16[18,128,128]{2,1,0:T(8,128)(2,1)} %collective-permute-done.83.b_ref), channel_id=1, source_target_pairs={{0,4},{4,0},{8,12},{12,8},{16,20},{20,16},{24,28},{28,24},{1,5},{5... | collective-permute-start | bytes 1769480 | tf_op jit(solution)/shard_map/cond/branch_1_fun/ppermute | solution.py:498
  170.6 76.3 %collective-permute-start.78 = (bf16[18,128,128]{2,1,0:T(8,128)(2,1)}, bf16[18,128,128]{2,1,0:T(8,128)(2,1)}, u32[]{:S(2)}, u32[]{:S(2)}) collective-permute-start(bf16[18,128,128]{2,1,0:T(8,128)(2,1)} %collective-permute-done.77.a_ref), channel_id=1, source_target_pairs={{0,4},{4,0},{8,12},{12,8},{16,20},{20,16},{24,28},{28,24},{1,5},{5... | collective-permute-start | bytes 1769480 | tf_op jit(solution)/shard_map/cond/branch_1_fun/ppermute | solution.py:498
  170.6 78.8 %collective-permute-start.81 = (bf16[18,128,128]{2,1,0:T(8,128)(2,1)}, bf16[18,128,128]{2,1,0:T(8,128)(2,1)}, u32[]{:S(2)}, u32[]{:S(2)}) collective-permute-start(bf16[18,128,128]{2,1,0:T(8,128)(2,1)} %collective-permute-done.80.b_ref), channel_id=1, source_target_pairs={{0,4},{4,0},{8,12},{12,8},{16,20},{20,16},{24,28},{28,24},{1,5},{5... | collective-permute-start | bytes 1769480 | tf_op jit(solution)/shard_map/cond/branch_1_fun/ppermute | solution.py:498
  187.4 104.1 %collective-permute-start.54 = (bf16[576,1280]{1,0:T(8,128)(2,1)}, bf16[576,1280]{1,0:T(8,128)(2,1)}, u32[]{:S(2)}, u32[]{:S(2)}) collective-permute-start(bf16[576,1280]{1,0:T(8,128)(2,1)} %collective-permute-done.53.refs_2_), channel_id=1, source_target_pairs={{0,1},{1,2},{2,3},{3,0},{4,5},{5,6},{6,7},{7,4},{8,9},{9,10},{10,1... | collective-permute-start | bytes 4423688 | tf_op jit(solution)/shard_map/cond/branch_1_fun/ppermute | solution.py:543
  245.4 66.7 %collective-permute-start.75 = (bf16[3,1280,128]{2,1,0:T(8,128)(2,1)}, bf16[3,1280,128]{2,1,0:T(8,128)(2,1)}, u32[]{:S(2)}, u32[]{:S(2)}) collective-permute-start(bf16[3,1280,128]{2,1,0:T(8,128)(2,1)} %branch_1_fun.57), channel_id=1, source_target_pairs={{0,4},{4,8},{8,12},{12,16},{16,20},{20,24},{24,28},{28,0},{1,5},{5... | collective-permute-start | bytes 2949128 | tf_op jit(solution)/shard_map/cond/branch_1_fun/ppermute | solution.py:564
  245.4 79.9 %collective-permute-start.73 = (bf16[3,1280,128]{2,1,0:T(8,128)(2,1)}, bf16[3,1280,128]{2,1,0:T(8,128)(2,1)}, u32[]{:S(2)}, u32[]{:S(2)}) collective-permute-start(bf16[3,1280,128]{2,1,0:T(8,128)(2,1)} %branch_1_fun.58), channel_id=1, source_target_pairs={{0,8},{4,12},{8,16},{12,20},{16,24},{20,28},{24,0},{28,4},{1,9},{5... | collective-permute-start | bytes 2949128 | tf_op jit(solution)/shard_map/cond/branch_1_fun/ppermute | solution.py:564
  246.9 91.3 %collective-permute-start.71 = (bf16[3,1280,128]{2,1,0:T(8,128)(2,1)}, bf16[3,1280,128]{2,1,0:T(8,128)(2,1)}, u32[]{:S(2)}, u32[]{:S(2)}) collective-permute-start(bf16[3,1280,128]{2,1,0:T(8,128)(2,1)} %branch_1_fun.59), channel_id=1, source_target_pairs={{0,12},{4,16},{8,20},{12,24},{16,28},{20,0},{24,4},{28,8},{1,13},{... | collective-permute-start | bytes 2949128 | tf_op jit(solution)/shard_map/cond/branch_1_fun/ppermute | solution.py:564
  249.4 101.0 %collective-permute-start.69 = (bf16[3,1280,128]{2,1,0:T(8,128)(2,1)}, bf16[3,1280,128]{2,1,0:T(8,128)(2,1)}, u32[]{:S(2)}, u32[]{:S(2)}) collective-permute-start(bf16[3,1280,128]{2,1,0:T(8,128)(2,1)} %branch_1_fun.60), channel_id=1, source_target_pairs={{0,16},{4,20},{8,24},{12,28},{16,0},{20,4},{24,8},{28,12},{1,17},{... | collective-permute-start | bytes 2949128 | tf_op jit(solution)/shard_map/cond/branch_1_fun/ppermute | solution.py:564
  325.3 35.3 %collective-permute-start.99 = (bf16[144,1280]{1,0:T(8,128)(2,1)S(1)}, bf16[144,1280]{1,0:T(8,128)(2,1)S(1)}, u32[]{:S(2)}, u32[]{:S(2)}) collective-permute-start(bf16[144,1280]{1,0:T(8,128)(2,1)S(1)} %branch_1_fun.83), channel_id=1, source_target_pairs={{0,1},{1,2},{2,3},{3,0},{4,5},{5,6},{6,7},{7,4},{8,9},{9,10},{10,1... | collective-permute-start | bytes 1105928 | tf_op jit(solution)/shard_map/cond/branch_1_fun/ppermute | solution.py:601
  336.5 29.0 %collective-permute-start.96 = (bf16[144,1280]{1,0:T(8,128)(2,1)S(1)}, bf16[144,1280]{1,0:T(8,128)(2,1)S(1)}, u32[]{:S(2)}, u32[]{:S(2)}) collective-permute-start(bf16[144,1280]{1,0:T(8,128)(2,1)S(1)} %branch_1_fun.80), channel_id=1, source_target_pairs={{0,1},{1,2},{2,3},{3,0},{4,5},{5,6},{6,7},{7,4},{8,9},{9,10},{10,1... | collective-permute-start | bytes 1105928 | tf_op jit(solution)/shard_map/cond/branch_1_fun/ppermute | solution.py:601
  401.2 27.9 %collective-permute-start.95 = (bf16[144,1280]{1,0:T(8,128)(2,1)S(1)}, bf16[144,1280]{1,0:T(8,128)(2,1)S(1)}, u32[]{:S(2)}, u32[]{:S(2)}) collective-permute-start(bf16[144,1280]{1,0:T(8,128)(2,1)S(1)} %branch_1_fun.79), channel_id=1, source_target_pairs={{0,1},{1,2},{2,3},{3,0},{4,5},{5,6},{6,7},{7,4},{8,9},{9,10},{10,1... | collective-permute-start | bytes 1105928 | tf_op jit(solution)/shard_map/cond/branch_1_fun/ppermute | solution.py:601
  (50 other events, 862.9 us)
Sparse Core Ops, SparseCore 0:
  58.3 47.9 all-gather.6

commit v2 on v0

--- a/solution.py
+++ b/solution.py
@@ -1,6 +1,10 @@
+import functools
+
 import jax
 import jax.numpy as jnp
 from jax import lax
+from jax.experimental import pallas as pl
+from jax.experimental.pallas import tpu as pltpu
 from jax.sharding import PartitionSpec as P
 
 NSTATE = 128
@@ -42,7 +46,7 @@
     return ((row_ids // BLOCK)[:, None] == jnp.arange(block_rows)[None, :]).astype(jnp.float32)
 
 
-def on_device(
+def general(
     frames_in,
     kept_state,
     moved_to,
@@ -145,6 +149,668 @@
     return (mixed.reshape(slots, FRAMES, patch_len, -1), carry_state)
 
 
+HEADDIM = 64
+XZ_SHARE = 0.66
+OUT_SHARE = 0.72
+BF16 = jnp.bfloat16
+F32 = jnp.float32
+MIB = 1 << 20
+
+
+def params(limit=48 * MIB):
+    return pltpu.CompilerParams(vmem_limit_bytes=limit)
+
+
+def cost():
+    return pl.CostEstimate(flops=1, bytes_accessed=1, transcendentals=0)
+
+
+def dot_nt(left, right):
+    return lax.dot_general(left, right, (((1,), (1,)), ((), ())), preferred_element_type=F32)
+
+
+def pack_kernel(block_rows, groups, columns, mask_columns, low_count, room, always, turn, at_ref, mask_ref, x_ref, *rest):
+    out_ref = rest[-1]
+    panel, shard = at_ref[0], at_ref[1]
+    base = 0
+    if low_count == 0:
+        base = 1 + block_rows * always
+        out_ref[0] = jnp.zeros((BLOCK, BLOCK), BF16)
+        for row in range(block_rows):
+            for column in range(always):
+                block = rest[0][column * BLOCK : (column + 1) * BLOCK, row * BLOCK : (row + 1) * BLOCK].T
+                short = BLOCK - block.shape[1]
+                if short:
+                    block = jnp.concatenate([block, jnp.zeros((BLOCK, short), BF16)], axis=1)
+                out_ref[1 + row * always + column] = block
+    count = jnp.int32(-low_count)
+    for row in range(block_rows):
+        for group in range(groups):
+            for column in range(columns):
+                place = ((panel * block_rows + row) * groups + group) * mask_columns + shard * columns + column
+                keep = mask_ref[place] != 0
+                low = (group * columns + column) * BLOCK
+
+                @pl.when(keep & (count >= 0) & (count < room))
+                def _(count=count, low=low, row=row):
+                    block = x_ref[row * BLOCK : (row + 1) * BLOCK, low : low + BLOCK]
+                    out_ref[base + count] = block.T if turn else block
+
+                count = count + keep.astype(jnp.int32)
+
+
+def pack(at, mask, panel, groups, low_count, room, turn, beside=None):
+    rows, width = panel.shape
+    columns = width // groups // BLOCK
+    always = 0 if beside is None else -(-beside.shape[0] // BLOCK)
+    smem = pl.BlockSpec(memory_space=pltpu.SMEM)
+    vmem = pl.BlockSpec(memory_space=pltpu.VMEM)
+    extra = () if beside is None else (beside,)
+    size = room if low_count else 1 + rows // BLOCK * always + room
+    return pl.pallas_call(
+        functools.partial(
+            pack_kernel, rows // BLOCK, groups, columns, mask.shape[-1], low_count, room, always, turn
+        ),
+        out_shape=jax.ShapeDtypeStruct((size, BLOCK, BLOCK), BF16),
+        in_specs=[smem, smem, vmem] + [vmem] * len(extra),
+        out_specs=vmem,
+        compiler_params=params(),
+        cost_estimate=cost(),
+    )(at, mask.reshape(-1), panel, *extra)
+
+
+def unwritten(shape):
+    return pl.pallas_call(
+        lambda out_ref: None,
+        out_shape=jax.ShapeDtypeStruct(shape, BF16),
+        out_specs=pl.BlockSpec(memory_space=pl.ANY),
+        cost_estimate=cost(),
+    )()
+
+
+def slot_table(mask, panels, shard, shards, always):
+    rows = mask.shape[0] // panels
+    mine = lax.dynamic_slice_in_dim(mask, shard * (mask.shape[-1] // shards), mask.shape[-1] // shards, mask.ndim - 1)
+    kept = mine.reshape(panels, -1)
+    size = kept.shape[1]
+    before = (jnp.arange(size)[:, None] < jnp.arange(size)[None, :]).astype(F32)
+    rank = jnp.dot(kept.astype(F32), before).astype(jnp.int32)
+    table = jnp.where(kept != 0, rank + 1 + rows * always, 0).reshape(panels, rows, -1)
+    fixed = 1 + jnp.arange(rows)[:, None] * always + jnp.arange(always)[None, :]
+    fixed = jnp.broadcast_to(fixed[None], (panels, rows, always)).astype(jnp.int32)
+    return jnp.concatenate([table, fixed], axis=2).reshape(-1)
+
+
+def panel_copies(parts, over, panel, held, sems):
+    copies, low = [], 0
+    for i, part in enumerate(parts):
+        copies.append(pltpu.make_async_copy(part, held.at[pl.ds(low, part.shape[0])], sems.at[i]))
+        low += part.shape[0]
+    return copies, pltpu.make_async_copy(over.at[panel], held.at[pl.ds(low, over.shape[1])], sems.at[2])
+
+
+def project_kernel(counts, block_rows, blocks, tiles, at_ref, table_ref, x_ref, over_ref, *refs):
+    out_ref, held, x_held, *dense, total, sems, x_sems, out_sems = refs[len(refs) - 9 :]
+    parts, low = [], 0
+    for count in counts:
+        parts.append(refs[low : low + count])
+        low += count
+    me, extra = at_ref[0], at_ref[2] != 0
+    depth = block_rows * BLOCK
+    pairs = len(counts) // 2
+
+    def fetch(pair):
+        slot, plain, more = pair % 2, [], []
+        for side in range(2):
+            panel = me ^ (2 * pair + side)
+            copies, over = panel_copies(
+                parts[2 * pair + side], over_ref, panel, held.at[slot, side], sems.at[slot, side]
+            )
+            columns = pl.ds(pl.multiple_of(panel * depth, BLOCK), depth)
+            copies.append(
+                pltpu.make_async_copy(
+                    x_ref.at[:, columns], x_held.at[slot, :, pl.ds(side * depth, depth)], x_sems.at[slot, side]
+                )
+            )
+            plain += copies
+            more.append(over)
+        return plain, more
+
+    def start(pair):
+        plain, more = fetch(pair)
+        for copy in plain:
+            copy.start()
+
+        @pl.when(extra)
+        def _():
+            for copy in more:
+                copy.start()
+
+    def wait(pair):
+        plain, more = fetch(pair)
+        for copy in plain:
+            copy.wait()
+
+        @pl.when(extra)
+        def _():
+            for copy in more:
+                copy.wait()
+
+    def out_copy(n):
+        first, size = tiles[n]
+        columns = pl.ds(first * BLOCK, size * BLOCK)
+        return pltpu.make_async_copy(total.at[:, columns], out_ref.at[:, columns], out_sems.at[n])
+
+    def fill(pair, n):
+        first, size = tiles[n]
+        for side in range(2):
+            panel = me ^ (2 * pair + side)
+            for row in range(block_rows):
+                line = (panel * block_rows + row) * blocks + first
+                high = (side * block_rows + row) * BLOCK
+                for column in range(size):
+                    dense[n % 2][high : high + BLOCK, column * BLOCK : (column + 1) * BLOCK] = held[
+                        pair % 2, side, table_ref[line + column]
+                    ]
+
+    def multiply(pair, n):
+        first, size = tiles[n]
+        columns = slice(first * BLOCK, (first + size) * BLOCK)
+        term = jnp.dot(x_held[pair % 2], dense[n % 2][:, : size * BLOCK], preferred_element_type=F32)
+        total[:, columns] = term + jnp.where(pair > 0, total[:, columns], 0.0)
+
+    start(0)
+
+    @pl.loop(0, pairs)
+    def _(pair):
+        for i in range(pairs):
+
+            @pl.when(pair == i)
+            def _(i=i):
+                wait(i)
+                if i + 1 < pairs:
+                    start(i + 1)
+
+        fill(pair, 0)
+        for n in range(len(tiles)):
+            if n + 1 < len(tiles):
+                fill(pair, n + 1)
+            multiply(pair, n)
+
+            @pl.when(pair == pairs - 1)
+            def _(n=n):
+                out_copy(n).start()
+
+    for n in range(len(tiles)):
+        out_copy(n).wait()
+
+
+def project(at, table, features, panels, over, block_rows, wide=4):
+    rows = features.shape[0]
+    count = len(panels)
+    blocks = table.shape[0] // (count * block_rows)
+    size = sum(part.shape[0] for part in panels[0]) + over.shape[1]
+    flat = [part for bits in range(count) for part in panels[bits]]
+    smem = pl.BlockSpec(memory_space=pltpu.SMEM)
+    anywhere = pl.BlockSpec(memory_space=pl.ANY)
+    depth = 2 * block_rows * BLOCK
+    tiles = [(first, min(wide, blocks - first)) for first in range(0, blocks, wide)]
+    return pl.pallas_call(
+        functools.partial(project_kernel, [len(panels[b]) for b in range(count)], block_rows, blocks, tiles),
+        out_shape=jax.ShapeDtypeStruct((rows, blocks * BLOCK), F32),
+        in_specs=[smem, smem] + [anywhere] * (2 + len(flat)),
+        out_specs=anywhere,
+        scratch_shapes=[
+            pltpu.VMEM((2, 2, size, BLOCK, BLOCK), BF16),
+            pltpu.VMEM((2, rows, depth), BF16),
+            pltpu.VMEM((depth, wide * BLOCK), BF16),
+            pltpu.VMEM((depth, wide * BLOCK), BF16),
+            pltpu.VMEM((rows, blocks * BLOCK), F32),
+            pltpu.SemaphoreType.DMA((2, 2, 3)),
+            pltpu.SemaphoreType.DMA((2, 2)),
+            pltpu.SemaphoreType.DMA((len(tiles),)),
+        ],
+        compiler_params=params(56 * MIB),
+        cost_estimate=cost(),
+    )(at, table, features, over, *flat)
+
+
+def expand_kernel(counts, first_pair, block_rows, blocks, at_ref, table_ref, over_ref, *refs):
+    out_ref, held, sems = refs[len(refs) - 3 :]
+    me, extra = at_ref[0], at_ref[2] != 0
+    pairs = len(counts) // 2
+    step = pl.program_id(0)
+
+    def copies(pair):
+        low = sum(counts[: 2 * pair])
+        plain, more = [], []
+        for side in range(2):
+            parts = refs[low : low + counts[2 * pair + side]]
+            low += counts[2 * pair + side]
+            panel = me ^ (2 * (first_pair + pair) + side)
+            some, over = panel_copies(parts, over_ref, panel, held.at[pair, side], sems.at[pair, side])
+            plain += some
+            more.append(over)
+        return plain, more
+
+    @pl.when(step == 0)
+    def _():
+        for pair in range(pairs):
+            plain, more = copies(pair)
+            for copy in plain:
+                copy.start()
+
+            @pl.when(extra)
+            def _(more=more):
+                for copy in more:
+                    copy.start()
+
+    for pair in range(pairs):
+
+        @pl.when(step == pair)
+        def _(pair=pair):
+            plain, more = copies(pair)
+            for copy in plain:
+                copy.wait()
+
+            @pl.when(extra)
+            def _():
+                for copy in more:
+                    copy.wait()
+
+    for side in range(2):
+        panel = me ^ (2 * (first_pair + step) + side)
+        place = (panel % 2) * (block_rows * BLOCK)
+        for row in range(block_rows):
+            columns = pl.ds(pl.multiple_of(place + row * BLOCK, BLOCK), BLOCK)
+            line = (panel * block_rows + row) * blocks
+            for column in range(blocks):
+                out_ref[0, column * BLOCK : (column + 1) * BLOCK, columns] = held[step, side, table_ref[line + column]]
+
+
+def expand(at, table, panels, over, first_pair, pairs, block_rows, before):
+    count = over.shape[0]
+    total_pairs = count // 2
+    blocks = table.shape[0] // (count * block_rows)
+    chosen = [panels[2 * first_pair + i] for i in range(2 * pairs)]
+    flat = [part for parts in chosen for part in parts]
+    size = sum(part.shape[0] for part in chosen[0]) + over.shape[1]
+    anywhere = pl.BlockSpec(memory_space=pl.ANY)
+    shape = (total_pairs, blocks * BLOCK, 2 * block_rows * BLOCK)
+    more = [] if before is None else [before]
+    return pl.pallas_call(
+        functools.partial(expand_kernel, [len(parts) for parts in chosen], first_pair, block_rows, blocks),
+        grid_spec=pltpu.PrefetchScalarGridSpec(
+            num_scalar_prefetch=2,
+            grid=(pairs,),
+            in_specs=[anywhere] * (1 + len(flat) + len(more)),
+            out_specs=pl.BlockSpec((1, *shape[1:]), lambda i, at, table: ((at[0] // 2) ^ (first_pair + i), 0, 0)),
+            scratch_shapes=[
+                pltpu.VMEM((pairs, 2, size, BLOCK, BLOCK), BF16),
+                pltpu.SemaphoreType.DMA((pairs, 2, 3)),
+            ],
+        ),
+        out_shape=jax.ShapeDtypeStruct(shape, BF16),
+        input_output_aliases={3 + len(flat): 0} if more else {},
+        compiler_params=params(),
+        cost_estimate=cost(),
+    )(at, table, over, *flat, *more)
+
+
+def pick_kernel(order_ref, x_ref, out_ref):
+    out_ref[...] = x_ref[...].astype(out_ref.dtype)
+
+
+def pick(order, states):
+    count, block = order.shape[0], (1,) + states.shape[1:]
+    return pl.pallas_call(
+        pick_kernel,
+        grid_spec=pltpu.PrefetchScalarGridSpec(
+            num_scalar_prefetch=1,
+            grid=(count,),
+            in_specs=[pl.BlockSpec(block, lambda i, order: (order[i], 0, 0))],
+            out_specs=pl.BlockSpec(block, lambda i, order: (i, 0, 0)),
+        ),
+        out_shape=jax.ShapeDtypeStruct((count,) + states.shape[1:], BF16),
+        compiler_params=params(),
+        cost_estimate=cost(),
+    )(order, states)
+
+
+def split(values):
+    high = values.astype(BF16)
+    left = values - high.astype(F32)
+    middle = left.astype(BF16)
+    return high, middle, (left - middle.astype(F32)).astype(BF16)
+
+
+def scan_kernel(heads, group_width, slots_ref, total_ref, state_ref, rows_ref, heads_ref, pick_ref, *rest):
+    normed_ref, carry_ref = rest[-2:]
+    length, width = normed_ref.shape
+    head_inputs = total_ref[:, :width]
+    gate_inputs = total_ref[:, width : 2 * width]
+    side = 2 * width
+    input_mix = total_ref[:, side : side + NSTATE].astype(BF16)
+    output_mix = total_ref[:, side + NSTATE : side + 2 * NSTATE].astype(BF16)
+    bias, decay = heads_ref[0:1, :], heads_ref[1:2, :]
+    skip, gain = rows_ref[0:1, :], rows_ref[1:2, :]
+    raw = total_ref[:, side + 2 * NSTATE : side + 2 * NSTATE + heads_ref.shape[1]] + bias
+    steps = jnp.maximum(raw, 0.0) + jnp.log1p(jnp.exp(-jnp.abs(raw)))
+    patch = length // FRAMES
+
+    def token(shape, axis, size):
+        row = lax.broadcasted_iota(jnp.int32, shape, axis) & (size - 1)
+        return (row & (FRAMES - 1)) * patch + row // FRAMES
+
+    square = (length, length)
+    lower = (token(square, 0, 64) >= token(square, 1, 64)).astype(BF16)
+    cumulative = sum(jnp.dot(lower, part, preferred_element_type=F32) for part in split(-(steps * decay)))
+    both = jnp.concatenate(split(jnp.concatenate([steps, cumulative], axis=0)), axis=1)
+    both = jnp.dot(both, pick_ref[...], preferred_element_type=F32)
+    steps, cumulative = both[:length], both[length:]
+    lane = lax.broadcasted_iota(jnp.int32, (length, width), 1) & (HEADDIM - 1)
+    line = lax.broadcasted_iota(jnp.int32, (length, width), 0)
+    own = lane == line
+    cum_row = jnp.sum(jnp.where(own, cumulative, 0.0), axis=0, keepdims=True)
+    step_row = jnp.sum(jnp.where(own, steps, 0.0), axis=0, keepdims=True)
+    last = cumulative[length - 1 : length, :]
+    causal = (token((length, width), 1, HEADDIM) <= token((length, width), 0, 64)) & (lane < length)
+    mixing = jnp.exp(jnp.where(causal, cumulative - cum_row, -1e30)) * step_row
+    half = lax.broadcasted_iota(jnp.int32, (length, 2 * HEADDIM), 1) < HEADDIM
+    spare = jnp.zeros((HEADDIM - length, NSTATE), BF16)
+    twice = jnp.concatenate([input_mix, spare, input_mix, spare], axis=0)
+    scores = dot_nt(output_mix, twice)
+    inputs16 = head_inputs.astype(BF16)
+    inside = []
+    for pair in range(heads // 2):
+        low = pair * 2 * HEADDIM
+        inputs = inputs16[:, low : low + 2 * HEADDIM]
+        zero = jnp.zeros_like(inputs)
+        pad = jnp.zeros((HEADDIM - length, 2 * HEADDIM), BF16)
+        both = jnp.concatenate([jnp.where(half, inputs, zero), pad, jnp.where(half, zero, inputs), pad], axis=0)
+        mix = (mixing[:, low : low + 2 * HEADDIM] * scores).astype(BF16)
+        inside.append(jnp.dot(mix, both, preferred_element_type=F32))
+    inside = jnp.concatenate(inside, axis=1)
+    state = state_ref[0]
+    carried = jnp.exp(cumulative) * dot_nt(output_mix, state)
+    scanned = inside + carried + skip * head_inputs
+    gated = scanned * (gate_inputs / (1.0 + jnp.exp(-gate_inputs)))
+    channel = lax.broadcasted_iota(jnp.int32, (width, 128), 0)
+    member = lax.broadcasted_iota(jnp.int32, (width, 128), 1) * group_width
+    member = ((channel >= member) & (channel < member + group_width)).astype(BF16)
+    squares = jnp.dot((gated * gated).astype(BF16), member, preferred_element_type=F32)
+    scale = lax.rsqrt(squares * (1.0 / group_width) + 1e-05)
+    position = lax.broadcasted_iota(jnp.int32, (length, width), 1)
+    spread_scale = jnp.broadcast_to(scale[:, 0:1], (length, width))
+    for group in range(1, width // group_width):
+        spread_scale = jnp.where(position >= group * group_width, scale[:, group : group + 1], spread_scale)
+    normed_ref[...] = (gated * spread_scale * gain).astype(BF16)
+    to_end = (jnp.exp(last - cumulative) * steps * head_inputs).astype(BF16)
+    added = lax.dot_general(to_end, input_mix, (((0,), (0,)), ((), ())), preferred_element_type=F32)
+    head_rows = -(-heads // 8) * 8
+    head_of = lax.broadcasted_iota(jnp.int32, (head_rows, width), 1)
+    first = lax.broadcasted_iota(jnp.int32, (head_rows, width), 0) * HEADDIM
+    whole = jnp.sum(jnp.where(head_of == first, last, 0.0), axis=1, keepdims=True)
+    whole = jnp.broadcast_to(jnp.exp(whole), (head_rows, NSTATE))
+    for head in range(heads):
+        rows = slice(head * HEADDIM, (head + 1) * HEADDIM)
+        carry_ref[0, rows, :] = state[rows].astype(F32) * whole[head : head + 1, :] + added[rows]
+
+
+def scan(slots, total, state, rows, per_head, picked, carry, total_slots, group_width):
+    count, width, _ = state.shape
+    length = total.shape[0] // total_slots
+    more = [] if carry is None else [pl.BlockSpec(memory_space=pl.ANY)]
+    return pl.pallas_call(
+        functools.partial(scan_kernel, width // HEADDIM, group_width),
+        grid_spec=pltpu.PrefetchScalarGridSpec(
+            num_scalar_prefetch=1,
+            grid=(count,),
+            in_specs=[
+                pl.BlockSpec((length, total.shape[1]), lambda i, slots: (slots[i], 0)),
+                pl.BlockSpec((1, width, NSTATE), lambda i, slots: (i, 0, 0)),
+                pl.BlockSpec(rows.shape, lambda i, slots: (0, 0)),
+                pl.BlockSpec(per_head.shape, lambda i, slots: (0, 0)),
+                pl.BlockSpec(picked.shape, lambda i, slots: (0, 0)),
+            ]
+            + more,
+            out_specs=(
+                pl.BlockSpec((length, width), lambda i, slots: (i, 0)),
+                pl.BlockSpec((1, width, NSTATE), lambda i, slots: (slots[i], 0, 0)),
+            ),
+        ),
+        out_shape=(
+            jax.ShapeDtypeStruct((count * length, width), BF16),
+            jax.ShapeDtypeStruct((total_slots, width, NSTATE), F32),
+        ),
+        input_output_aliases={} if carry is None else {6: 1},
+        compiler_params=params(),
+        cost_estimate=cost(),
+    )(slots, total, state, rows, per_head, picked, *(() if carry is None else (carry,)))
+
+
+def terms_kernel(at_ref, normed_ref, dense_ref, out_ref):
+    out_ref[0] = jnp.dot(normed_ref[...], dense_ref[0], preferred_element_type=F32).astype(BF16)
+
+
+def terms(at, normed, dense, first, count):
+    rows, depth = normed.shape
+    shards, _, width = dense.shape
+    return pl.pallas_call(
+        terms_kernel,
+        grid_spec=pltpu.PrefetchScalarGridSpec(
+            num_scalar_prefetch=1,
+            grid=(count,),
+            in_specs=[
+                pl.BlockSpec((rows, depth), lambda i, at: (0, 0)),
+                pl.BlockSpec((1, depth, width), lambda i, at: (lax.rem(at[1] + 2 * shards - first - i, shards), 0, 0)),
+            ],
+            out_specs=pl.BlockSpec((1, rows, width), lambda i, at: (i, 0, 0)),
+        ),
+        out_shape=jax.ShapeDtypeStruct((count, rows, width), BF16),
+        compiler_params=params(),
+        cost_estimate=cost(),
+    )(at, normed, dense)
+
+
+def add(got, term):
+    return (got.astype(F32) + term.astype(F32)).astype(BF16)
+
+
+def place_kernel(slots_ref, got_ref, term_ref, *rest):
+    out_ref = rest[-1]
+    total = got_ref[...].astype(F32) + term_ref[0].astype(F32)
+    patch, frames = out_ref.shape[1:3]
+    for token in range(patch):
+        out_ref[0, token] = total[token * frames : (token + 1) * frames].astype(BF16)
+
+
+def place(slots, got, term, which, total_slots, before):
+    rows, width = got.shape
+    count = slots.shape[0]
+    patch = rows // count // FRAMES
+    return pl.pallas_call(
+        place_kernel,
+        grid_spec=pltpu.PrefetchScalarGridSpec(
+            num_scalar_prefetch=1,
+            grid=(count,),
+            in_specs=[
+                pl.BlockSpec((rows // count, width), lambda i, slots: (i, 0)),
+                pl.BlockSpec((1, rows // count, width), lambda i, slots: (which, i, 0)),
+            ]
+            + ([] if before is None else [pl.BlockSpec(memory_space=pl.ANY)]),
+            out_specs=pl.BlockSpec((1, patch, FRAMES, width), lambda i, slots: (slots[i], 0, 0, 0)),
+        ),
+        out_shape=jax.ShapeDtypeStruct((total_slots, patch, FRAMES, width), BF16),
+        input_output_aliases={} if before is None else {3: 0},
+        compiler_params=params(),
+        cost_estimate=cost(),
+    )(slots, got, term, *(() if before is None else (before,)))
+
+
+def swap(value, bit, size):
+    return lax.ppermute(value, "stream", [(i, i ^ bit) for i in range(size)])
+
+
+def cube(own, size):
+    return {0: [own], 2: [swap(own, 2, size)], 4: [swap(own, 4, size)]}
+
+
+def cube_rest(got, size, near):
+    half = got[0][0].shape[0] // 2
+    got[6] = [swap(got[4][0][:half], 2, size), swap(got[2][0][half:], 4, size)]
+    for bits in near:
+        got[bits | 1] = [swap(part, 1, size) for part in got[bits]]
+    return got
+
+
+def after(values, earlier):
+    return lax.optimization_barrier((values, earlier))[0]
+
+
+def sparse(
+    frames_in,
+    kept_state,
+    moved_to,
+    xz_weight,
+    side_weight,
+    xz_mask,
+    dt_bias,
+    decay_rate,
+    skip_gain,
+    norm_gain,
+    out_weight,
+    out_mask,
+):
+    streams, shards = lax.axis_size("stream"), lax.axis_size("shard")
+    me, shard = lax.axis_index("stream"), lax.axis_index("shard")
+    slots, heads = kept_state.shape[:2]
+    width = heads * HEADDIM
+    block_rows = out_weight.shape[0] // BLOCK
+    out_blocks = block_rows * (width // BLOCK)
+    xz_room, out_room = int(2 * out_blocks * XZ_SHARE), int(out_blocks * OUT_SHARE)
+    at = jnp.stack([me, shard]).astype(jnp.int32)
+
+    frames = frames_in.transpose(0, 2, 1, 3).reshape(-1, frames_in.shape[3])
+    features = lax.all_gather(frames, "shard", axis=1, tiled=True)
+
+    side_blocks = -(-side_weight.shape[1] // BLOCK)
+    xz_panel = after(xz_weight, frames).reshape(xz_weight.shape[0], -1)
+    xz_packed = pack(at, xz_mask, xz_panel, 2, 0, xz_room, False, side_weight.T)
+    xz_panels = cube(xz_packed, streams)
+
+    steps = (1, 2, 3, streams // 2)
+    match = (moved_to // slots - me) % streams == jnp.array(steps)[:, None]
+    rank = jnp.cumsum(match.astype(jnp.int32), axis=1) - 1
+    chosen = match[:, None, :] & (rank[:, None, :] == jnp.arange(MOST)[None, :, None])
+    order = jnp.sum(jnp.where(chosen, jnp.arange(slots), 0), axis=2, dtype=jnp.int32)
+    landing = jnp.sum(jnp.where(chosen, moved_to % slots, 0), axis=2, dtype=jnp.int32)
+
+    def move(values, k):
+        return lax.ppermute(values, "stream", [(i, (i + steps[k]) % streams) for i in range(streams)])
+
+    landing = [move(after(landing, xz_packed)[k], k) for k in range(len(steps))]
+    order = after(order, xz_packed)
+    flat_state = kept_state.reshape(slots, width, NSTATE)
+    sends = [pick(order[k], flat_state) for k in range(len(steps))]
+    out_packed = pack(at, after(out_mask, xz_packed), out_weight, 1, 0, out_room, True)
+    xz_table = slot_table(xz_mask, streams, shard, shards, side_blocks)
+    out_table = slot_table(out_mask, streams, shard, shards, 0)
+    head_of = jnp.arange(width) // HEADDIM
+    picked = (shard * heads + head_of[None, :] == jnp.arange(BLOCK)[:, None]).astype(BF16)
+    picked = jnp.concatenate([picked] * 3, axis=0)
+    per_head = jnp.zeros((8, BLOCK), F32)
+    per_head = lax.dynamic_update_slice(per_head, jnp.stack([dt_bias, decay_rate]), (0, shard * heads))
+    rows = jnp.stack([jnp.repeat(skip_gain, HEADDIM), norm_gain] + [jnp.zeros_like(norm_gain)] * 6)
+
+    xz_panels[2], xz_panels[4] = after(
+        (xz_panels[2], xz_panels[4]), (sends, out_packed, xz_table, out_table, picked, per_head, rows, landing)
+    )
+    xz_panels = cube_rest(xz_panels, streams, (0, 2, 4, 6))
+
+    sends[0], out_packed = after((sends[0], out_packed), xz_panels[6])
+    got = [move(sends[0], 0)]
+    out_panels = cube(out_packed, streams)
+    masks = after((xz_mask, out_mask), (xz_panels[6], features))
+    kept_xz, kept_out = (fullest(mask, streams, shards) for mask in masks)
+    extra = (kept_xz > xz_room) | (kept_out > out_room)
+    spare_xz, spare_out = 2 * out_blocks - xz_room, out_blocks - out_room
+
+    def none(*_):
+        return unwritten((streams, spare_xz, BLOCK, BLOCK)), unwritten((streams, spare_out, BLOCK, BLOCK))
+
+    def some(xz_panel, out_weight):
+        over_xz = pack(at, xz_mask, xz_panel, 2, xz_room, spare_xz, False)
+        over_out = pack(at, out_mask, out_weight, 1, out_room, spare_out, True)
+        return tuple(lax.all_gather(over, "stream", axis=0) for over in (over_xz, over_out))
+
+    over_xz, over_out = lax.cond(extra, some, none, xz_panel, out_weight)
+    at = jnp.concatenate([at, extra.astype(jnp.int32)[None]])
+    total = project(after(at, got[0]), xz_table, features, xz_panels, over_xz, block_rows)
+    out_panels[2], out_panels[4], total = lax.optimization_barrier((out_panels[2], out_panels[4], total))
+    out_panels = cube_rest(out_panels, streams, (0, 2, 4))
+    sends[1:] = after(sends[1:], out_panels[6])
+    got += [move(sends[k], k) for k in range(1, len(steps))]
+
+    pairs = streams // 2
+    ring = [(i, (i + 1) % shards) for i in range(shards)]
+    count = len(steps)
+
+    def scan_chunk(k, total, carry):
+        return scan(landing[k], total, got[k], rows, per_head, picked, carry, slots, DINNER // NORM_GROUPS)
+
+    dense = expand(at, out_table, out_panels, over_out, 0, pairs - 1, block_rows, None)
+    done, carry = scan_chunk(0, total, None)
+    last = after(out_panels[2 * pairs - 2], (dense, done))
+    out_panels[2 * pairs - 2] = last
+    out_panels[2 * pairs - 1] = [swap(part, 1, streams) for part in last]
+    dense = expand(at, out_table, out_panels, over_out, pairs - 1, 1, block_rows, dense)
+
+    mixed, moving, term = None, [], []
+    for step in range(count + shards - 1):
+        if step < count:
+            if step:
+                done, carry = scan_chunk(step, total, carry)
+            first = terms(at, done, dense, 1, 1)
+            moving.append(lax.ppermute(first[0], "shard", ring))
+            term.append(terms(at, after(done, first), dense, 2, shards - 1))
+        passed = []
+        for k in range(max(step - shards, 0), min(step, count)):
+            hop = step - k + 1
+            if hop < shards:
+                passed.append(add(moving[k], term[k][hop - 2]))
+                moving[k] = lax.ppermute(passed[-1], "shard", ring)
+            elif hop == shards:
+                mixed = place(landing[k], moving[k], term[k], shards - 2, slots, mixed)
+        total = after(total, (term[-1], passed))
+    return mixed.transpose(0, 2, 1, 3), carry.reshape(kept_state.shape)
+
+
+def fullest(mask, panels, shards):
+    rows = mask.reshape(panels, -1, mask.shape[-1])
+    cells = rows.reshape(panels, rows.shape[1], shards, -1)
+    return jnp.max(jnp.sum(cells, axis=(1, 3)))
+
+
+def on_device(streams, shards, *args):
+    xz_weight, out_weight, kept_state = args[3], args[10], args[1]
+    rows, width = out_weight.shape
+    regular = (
+        streams == 8
+        and streams % shards == 0
+        and rows % BLOCK == 0
+        and width % BLOCK == 0
+        and width % (DINNER // NORM_GROUPS) == 0
+        and width == (streams // shards) * rows
+        and streams // shards == 2
+        and args[9].shape[0] == width
+        and kept_state.shape[1] % 2 == 0
+    )
+    if not regular:
+        return general(*args)
+    return sparse(*args)
+
+
 def solution(mesh):
     placed = (
         P("stream", None, None, "shard"),
@@ -161,7 +827,7 @@
         P(),
     )
     return jax.shard_map(
-        on_device,
+        functools.partial(on_device, mesh.shape["stream"], mesh.shape["shard"]),
         mesh=mesh,
         in_specs=placed,
         out_specs=(P("stream", None, None, "shard"), P("stream", "shard", None, None)),

time: 648 us -> 343 us (0.53)
  matrix products: 210 us -> 0.26 us
  Pallas kernels: 0 us -> 125 us
  waiting for transfers between devices: 252 us -> 140 us
  local copies, waits for them, and re-layouts: 122 us -> 24.3 us
  other arithmetic: 33.3 us -> 6.8 us
  starting transfers between devices: 10.4 us -> 30.5 us
    dot_general x21 -> x2, matrix products: 210 us -> 0.26 us  [slot_table(): rank = jnp.dot(kept.astype(F32), before).astype(jnp.int32)]
    ppermute x0 -> x38, waiting for transfers between devices: none -> 140 us  [the longest x8 60 us: move(): lax.ppermute(values, 'stream', [(i, (i + steps[k]) % streams) for i in ra...]
    pallas_call x0 -> x27, Pallas kernels: none -> 125 us  [the longest x8 35.9 us: terms(): pl.pallas_call(terms_kernel, grid_spec=pltpu.PrefetchScalarGridSpec(num_s...]
    reduce_scatter x1 -> x0, waiting for transfers between devices: 85.9 us -> none  [on_device(): lax.psum_scatter(partial_out.astype(jnp.bfloat16), 'shard', scatter_dimen...]
    all_to_all x2 -> x0, waiting for transfers between devices: 84.3 us -> none  [the longest x1 84.3 us: on_device(): lax.all_to_all(send_states.astype(jnp.bfloat16), 'stream', split_axis=0,...]
    all_gather x4 -> x1, waiting for transfers between devices: 79.6 us -> 0.01 us  [sparse(): features = lax.all_gather(frames, 'shard', axis=1, tiled=True)]
    scatter x3 -> x0, local copies, waits for them, and re-layouts: 38.2 us -> none  [the longest x1 24.1 us: on_device(): jnp.zeros_like(kept_state).at[landing].set(got_states, mode='drop')]
    ppermute x0 -> x38, starting transfers between devices: none -> 30.5 us  [the longest x18 13.9 us: swap(): return lax.ppermute(value, 'stream', [(i, i ^ bit) for i in range(size)])]
  transfers between devices with their start and end apart: 7 -> 39, of which waited for: 3 -> 14; matrix products, arithmetic and copies ran while one was open for 53% -> 6% of each run, Pallas kernels for 0% -> 36%
where the time goes in v2:
time: 343 us; the launch traced here: 342 us
  waiting for transfers between devices  140 us (41%)
  Pallas kernels  125 us (36%)
  starting transfers between devices  30.5 us (9%)
  local copies, waits for them, and re-layouts  24.3 us (7%)
  between operations  15.9 us (5%)
  other arithmetic  6.8 us (2%)
    ppermute x8, waiting for transfers between devices, move(): lax.ppermute(values, 'stream', [(i, (i + steps[k]) % streams) for i in ra...  60 us
    pallas_call x8, Pallas kernels, terms(): pl.pallas_call(terms_kernel, grid_spec=pltpu.PrefetchScalarGridSpec(num_s...  35.9 us
    ppermute x18, waiting for transfers between devices, swap(): return lax.ppermute(value, 'stream', [(i, i ^ bit) for i in range(size)])  31.1 us
    pallas_call x1, Pallas kernels, project(): pl.pallas_call(functools.partial(project_kernel, [len(panels[b]) for b in...  26.5 us
    ppermute x4, waiting for transfers between devices, sparse(): moving.append(lax.ppermute(first[0], 'shard', ring))  25 us
    pallas_call x4, Pallas kernels, scan(): pl.pallas_call(functools.partial(scan_kernel, width // HEADDIM, group_wid...  24.2 us
    ppermute x8, waiting for transfers between devices, sparse(): moving[k] = lax.ppermute(passed[-1], 'shard', ring)  23.5 us
    ppermute x18, starting transfers between devices, swap(): return lax.ppermute(value, 'stream', [(i, i ^ bit) for i in range(size)])  13.9 us
  transfers between devices with their start and end apart: 39, of which 14 were waited for; matrix products, arithmetic and copies ran while one was open for 6% of the time, Pallas kernels for 36%

profile of v2, /device:TPU:0, one launch (start us, length us, event | category | flops | bytes accessed | tf_op | source)
XLA Modules:
  0.0 342.1 jit_solution(15454351359083143952)
XLA Ops:
  7.2 3.6 %reshape.150 = bf16[576,1280]{1,0:T(8,128)(2,1)} reshape(bf16[12,12,4,1280]{3,2,1,0:T(4,128)(2,1)} %bitcast.76) | data formatting | bytes 2949120 | tf_op jit(solution)/shard_map/reshape | solution.py:694
  10.9 4.2 %copy.28 = bf16[80,8,2,1280]{3,1,2,0:T(8,128)(2,1)} copy(bf16[80,8,2,1280]{3,2,1,0:T(2,128)(2,1)} %bitcast.75) | data formatting | bytes 6553600
  15.3 4.7 %shard_map.140.refs_0_ = bf16[82,128,128]{2,1,0:T(8,128)(2,1)} custom-call(s32[2]{0:T(128)S(1)} %pad_add_fusion.1.at_ref, s32[3200]{0:T(1024)S(1)} %reshape.149.mask_ref, bf16[640,2560]{1,0:T(8,128)(2,1)} %bitcast.72, bf16[336,640]{1,0:T(8,128)(2,1)S(1)} %bitcast.60), custom_call_target="tpu_custom_call" | custom-call | flops 1 | bytes 1 | tf_op jit(solution)/shard_map/pallas_call | solution.py:210
  48.0 35.0 %collective-permute-done.slots_ref = s32[3]{0:T(128)S(1)} collective-permute-done((s32[3]{0:T(128)S(1)}, s32[3]{0:T(128)S(1)}, u32[]{:S(2)}, u32[]{:S(2)}) %collective-permute-start) | collective-permute-done | bytes 44 | tf_op jit(solution)/shard_map/ppermute | solution.py:710
  93.0 27.6 %collective-permute-done.6.refs_6_ = bf16[41,128,128]{2,1,0:T(8,128)(2,1)S(1)} collective-permute-done((bf16[41,128,128]{2,1,0:T(8,128)(2,1)S(1)}, bf16[41,128,128]{2,1,0:T(8,128)(2,1)S(1)}, u32[]{:S(2)}, u32[]{:S(2)}) %collective-permute-start.6) | collective-permute-done | bytes 1343520 | tf_op jit(solution)/shard_map/ppermute | solution.py:652
  124.1 12.6 %collective-permute-done.10.state_ref = bf16[3,1280,128]{2,1,0:T(8,128)(2,1)S(1)} collective-permute-done((bf16[3,1280,128]{2,1,0:T(8,128)(2,1)S(1)}, bf16[3,1280,128]{2,1,0:T(8,128)(2,1)S(1)}, u32[]{:S(2)}, u32[]{:S(2)}) %collective-permute-start.10) | collective-permute-done | bytes 983072 | tf_op jit(solution)/shard_map/ppermute | solution.py:710
  149.4 26.5 %shard_map.146.total_ref = f32[576,2944]{1,0:T(8,128)} custom-call(s32[3]{0:T(128)} %pad_add_fusion.2.at_ref, s32[920]{0:T(1024)} %reshape.155.table_ref, bf16[576,5120]{1,0:T(8,128)(2,1)} %all-gather.10.cloned.1.call-done.x_ref, bf16[8,34,128,128]{3,2,1,0:T(8,128)(2,1)} %get-tuple-element.64.over_ref, bf16[82,128,128]{2,1,0:T(8,128)(2,1)} %shard_map.140.refs_0_, ...), custom_call_target="tpu_custom_call" | custom-call | flops 1 | bytes 1 | tf_op jit(solution)/shard_map/pallas_call | solution.py:358
  180.3 6.3 %shard_map.147 = (bf16[144,1280]{1,0:T(8,128)(2,1)S(1)}, f32[12,1280,128]{2,1,0:T(8,128)}) custom-call(s32[3]{0:T(128)S(1)} %collective-permute-done.3.slots_ref, f32[576,2944]{1,0:T(8,128)} %shard_map.146.total_ref, bf16[3,1280,128]{2,1,0:T(8,128)(2,1)S(1)} %copy-done.8, f32[8,1280]{1,0:T(8,128)S(1)} %maximum_maximum_fusion.rows_ref, ...), custom_call_target="tpu_custom_call" | custom-call | flops 1 | bytes 1 | tf_op jit(solution)/shard_map/pallas_call | solution.py:564
  187.6 7.2 %shard_map.148.refs_4_ = bf16[4,1280,1280]{2,1,0:T(8,128)(2,1)} custom-call(s32[3]{0:T(128)S(1)} %copy-done.12, s32[400]{0:T(512)S(1)} %reshape_reshape.7.table_ref, bf16[8,14,128,128]{3,2,1,0:T(8,128)(2,1)S(1)} %copy-done.13, bf16[37,128,128]{2,1,0:T(8,128)(2,1)S(1)} %shard_map.145.refs_0_, bf16[37,128,128]{2,1,0:T(8,128)(2,1)S(1)} %collective-permute-done.18.refs_1_, ...), custom_call_target="tpu_custom_call" | custom-call | flops 1 | bytes 1 | tf_op jit(solution)/shard_map/pallas_call | solution.py:441
  197.9 3.7 %shard_map.149.dense_ref = bf16[4,1280,1280]{2,1,0:T(8,128)(2,1)} custom-call(s32[3]{0:T(128)S(1)} %copy-done.12, s32[400]{0:T(512)S(1)} %reshape_reshape.7.table_ref, bf16[8,14,128,128]{3,2,1,0:T(8,128)(2,1)S(1)} %copy-done.13, bf16[18,128,128]{2,1,0:T(8,128)(2,1)S(1)} %collective-permute-done.16.refs_0_, ...), custom_call_target="tpu_custom_call", output_to_operand_aliasing={{}: (7, {})} | custom-call | flops 1 | bytes 1 | tf_op jit(solution)/shard_map/pallas_call | solution.py:441
  208.3 5.8 %shard_map.151.term_ref = bf16[3,144,1280]{2,1,0:T(8,128)(2,1)S(1)} custom-call(s32[3]{0:T(128)S(1)} %copy-done.12, bf16[144,1280]{1,0:T(8,128)(2,1)S(1)} %get-tuple-element.72.normed_ref, bf16[4,1280,1280]{2,1,0:T(8,128)(2,1)} %shard_map.149.dense_ref), custom_call_target="tpu_custom_call" | custom-call | flops 1 | bytes 1 | tf_op jit(solution)/shard_map/pallas_call | solution.py:599
  214.1 5.9 %collective-permute-done.23.state_ref = bf16[3,1280,128]{2,1,0:T(8,128)(2,1)S(1)} collective-permute-done((bf16[3,1280,128]{2,1,0:T(8,128)(2,1)S(1)}, bf16[3,1280,128]{2,1,0:T(8,128)(2,1)S(1)}, u32[]{:S(2)}, u32[]{:S(2)}) %collective-permute-start.23) | collective-permute-done | bytes 983072 | tf_op jit(solution)/shard_map/ppermute | solution.py:710
  220.0 6.0 %shard_map.152 = (bf16[144,1280]{1,0:T(8,128)(2,1)S(1)}, f32[12,1280,128]{2,1,0:T(8,128)}) custom-call(s32[3]{0:T(128)S(1)} %collective-permute-done.4.slots_ref, f32[576,2944]{1,0:T(8,128)} %shard_map.146.total_ref, bf16[3,1280,128]{2,1,0:T(8,128)(2,1)S(1)} %collective-permute-done.23.state_ref, ...), custom_call_target="tpu_custom_call", output_to_operand_aliasing={{1}: (6, {})} | custom-call | flops 1 | bytes 1 | tf_op jit(solution)/shard_map/pallas_call | solution.py:564
  229.2 5.8 %shard_map.154.term_ref = bf16[3,144,1280]{2,1,0:T(8,128)(2,1)S(1)} custom-call(s32[3]{0:T(128)S(1)} %copy-done.12, bf16[144,1280]{1,0:T(8,128)(2,1)S(1)} %get-tuple-element.77.normed_ref, bf16[4,1280,1280]{2,1,0:T(8,128)(2,1)} %shard_map.149.dense_ref), custom_call_target="tpu_custom_call" | custom-call | flops 1 | bytes 1 | tf_op jit(solution)/shard_map/pallas_call | solution.py:599
  238.6 9.8 %collective-permute-done.27 = bf16[144,1280]{1,0:T(8,128)(2,1)S(1)} collective-permute-done((bf16[144,1280]{1,0:T(8,128)(2,1)S(1)}, bf16[144,1280]{1,0:T(8,128)(2,1)S(1)}, u32[]{:S(2)}, u32[]{:S(2)}) %collective-permute-start.27) | collective-permute-done | bytes 368672 | tf_op jit(solution)/shard_map/ppermute | solution.py:775
  251.4 6.0 %shard_map.155 = (bf16[144,1280]{1,0:T(8,128)(2,1)S(1)}, f32[12,1280,128]{2,1,0:T(8,128)}) custom-call(s32[3]{0:T(128)S(1)} %collective-permute-done.5.slots_ref, f32[576,2944]{1,0:T(8,128)} %shard_map.146.total_ref, bf16[3,1280,128]{2,1,0:T(8,128)(2,1)S(1)} %collective-permute-done.25.state_ref, ...), custom_call_target="tpu_custom_call", output_to_operand_aliasing={{1}: (6, {})} | custom-call | flops 1 | bytes 1 | tf_op jit(solution)/shard_map/pallas_call | solution.py:564
  260.6 5.8 %shard_map.157.term_ref = bf16[3,144,1280]{2,1,0:T(8,128)(2,1)S(1)} custom-call(s32[3]{0:T(128)S(1)} %copy-done.12, bf16[144,1280]{1,0:T(8,128)(2,1)S(1)} %get-tuple-element.82.normed_ref, bf16[4,1280,1280]{2,1,0:T(8,128)(2,1)} %shard_map.149.dense_ref), custom_call_target="tpu_custom_call" | custom-call | flops 1 | bytes 1 | tf_op jit(solution)/shard_map/pallas_call | solution.py:599
  271.5 6.0 %shard_map.158 = (bf16[144,1280]{1,0:T(8,128)(2,1)S(1)}, f32[12,1280,128]{2,1,0:T(8,128)}) custom-call(s32[3]{0:T(128)S(1)} %collective-permute-done.slots_ref, f32[576,2944]{1,0:T(8,128)} %shard_map.146.total_ref, bf16[3,1280,128]{2,1,0:T(8,128)(2,1)S(1)} %collective-permute-done.28.state_ref, ...), custom_call_target="tpu_custom_call", output_to_operand_aliasing={{1}: (6, {})} | custom-call | flops 1 | bytes 1 | tf_op jit(solution)/shard_map/pallas_call | solution.py:564
  282.4 5.8 %shard_map.160.term_ref = bf16[3,144,1280]{2,1,0:T(8,128)(2,1)S(1)} custom-call(s32[3]{0:T(128)S(1)} %copy-done.12, bf16[144,1280]{1,0:T(8,128)(2,1)S(1)} %get-tuple-element.87.normed_ref, bf16[4,1280,1280]{2,1,0:T(8,128)(2,1)} %shard_map.149.dense_ref), custom_call_target="tpu_custom_call" | custom-call | flops 1 | bytes 1 | tf_op jit(solution)/shard_map/pallas_call | solution.py:599
  288.3 15.2 %collective-permute-done.29 = bf16[144,1280]{1,0:T(8,128)(2,1)S(1)} collective-permute-done((bf16[144,1280]{1,0:T(8,128)(2,1)S(1)}, bf16[144,1280]{1,0:T(8,128)(2,1)S(1)}, u32[]{:S(2)}, u32[]{:S(2)}) %collective-permute-start.29) | collective-permute-done | bytes 368672 | tf_op jit(solution)/shard_map/ppermute | solution.py:775
  303.7 7.7 %collective-permute-done.33 = bf16[144,1280]{1,0:T(8,128)(2,1)S(1)} collective-permute-done((bf16[144,1280]{1,0:T(8,128)(2,1)S(1)}, bf16[144,1280]{1,0:T(8,128)(2,1)S(1)}, u32[]{:S(2)}, u32[]{:S(2)}) %collective-permute-start.33) | collective-permute-done | bytes 368672 | tf_op jit(solution)/shard_map/ppermute | solution.py:782
  311.6 7.7 %collective-permute-done.30 = bf16[144,1280]{1,0:T(8,128)(2,1)S(1)} collective-permute-done((bf16[144,1280]{1,0:T(8,128)(2,1)S(1)}, bf16[144,1280]{1,0:T(8,128)(2,1)S(1)}, u32[]{:S(2)}, u32[]{:S(2)}) %collective-permute-start.30) | collective-permute-done | bytes 368672 | tf_op jit(solution)/shard_map/ppermute | solution.py:782
  323.4 3.8 %collective-permute-done.34.got_ref = bf16[144,1280]{1,0:T(8,128)(2,1)S(1)} collective-permute-done((bf16[144,1280]{1,0:T(8,128)(2,1)S(1)}, bf16[144,1280]{1,0:T(8,128)(2,1)S(1)}, u32[]{:S(2)}, u32[]{:S(2)}) %collective-permute-start.34) | collective-permute-done | bytes 368672 | tf_op jit(solution)/shard_map/ppermute | solution.py:782
  329.1 4.2 %collective-permute-done.31.got_ref = bf16[144,1280]{1,0:T(8,128)(2,1)S(1)} collective-permute-done((bf16[144,1280]{1,0:T(8,128)(2,1)S(1)}, bf16[144,1280]{1,0:T(8,128)(2,1)S(1)}, u32[]{:S(2)}, u32[]{:S(2)}) %collective-permute-start.31) | collective-permute-done | bytes 368672 | tf_op jit(solution)/shard_map/ppermute | solution.py:782
  (194 shorter events, 99.1 us)
Async XLA Ops:
  7.2 133.9 %all-gather.10.cloned.1.call-start = ((), (), s32[]{:S(2)}) async-start(), calls=%async_computation.2 | async-start | bytes 7372800 | tf_op jit(solution)/shard_map/all_gather | solution.py:695
  20.0 67.5 %collective-permute-start.1 = (bf16[82,128,128]{2,1,0:T(8,128)(2,1)}, bf16[82,128,128]{2,1,0:T(8,128)(2,1)}, u32[]{:S(2)}, u32[]{:S(2)}) collective-permute-start(bf16[82,128,128]{2,1,0:T(8,128)(2,1)} %shard_map.140.refs_0_), channel_id=1, source_target_pairs={{0,8},{4,12},{8,0},{12,4},{16,24},{20,28},{24,16},{28,20},{1,9},{5... | collective-permute-start | bytes 8060936 | tf_op jit(solution)/shard_map/ppermute | solution.py:652
  23.0 64.5 %collective-permute-start.2 = (bf16[82,128,128]{2,1,0:T(8,128)(2,1)}, bf16[82,128,128]{2,1,0:T(8,128)(2,1)}, u32[]{:S(2)}, u32[]{:S(2)}) collective-permute-start(bf16[82,128,128]{2,1,0:T(8,128)(2,1)} %shard_map.140.refs_0_), channel_id=1, source_target_pairs={{0,16},{4,20},{8,24},{12,28},{16,0},{20,4},{24,8},{28,12},{1,17},{... | collective-permute-start | bytes 8060936 | tf_op jit(solution)/shard_map/ppermute | solution.py:652
  24.5 97.8 %collective-permute-start.11 = (bf16[82,128,128]{2,1,0:T(8,128)(2,1)}, bf16[82,128,128]{2,1,0:T(8,128)(2,1)}, u32[]{:S(2)}, u32[]{:S(2)}) collective-permute-start(bf16[82,128,128]{2,1,0:T(8,128)(2,1)} %shard_map.140.refs_0_), channel_id=1, source_target_pairs={{0,4},{4,0},{8,12},{12,8},{16,20},{20,16},{24,28},{28,24},{1,5},{5... | collective-permute-start | bytes 8060936 | tf_op jit(solution)/shard_map/ppermute | solution.py:652
  25.2 57.8 %collective-permute-start = (s32[3]{0:T(128)S(1)}, s32[3]{0:T(128)S(1)}, u32[]{:S(2)}, u32[]{:S(2)}) collective-permute-start(s32[3]{0:T(128)S(1)} %get-tuple-element.94), channel_id=1, source_target_pairs={{0,16},{4,20},{8,24},{12,28},{16,0},{20,4},{24,8},{28,12},{1,17},{... | collective-permute-start | bytes 44 | tf_op jit(solution)/shard_map/ppermute | solution.py:710
  25.8 57.6 %collective-permute-start.3 = (s32[3]{0:T(128)S(1)}, s32[3]{0:T(128)S(1)}, u32[]{:S(2)}, u32[]{:S(2)}) collective-permute-start(s32[3]{0:T(128)S(1)} %get-tuple-element.93), channel_id=1, source_target_pairs={{0,4},{4,8},{8,12},{12,16},{16,20},{20,24},{24,28},{28,0},{1,5},{5... | collective-permute-start | bytes 44 | tf_op jit(solution)/shard_map/ppermute | solution.py:710
  88.9 31.7 %collective-permute-start.6 = (bf16[41,128,128]{2,1,0:T(8,128)(2,1)S(1)}, bf16[41,128,128]{2,1,0:T(8,128)(2,1)S(1)}, u32[]{:S(2)}, u32[]{:S(2)}) collective-permute-start(bf16[41,128,128]{2,1,0:T(8,128)(2,1)S(1)} %slice.68), channel_id=1, source_target_pairs={{0,8},{4,12},{8,0},{12,4},{16,24},{20,28},{24,16},{28,20},{1,9},{5... | collective-permute-start | bytes 4030472 | tf_op jit(solution)/shard_map/ppermute | solution.py:652
  91.9 30.3 %collective-permute-start.7 = (bf16[41,128,128]{2,1,0:T(8,128)(2,1)S(1)}, bf16[41,128,128]{2,1,0:T(8,128)(2,1)}, u32[]{:S(2)}, u32[]{:S(2)}) collective-permute-start(bf16[41,128,128]{2,1,0:T(8,128)(2,1)S(1)} %slice.69), channel_id=1, source_target_pairs={{0,16},{4,20},{8,24},{12,28},{16,0},{20,4},{24,8},{28,12},{1,17},{... | collective-permute-start | bytes 4030472 | tf_op jit(solution)/shard_map/ppermute | solution.py:652
  92.5 56.8 %collective-permute-start.12 = (bf16[82,128,128]{2,1,0:T(8,128)(2,1)}, bf16[82,128,128]{2,1,0:T(8,128)(2,1)}, u32[]{:S(2)}, u32[]{:S(2)}) collective-permute-start(bf16[82,128,128]{2,1,0:T(8,128)(2,1)} %collective-permute-done.1.refs_2_), channel_id=1, source_target_pairs={{0,4},{4,0},{8,12},{12,8},{16,20},{20,16},{24,28},{28,24},{1,5},{5... | collective-permute-start | bytes 8060936 | tf_op jit(solution)/shard_map/ppermute | solution.py:652
  92.5 56.8 %collective-permute-start.13 = (bf16[82,128,128]{2,1,0:T(8,128)(2,1)}, bf16[82,128,128]{2,1,0:T(8,128)(2,1)}, u32[]{:S(2)}, u32[]{:S(2)}) collective-permute-start(bf16[82,128,128]{2,1,0:T(8,128)(2,1)} %collective-permute-done.2.refs_4_), channel_id=1, source_target_pairs={{0,4},{4,0},{8,12},{12,8},{16,20},{20,16},{24,28},{28,24},{1,5},{5... | collective-permute-start | bytes 8060936 | tf_op jit(solution)/shard_map/ppermute | solution.py:652
  122.3 27.0 %collective-permute-start.15 = (bf16[41,128,128]{2,1,0:T(8,128)(2,1)}, bf16[41,128,128]{2,1,0:T(8,128)(2,1)}, u32[]{:S(2)}, u32[]{:S(2)}) collective-permute-start(bf16[41,128,128]{2,1,0:T(8,128)(2,1)} %collective-permute-done.7.refs_7_), channel_id=1, source_target_pairs={{0,4},{4,0},{8,12},{12,8},{16,20},{20,16},{24,28},{28,24},{1,5},{5... | collective-permute-start | bytes 4030472 | tf_op jit(solution)/shard_map/ppermute | solution.py:652
  137.7 38.2 %collective-permute-start.8 = (bf16[37,128,128]{2,1,0:T(8,128)(2,1)S(1)}, bf16[37,128,128]{2,1,0:T(8,128)(2,1)S(1)}, u32[]{:S(2)}, u32[]{:S(2)}) collective-permute-start(bf16[37,128,128]{2,1,0:T(8,128)(2,1)S(1)} %shard_map.145.refs_0_), channel_id=1, source_target_pairs={{0,8},{4,12},{8,0},{12,4},{16,24},{20,28},{24,16},{28,20},{1,9},{5... | collective-permute-start | bytes 3637256 | tf_op jit(solution)/shard_map/ppermute | solution.py:652
  139.5 36.3 %collective-permute-start.9 = (bf16[37,128,128]{2,1,0:T(8,128)(2,1)S(1)}, bf16[37,128,128]{2,1,0:T(8,128)(2,1)}, u32[]{:S(2)}, u32[]{:S(2)}) collective-permute-start(bf16[37,128,128]{2,1,0:T(8,128)(2,1)S(1)} %shard_map.145.refs_0_), channel_id=1, source_target_pairs={{0,16},{4,20},{8,24},{12,28},{16,0},{20,4},{24,8},{28,12},{1,17},{... | collective-permute-start | bytes 3637256 | tf_op jit(solution)/shard_map/ppermute | solution.py:652
  149.3 37.2 %collective-permute-start.18 = (bf16[37,128,128]{2,1,0:T(8,128)(2,1)S(1)}, bf16[37,128,128]{2,1,0:T(8,128)(2,1)S(1)}, u32[]{:S(2)}, u32[]{:S(2)}) collective-permute-start(bf16[37,128,128]{2,1,0:T(8,128)(2,1)S(1)} %shard_map.145.refs_0_), channel_id=1, source_target_pairs={{0,4},{4,0},{8,12},{12,8},{16,20},{20,16},{24,28},{28,24},{1,5},{5... | collective-permute-start | bytes 3637256 | tf_op jit(solution)/shard_map/ppermute | solution.py:652
  194.9 25.1 %collective-permute-start.23 = (bf16[3,1280,128]{2,1,0:T(8,128)(2,1)S(1)}, bf16[3,1280,128]{2,1,0:T(8,128)(2,1)S(1)}, u32[]{:S(2)}, u32[]{:S(2)}) collective-permute-start(bf16[3,1280,128]{2,1,0:T(8,128)(2,1)S(1)} %copy-done.6), channel_id=1, source_target_pairs={{0,8},{4,12},{8,16},{12,20},{16,24},{20,28},{24,0},{28,4},{1,9},{5... | collective-permute-start | bytes 2949128 | tf_op jit(solution)/shard_map/ppermute | solution.py:710
  204.8 31.6 %collective-permute-start.24 = (bf16[144,1280]{1,0:T(8,128)(2,1)S(1)}, bf16[144,1280]{1,0:T(8,128)(2,1)S(1)}, u32[]{:S(2)}, u32[]{:S(2)}) collective-permute-start(bf16[144,1280]{1,0:T(8,128)(2,1)S(1)} %bitcast.62), channel_id=1, source_target_pairs={{0,1},{1,2},{2,3},{3,0},{4,5},{5,6},{6,7},{7,4},{8,9},{9,10},{10,1... | collective-permute-start | bytes 1105928 | tf_op jit(solution)/shard_map/ppermute | solution.py:775
  206.3 45.2 %collective-permute-start.25 = (bf16[3,1280,128]{2,1,0:T(8,128)(2,1)S(1)}, bf16[3,1280,128]{2,1,0:T(8,128)(2,1)S(1)}, u32[]{:S(2)}, u32[]{:S(2)}) collective-permute-start(bf16[3,1280,128]{2,1,0:T(8,128)(2,1)S(1)} %copy-done.4), channel_id=1, source_target_pairs={{0,12},{4,16},{8,20},{12,24},{16,28},{20,0},{24,4},{28,8},{1,13},{... | collective-permute-start | bytes 2949128 | tf_op jit(solution)/shard_map/ppermute | solution.py:710
  207.7 63.8 %collective-permute-start.28 = (bf16[3,1280,128]{2,1,0:T(8,128)(2,1)S(1)}, bf16[3,1280,128]{2,1,0:T(8,128)(2,1)S(1)}, u32[]{:S(2)}, u32[]{:S(2)}) collective-permute-start(bf16[3,1280,128]{2,1,0:T(8,128)(2,1)S(1)} %copy-done.2), channel_id=1, source_target_pairs={{0,16},{4,20},{8,24},{12,28},{16,0},{20,4},{24,8},{28,12},{1,17},{... | collective-permute-start | bytes 2949128 | tf_op jit(solution)/shard_map/ppermute | solution.py:710
  236.5 31.3 %collective-permute-start.26 = (bf16[144,1280]{1,0:T(8,128)(2,1)S(1)}, bf16[144,1280]{1,0:T(8,128)(2,1)S(1)}, u32[]{:S(2)}, u32[]{:S(2)}) collective-permute-start(bf16[144,1280]{1,0:T(8,128)(2,1)S(1)} %fusion.11), channel_id=1, source_target_pairs={{0,1},{1,2},{2,3},{3,0},{4,5},{5,6},{6,7},{7,4},{8,9},{9,10},{10,1... | collective-permute-start | bytes 1105928 | tf_op jit(solution)/shard_map/ppermute | solution.py:782
  248.5 21.3 %collective-permute-start.35 = (bf16[144,1280]{1,0:T(8,128)(2,1)S(1)}, bf16[144,1280]{1,0:T(8,128)(2,1)S(1)}, u32[]{:S(2)}, u32[]{:S(2)}) collective-permute-start(bf16[144,1280]{1,0:T(8,128)(2,1)S(1)} %fusion.9), channel_id=1, source_target_pairs={{0,1},{1,2},{2,3},{3,0},{4,5},{5,6},{6,7},{7,4},{8,9},{9,10},{10,1... | collective-permute-start | bytes 1105928 | tf_op jit(solution)/shard_map/ppermute | solution.py:782
  267.9 51.5 %collective-permute-start.37 = (bf16[144,1280]{1,0:T(8,128)(2,1)S(1)}, bf16[144,1280]{1,0:T(8,128)(2,1)S(1)}, u32[]{:S(2)}, u32[]{:S(2)}) collective-permute-start(bf16[144,1280]{1,0:T(8,128)(2,1)S(1)} %fusion.10), channel_id=1, source_target_pairs={{0,1},{1,2},{2,3},{3,0},{4,5},{5,6},{6,7},{7,4},{8,9},{9,10},{10,1... | collective-permute-start | bytes 1105928 | tf_op jit(solution)/shard_map/ppermute | solution.py:782
  269.9 51.6 %collective-permute-start.36 = (bf16[144,1280]{1,0:T(8,128)(2,1)S(1)}, bf16[144,1280]{1,0:T(8,128)(2,1)S(1)}, u32[]{:S(2)}, u32[]{:S(2)}) collective-permute-start(bf16[144,1280]{1,0:T(8,128)(2,1)S(1)} %fusion.4), channel_id=1, source_target_pairs={{0,1},{1,2},{2,3},{3,0},{4,5},{5,6},{6,7},{7,4},{8,9},{9,10},{10,1... | collective-permute-start | bytes 1105928 | tf_op jit(solution)/shard_map/ppermute | solution.py:782
  280.7 22.9 %collective-permute-start.29 = (bf16[144,1280]{1,0:T(8,128)(2,1)S(1)}, bf16[144,1280]{1,0:T(8,128)(2,1)S(1)}, u32[]{:S(2)}, u32[]{:S(2)}) collective-permute-start(bf16[144,1280]{1,0:T(8,128)(2,1)S(1)} %bitcast.63), channel_id=1, source_target_pairs={{0,1},{1,2},{2,3},{3,0},{4,5},{5,6},{6,7},{7,4},{8,9},{9,10},{10,1... | collective-permute-start | bytes 1105928 | tf_op jit(solution)/shard_map/ppermute | solution.py:775
  281.0 30.4 %collective-permute-start.33 = (bf16[144,1280]{1,0:T(8,128)(2,1)S(1)}, bf16[144,1280]{1,0:T(8,128)(2,1)S(1)}, u32[]{:S(2)}, u32[]{:S(2)}) collective-permute-start(bf16[144,1280]{1,0:T(8,128)(2,1)S(1)} %fusion.6), channel_id=1, source_target_pairs={{0,1},{1,2},{2,3},{3,0},{4,5},{5,6},{6,7},{7,4},{8,9},{9,10},{10,1... | collective-permute-start | bytes 1105928 | tf_op jit(solution)/shard_map/ppermute | solution.py:782
  (39 other events, 340.3 us)
Sparse Core Ops, SparseCore 0:
  10.9 111.5 all-gather.9

commit v3 on v2

--- a/solution.py
+++ b/solution.py
@@ -373,88 +373,6 @@
         compiler_params=params(56 * MIB),
         cost_estimate=cost(),
     )(at, table, features, over, *flat)
-
-
-def expand_kernel(counts, first_pair, block_rows, blocks, at_ref, table_ref, over_ref, *refs):
-    out_ref, held, sems = refs[len(refs) - 3 :]
-    me, extra = at_ref[0], at_ref[2] != 0
-    pairs = len(counts) // 2
-    step = pl.program_id(0)
-
-    def copies(pair):
-        low = sum(counts[: 2 * pair])
-        plain, more = [], []
-        for side in range(2):
-            parts = refs[low : low + counts[2 * pair + side]]
-            low += counts[2 * pair + side]
-            panel = me ^ (2 * (first_pair + pair) + side)
-            some, over = panel_copies(parts, over_ref, panel, held.at[pair, side], sems.at[pair, side])
-            plain += some
-            more.append(over)
-        return plain, more
-
-    @pl.when(step == 0)
-    def _():
-        for pair in range(pairs):
-            plain, more = copies(pair)
-            for copy in plain:
-                copy.start()
-
-            @pl.when(extra)
-            def _(more=more):
-                for copy in more:
-                    copy.start()
-
-    for pair in range(pairs):
-
-        @pl.when(step == pair)
-        def _(pair=pair):
-            plain, more = copies(pair)
-            for copy in plain:
-                copy.wait()
-
-            @pl.when(extra)
-            def _():
-                for copy in more:
-                    copy.wait()
-
-    for side in range(2):
-        panel = me ^ (2 * (first_pair + step) + side)
-        place = (panel % 2) * (block_rows * BLOCK)
-        for row in range(block_rows):
-            columns = pl.ds(pl.multiple_of(place + row * BLOCK, BLOCK), BLOCK)
-            line = (panel * block_rows + row) * blocks
-            for column in range(blocks):
-                out_ref[0, column * BLOCK : (column + 1) * BLOCK, columns] = held[step, side, table_ref[line + column]]
-
-
-def expand(at, table, panels, over, first_pair, pairs, block_rows, before):
-    count = over.shape[0]
-    total_pairs = count // 2
-    blocks = table.shape[0] // (count * block_rows)
-    chosen = [panels[2 * first_pair + i] for i in range(2 * pairs)]
-    flat = [part for parts in chosen for part in parts]
-    size = sum(part.shape[0] for part in chosen[0]) + over.shape[1]
-    anywhere = pl.BlockSpec(memory_space=pl.ANY)
-    shape = (total_pairs, blocks * BLOCK, 2 * block_rows * BLOCK)
-    more = [] if before is None else [before]
-    return pl.pallas_call(
-        functools.partial(expand_kernel, [len(parts) for parts in chosen], first_pair, block_rows, blocks),
-        grid_spec=pltpu.PrefetchScalarGridSpec(
-            num_scalar_prefetch=2,
-            grid=(pairs,),
-            in_specs=[anywhere] * (1 + len(flat) + len(more)),
-            out_specs=pl.BlockSpec((1, *shape[1:]), lambda i, at, table: ((at[0] // 2) ^ (first_pair + i), 0, 0)),
-            scratch_shapes=[
-                pltpu.VMEM((pairs, 2, size, BLOCK, BLOCK), BF16),
-                pltpu.SemaphoreType.DMA((pairs, 2, 3)),
-            ],
-        ),
-        out_shape=jax.ShapeDtypeStruct(shape, BF16),
-        input_output_aliases={3 + len(flat): 0} if more else {},
-        compiler_params=params(),
-        cost_estimate=cost(),
-    )(at, table, over, *flat, *more)
 
 
 def pick_kernel(order_ref, x_ref, out_ref):
@@ -589,43 +507,127 @@
     )(slots, total, state, rows, per_head, picked, *(() if carry is None else (carry,)))
 
 
-def terms_kernel(at_ref, normed_ref, dense_ref, out_ref):
-    out_ref[0] = jnp.dot(normed_ref[...], dense_ref[0], preferred_element_type=F32).astype(BF16)
-
-
-def terms(at, normed, dense, first, count):
+def expand_terms_kernel(counts, block_rows, blocks, first_pair, at_ref, table_ref, normed_ref, over_ref, *refs):
+    term_ref, dense_ref, held, sems = refs[len(refs) - 4 :]
+    me, extra = at_ref[0], at_ref[2] != 0
+    pairs = len(counts) // 2
+    step = pl.program_id(0)
+
+    def each(number, act):
+        slot = number % 2
+        for pair in range(pairs):
+            low = sum(counts[: 2 * pair])
+
+            @pl.when(number == pair)
+            def _(pair=pair, low=low):
+                for side in range(2):
+                    parts = refs[low : low + counts[2 * pair + side]]
+                    low += counts[2 * pair + side]
+                    panel = me ^ (2 * (first_pair + pair) + side)
+                    plain, over = panel_copies(parts, over_ref, panel, held.at[slot, side], sems.at[slot, side])
+                    for copy in plain:
+                        act(copy)
+
+                    @pl.when(extra)
+                    def _(over=over):
+                        act(over)
+
+    @pl.when(step == 0)
+    def _():
+        each(0, lambda copy: copy.start())
+
+    @pl.when(step + 1 < pairs)
+    def _():
+        each(step + 1, lambda copy: copy.start())
+
+    each(step, lambda copy: copy.wait())
+    for side in range(2):
+        panel = me ^ (2 * (first_pair + step) + side)
+        place = (panel % 2) * (block_rows * BLOCK)
+        for row in range(block_rows):
+            columns = pl.ds(pl.multiple_of(place + row * BLOCK, BLOCK), BLOCK)
+            line = (panel * block_rows + row) * blocks
+            for column in range(blocks):
+                dense_ref[0, column * BLOCK : (column + 1) * BLOCK, columns] = held[
+                    step % 2, side, table_ref[line + column]
+                ]
+    term_ref[...] = jnp.dot(normed_ref[...], dense_ref[0], preferred_element_type=F32).astype(BF16)
+
+
+def expand_terms(at, table, normed, panels, over, first_pair, pairs, block_rows, before):
+    rows, depth = normed.shape
+    count = over.shape[0]
+    blocks = table.shape[0] // (count * block_rows)
+    chosen = [panels[2 * first_pair + i] for i in range(2 * pairs)]
+    flat = [part for parts in chosen for part in parts]
+    size = sum(part.shape[0] for part in chosen[0]) + over.shape[1]
+    anywhere = pl.BlockSpec(memory_space=pl.ANY)
+    width = 2 * block_rows * BLOCK
+    more = [] if before is None else list(before)
+
+    def dest(i, at):
+        return (at[0] // 2) ^ (first_pair + i)
+
+    return pl.pallas_call(
+        functools.partial(expand_terms_kernel, [len(parts) for parts in chosen], block_rows, blocks, first_pair),
+        grid_spec=pltpu.PrefetchScalarGridSpec(
+            num_scalar_prefetch=2,
+            grid=(pairs,),
+            in_specs=[pl.BlockSpec((rows, depth), lambda i, at, table: (0, 0))]
+            + [anywhere] * (1 + len(flat) + len(more)),
+            out_specs=(
+                pl.BlockSpec((rows, width), lambda i, at, table: (0, dest(i, at))),
+                pl.BlockSpec((1, depth, width), lambda i, at, table: (dest(i, at), 0, 0)),
+            ),
+            scratch_shapes=[
+                pltpu.VMEM((2, 2, size, BLOCK, BLOCK), BF16),
+                pltpu.SemaphoreType.DMA((2, 2, 3)),
+            ],
+        ),
+        out_shape=(
+            jax.ShapeDtypeStruct((rows, count // 2 * width), BF16),
+            jax.ShapeDtypeStruct((count // 2, depth, width), BF16),
+        ),
+        input_output_aliases={4 + len(flat): 0, 5 + len(flat): 1} if more else {},
+        compiler_params=params(),
+        cost_estimate=cost(),
+    )(at, table, normed, over, *flat, *more)
+
+
+def terms_kernel(normed_ref, dense_ref, out_ref):
+    out_ref[...] = jnp.dot(normed_ref[...], dense_ref[0], preferred_element_type=F32).astype(BF16)
+
+
+def terms(normed, dense):
     rows, depth = normed.shape
     shards, _, width = dense.shape
     return pl.pallas_call(
         terms_kernel,
-        grid_spec=pltpu.PrefetchScalarGridSpec(
-            num_scalar_prefetch=1,
-            grid=(count,),
-            in_specs=[
-                pl.BlockSpec((rows, depth), lambda i, at: (0, 0)),
-                pl.BlockSpec((1, depth, width), lambda i, at: (lax.rem(at[1] + 2 * shards - first - i, shards), 0, 0)),
-            ],
-            out_specs=pl.BlockSpec((1, rows, width), lambda i, at: (i, 0, 0)),
-        ),
-        out_shape=jax.ShapeDtypeStruct((count, rows, width), BF16),
+        grid=(shards,),
+        in_specs=[
+            pl.BlockSpec((rows, depth), lambda i: (0, 0)),
+            pl.BlockSpec((1, depth, width), lambda i: (i, 0, 0)),
+        ],
+        out_specs=pl.BlockSpec((rows, width), lambda i: (0, i)),
+        out_shape=jax.ShapeDtypeStruct((rows, shards * width), BF16),
         compiler_params=params(),
         cost_estimate=cost(),
-    )(at, normed, dense)
+    )(normed, dense)
 
 
 def add(got, term):
     return (got.astype(F32) + term.astype(F32)).astype(BF16)
 
 
-def place_kernel(slots_ref, got_ref, term_ref, *rest):
+def place_kernel(slots_ref, got_ref, *rest):
     out_ref = rest[-1]
-    total = got_ref[...].astype(F32) + term_ref[0].astype(F32)
+    total = got_ref[...].astype(F32)
     patch, frames = out_ref.shape[1:3]
     for token in range(patch):
         out_ref[0, token] = total[token * frames : (token + 1) * frames].astype(BF16)
 
 
-def place(slots, got, term, which, total_slots, before):
+def place(slots, got, total_slots, before):
     rows, width = got.shape
     count = slots.shape[0]
     patch = rows // count // FRAMES
@@ -634,18 +636,15 @@
         grid_spec=pltpu.PrefetchScalarGridSpec(
             num_scalar_prefetch=1,
             grid=(count,),
-            in_specs=[
-                pl.BlockSpec((rows // count, width), lambda i, slots: (i, 0)),
-                pl.BlockSpec((1, rows // count, width), lambda i, slots: (which, i, 0)),
-            ]
+            in_specs=[pl.BlockSpec((rows // count, width), lambda i, slots: (i, 0))]
             + ([] if before is None else [pl.BlockSpec(memory_space=pl.ANY)]),
             out_specs=pl.BlockSpec((1, patch, FRAMES, width), lambda i, slots: (slots[i], 0, 0, 0)),
         ),
         out_shape=jax.ShapeDtypeStruct((total_slots, patch, FRAMES, width), BF16),
-        input_output_aliases={} if before is None else {3: 0},
+        input_output_aliases={} if before is None else {2: 0},
         compiler_params=params(),
         cost_estimate=cost(),
-    )(slots, got, term, *(() if before is None else (before,)))
+    )(slots, got, *(() if before is None else (before,)))
 
 
 def swap(value, bit, size):
@@ -653,7 +652,7 @@
 
 
 def cube(own, size):
-    return {0: [own], 2: [swap(own, 2, size)], 4: [swap(own, 4, size)]}
+    return {0: [own], 2: [swap(own, 2, size)], 4: [swap(own, 4, size)], 1: [swap(own, 1, size)]}
 
 
 def cube_rest(got, size, near):
@@ -714,6 +713,8 @@
     flat_state = kept_state.reshape(slots, width, NSTATE)
     sends = [pick(order[k], flat_state) for k in range(len(steps))]
     out_packed = pack(at, after(out_mask, xz_packed), out_weight, 1, 0, out_room, True)
+    masks = after((xz_mask, out_mask), sends)
+    kept_xz, kept_out = (fullest(mask, streams, shards) for mask in masks)
     xz_table = slot_table(xz_mask, streams, shard, shards, side_blocks)
     out_table = slot_table(out_mask, streams, shard, shards, 0)
     head_of = jnp.arange(width) // HEADDIM
@@ -723,17 +724,15 @@
     per_head = lax.dynamic_update_slice(per_head, jnp.stack([dt_bias, decay_rate]), (0, shard * heads))
     rows = jnp.stack([jnp.repeat(skip_gain, HEADDIM), norm_gain] + [jnp.zeros_like(norm_gain)] * 6)
 
-    xz_panels[2], xz_panels[4] = after(
-        (xz_panels[2], xz_panels[4]), (sends, out_packed, xz_table, out_table, picked, per_head, rows, landing)
-    )
-    xz_panels = cube_rest(xz_panels, streams, (0, 2, 4, 6))
-
-    sends[0], out_packed = after((sends[0], out_packed), xz_panels[6])
+    (xz_panels[2], xz_panels[4], sends[0]) = after(
+        (xz_panels[2], xz_panels[4], sends[0]), (xz_panels[1], sends, out_packed, kept_xz, kept_out, xz_table, out_table, picked, per_head, rows, landing)
+    )
     got = [move(sends[0], 0)]
+    xz_panels = cube_rest(xz_panels, streams, (2, 4, 6))
+
+    out_packed = after(out_packed, (xz_panels[6], got))
     out_panels = cube(out_packed, streams)
-    masks = after((xz_mask, out_mask), (xz_panels[6], features))
-    kept_xz, kept_out = (fullest(mask, streams, shards) for mask in masks)
-    extra = (kept_xz > xz_room) | (kept_out > out_room)
+    extra = after((kept_xz > xz_room) | (kept_out > out_room), (xz_panels[6], features))
     spare_xz, spare_out = 2 * out_blocks - xz_room, out_blocks - out_room
 
     def none(*_):
@@ -746,43 +745,48 @@
 
     over_xz, over_out = lax.cond(extra, some, none, xz_panel, out_weight)
     at = jnp.concatenate([at, extra.astype(jnp.int32)[None]])
-    total = project(after(at, got[0]), xz_table, features, xz_panels, over_xz, block_rows)
-    out_panels[2], out_panels[4], total = lax.optimization_barrier((out_panels[2], out_panels[4], total))
-    out_panels = cube_rest(out_panels, streams, (0, 2, 4))
+    total = project(at, xz_table, features, xz_panels, over_xz, block_rows)
+    out_panels, total = lax.optimization_barrier((out_panels, total))
+    out_panels = cube_rest(out_panels, streams, (2, 4))
     sends[1:] = after(sends[1:], out_panels[6])
-    got += [move(sends[k], k) for k in range(1, len(steps))]
+    got.append(move(sends[1], 1))
+    got += [move(sends[k], k) for k in range(2, len(steps))]
 
     pairs = streams // 2
-    ring = [(i, (i + 1) % shards) for i in range(shards)]
     count = len(steps)
 
     def scan_chunk(k, total, carry):
         return scan(landing[k], total, got[k], rows, per_head, picked, carry, slots, DINNER // NORM_GROUPS)
 
-    dense = expand(at, out_table, out_panels, over_out, 0, pairs - 1, block_rows, None)
     done, carry = scan_chunk(0, total, None)
-    last = after(out_panels[2 * pairs - 2], (dense, done))
+    most = expand_terms(at, out_table, done, out_panels, over_out, 0, pairs - 1, block_rows, None)
+    last = after(out_panels[2 * pairs - 2], most)
     out_panels[2 * pairs - 2] = last
     out_panels[2 * pairs - 1] = [swap(part, 1, streams) for part in last]
-    dense = expand(at, out_table, out_panels, over_out, pairs - 1, 1, block_rows, dense)
-
-    mixed, moving, term = None, [], []
+    term, dense = expand_terms(at, out_table, done, out_panels, over_out, pairs - 1, 1, block_rows, most)
+
+    ring = [(i, (i + 1) % shards) for i in range(shards)]
+
+    def term_for(k, hop):
+        return lax.dynamic_slice_in_dim(terms_of[k], (shard - hop) % shards * width, width, 1)
+
+    mixed, moving, terms_of = None, [], [term]
     for step in range(count + shards - 1):
         if step < count:
             if step:
                 done, carry = scan_chunk(step, total, carry)
-            first = terms(at, done, dense, 1, 1)
-            moving.append(lax.ppermute(first[0], "shard", ring))
-            term.append(terms(at, after(done, first), dense, 2, shards - 1))
+                terms_of.append(terms(done, dense))
+            moving.append(lax.ppermute(term_for(step, 1), "shard", ring))
         passed = []
-        for k in range(max(step - shards, 0), min(step, count)):
+        for k in range(max(step - shards + 1, 0), min(step, count)):
             hop = step - k + 1
+            value = add(moving[k], term_for(k, hop))
+            passed.append(value)
             if hop < shards:
-                passed.append(add(moving[k], term[k][hop - 2]))
-                moving[k] = lax.ppermute(passed[-1], "shard", ring)
-            elif hop == shards:
-                mixed = place(landing[k], moving[k], term[k], shards - 2, slots, mixed)
-        total = after(total, (term[-1], passed))
+                moving[k] = lax.ppermute(value, "shard", ring)
+            else:
+                mixed = place(landing[k], value, slots, mixed)
+        total = after(total, (terms_of[-1], passed))
     return mixed.transpose(0, 2, 1, 3), carry.reshape(kept_state.shape)
 
 

time: 343 us -> 336 us (0.980)
  Pallas kernels: 125 us -> 114 us
    pallas_call x10 -> x5, Pallas kernels: 46.8 us -> 34.1 us  [the longest x3 19.5 us: terms(): pl.pallas_call(terms_kernel, grid=(shards,), in_specs=[pl.BlockSpec((rows...]
    unnamed x49 -> x63, local copies, waits for them, and re-layouts: 11.2 us -> 15.5 us
  transfers between devices with their start and end apart: 39 -> 39, of which waited for: 14 -> 14; matrix products, arithmetic and copies ran while one was open for 6% -> 5% of each run, Pallas kernels for 36% -> 33%
where the time goes in v3:
time: 336 us; the launch traced here: 335 us
  waiting for transfers between devices  143 us (43%)
  Pallas kernels  114 us (34%)
  starting transfers between devices  30.3 us (9%)
  local copies, waits for them, and re-layouts  25.8 us (8%)
  between operations  16 us (5%)
  other arithmetic  5.95 us (2%)
    ppermute x8, waiting for transfers between devices, move(): lax.ppermute(values, 'stream', [(i, (i + steps[k]) % streams) for i in ra...  62 us
    ppermute x18, waiting for transfers between devices, swap(): return lax.ppermute(value, 'stream', [(i, i ^ bit) for i in range(size)])  31.7 us
    pallas_call x1, Pallas kernels, project(): pl.pallas_call(functools.partial(project_kernel, [len(panels[b]) for b in...  26.6 us
    ppermute x4, waiting for transfers between devices, sparse(): moving.append(lax.ppermute(term_for(step, 1), 'shard', ring))  26.5 us
    pallas_call x4, Pallas kernels, scan(): pl.pallas_call(functools.partial(scan_kernel, width // HEADDIM, group_wid...  24.5 us
    ppermute x8, waiting for transfers between devices, sparse(): moving[k] = lax.ppermute(value, 'shard', ring)  22.8 us
    pallas_call x3, Pallas kernels, terms(): pl.pallas_call(terms_kernel, grid=(shards,), in_specs=[pl.BlockSpec((rows...  19.5 us
    unnamed x63, local copies, waits for them, and re-layouts  15.5 us
  transfers between devices with their start and end apart: 39, of which 14 were waited for; matrix products, arithmetic and copies ran while one was open for 5% of the time, Pallas kernels for 33%

profile of v3, /device:TPU:0, one launch (start us, length us, event | category | flops | bytes accessed | tf_op | source)
XLA Modules:
  0.0 335.3 jit_solution(9253873479035022300)
XLA Ops:
  10.9 4.2 %copy.29 = bf16[80,8,2,1280]{3,1,2,0:T(8,128)(2,1)} copy(bf16[80,8,2,1280]{3,2,1,0:T(2,128)(2,1)} %bitcast.27) | data formatting | bytes 6553600
  15.3 4.7 %shard_map.140.refs_0_ = bf16[82,128,128]{2,1,0:T(8,128)(2,1)} custom-call(s32[2]{0:T(128)S(1)} %pad_add_fusion.1.at_ref, s32[3200]{0:T(1024)S(1)} %reshape.133.mask_ref, bf16[640,2560]{1,0:T(8,128)(2,1)} %bitcast.24, bf16[336,640]{1,0:T(8,128)(2,1)S(1)} %bitcast.16), custom_call_target="tpu_custom_call" | custom-call | flops 1 | bytes 1 | tf_op jit(solution)/shard_map/pallas_call | solution.py:210
  33.5 3.8 %shard_map.143 = bf16[3,1280,128]{2,1,0:T(8,128)(2,1)} custom-call(s32[3]{0:T(128)S(1)} %get-tuple-element.108.order_ref, f32[12,1280,128]{2,1,0:T(8,128)} %bitcast.19), custom_call_target="tpu_custom_call" | custom-call | flops 1 | bytes 1 | tf_op jit(solution)/shard_map/pallas_call | solution.py:384
  40.3 3.8 %shard_map.141.refs_0_ = bf16[37,128,128]{2,1,0:T(8,128)(2,1)S(1)} custom-call(s32[2]{0:T(128)S(1)} %pad_add_fusion.1.at_ref, s32[1600]{0:T(1024)S(1)} %reshape.136.mask_ref, bf16[640,1280]{1,0:T(8,128)(2,1)} %x_ref.1), custom_call_target="tpu_custom_call" | custom-call | flops 1 | bytes 1 | tf_op jit(solution)/shard_map/pallas_call | solution.py:210
  49.3 34.4 %collective-permute-done.slots_ref = s32[3]{0:T(128)S(1)} collective-permute-done((s32[3]{0:T(128)S(1)}, s32[3]{0:T(128)S(1)}, u32[]{:S(2)}, u32[]{:S(2)}) %collective-permute-start) | collective-permute-done | bytes 44 | tf_op jit(solution)/shard_map/ppermute | solution.py:709
  93.7 27.6 %collective-permute-done.7.refs_6_ = bf16[41,128,128]{2,1,0:T(8,128)(2,1)S(1)} collective-permute-done((bf16[41,128,128]{2,1,0:T(8,128)(2,1)S(1)}, bf16[41,128,128]{2,1,0:T(8,128)(2,1)S(1)}, u32[]{:S(2)}, u32[]{:S(2)}) %collective-permute-start.7) | collective-permute-done | bytes 1343520 | tf_op jit(solution)/shard_map/ppermute | solution.py:651
  123.8 13.9 %collective-permute-done.9.state_ref = bf16[3,1280,128]{2,1,0:T(8,128)(2,1)S(1)} collective-permute-done((bf16[3,1280,128]{2,1,0:T(8,128)(2,1)S(1)}, bf16[3,1280,128]{2,1,0:T(8,128)(2,1)S(1)}, u32[]{:S(2)}, u32[]{:S(2)}) %collective-permute-start.9) | collective-permute-done | bytes 983072 | tf_op jit(solution)/shard_map/ppermute | solution.py:709
  142.9 26.6 %shard_map.146.total_ref = f32[576,2944]{1,0:T(8,128)} custom-call(s32[3]{0:T(128)} %pad_add_fusion.2.at_ref, s32[920]{0:T(1024)} %reshape.139.table_ref, bf16[576,5120]{1,0:T(8,128)(2,1)} %all-gather.10.cloned.1.call-done.x_ref, bf16[8,34,128,128]{3,2,1,0:T(8,128)(2,1)} %get-tuple-element.66.over_ref, bf16[82,128,128]{2,1,0:T(8,128)(2,1)} %shard_map.140.refs_0_, ...), custom_call_target="tpu_custom_call" | custom-call | flops 1 | bytes 1 | tf_op jit(solution)/shard_map/pallas_call | solution.py:358
  173.6 6.3 %shard_map.147 = (bf16[144,1280]{1,0:T(8,128)(2,1)S(1)}, f32[12,1280,128]{2,1,0:T(8,128)}) custom-call(s32[3]{0:T(128)S(1)} %collective-permute-done.4.slots_ref, f32[576,2944]{1,0:T(8,128)} %shard_map.146.total_ref, bf16[3,1280,128]{2,1,0:T(8,128)(2,1)S(1)} %copy-done.11, f32[8,1280]{1,0:T(8,128)S(1)} %maximum_maximum_fusion.rows_ref, ...), custom_call_target="tpu_custom_call" | custom-call | flops 1 | bytes 1 | tf_op jit(solution)/shard_map/pallas_call | solution.py:482
  181.0 9.6 %shard_map.148 = (bf16[144,5120]{1,0:T(8,128)(2,1)}, bf16[4,1280,1280]{2,1,0:T(8,128)(2,1)}) custom-call(s32[3]{0:T(128)S(1)} %copy-done.17, s32[400]{0:T(512)S(1)} %reshape_reshape.8.table_ref, bf16[144,1280]{1,0:T(8,128)(2,1)S(1)} %get-tuple-element.68.normed_ref, bf16[8,14,128,128]{3,2,1,0:T(8,128)(2,1)S(1)} %copy-done.18, ...), custom_call_target="tpu_custom_call" | custom-call | flops 1 | bytes 1 | tf_op jit(solution)/shard_map/pallas_call | solution.py:571
  200.0 5.0 %shard_map.149 = (bf16[144,5120]{1,0:T(8,128)(2,1)S(1)}, bf16[4,1280,1280]{2,1,0:T(8,128)(2,1)}) custom-call(s32[3]{0:T(128)S(1)} %copy-done.17, s32[400]{0:T(512)S(1)} %reshape_reshape.8.table_ref, bf16[144,1280]{1,0:T(8,128)(2,1)S(1)} %copy-done.5, ...), custom_call_target="tpu_custom_call", output_to_operand_aliasing={{0}: (8, {}), {1}: (9, {})} | custom-call | flops 1 | bytes 1 | tf_op jit(solution)/shard_map/pallas_call | solution.py:571
  210.0 6.2 %collective-permute-done.23.state_ref = bf16[3,1280,128]{2,1,0:T(8,128)(2,1)} collective-permute-done((bf16[3,1280,128]{2,1,0:T(8,128)(2,1)}, bf16[3,1280,128]{2,1,0:T(8,128)(2,1)}, u32[]{:S(2)}, u32[]{:S(2)}) %collective-permute-start.23) | collective-permute-done | bytes 983072 | tf_op jit(solution)/shard_map/ppermute | solution.py:709
  216.2 6.2 %shard_map.150 = (bf16[144,1280]{1,0:T(8,128)(2,1)S(1)}, f32[12,1280,128]{2,1,0:T(8,128)}) custom-call(s32[3]{0:T(128)S(1)} %collective-permute-done.5.slots_ref, f32[576,2944]{1,0:T(8,128)} %shard_map.146.total_ref, bf16[3,1280,128]{2,1,0:T(8,128)(2,1)} %collective-permute-done.23.state_ref, ...), custom_call_target="tpu_custom_call", output_to_operand_aliasing={{1}: (6, {})} | custom-call | flops 1 | bytes 1 | tf_op jit(solution)/shard_map/pallas_call | solution.py:482
  222.4 6.6 %shard_map.151 = bf16[144,5120]{1,0:T(8,128)(2,1)S(1)} custom-call(bf16[144,1280]{1,0:T(8,128)(2,1)S(1)} %get-tuple-element.82.normed_ref, bf16[4,1280,1280]{2,1,0:T(8,128)(2,1)} %get-tuple-element.83.dense_ref), custom_call_target="tpu_custom_call" | custom-call | flops 1 | bytes 1 | tf_op jit(solution)/shard_map/pallas_call | solution.py:604
  233.3 9.0 %collective-permute-done.27 = bf16[144,1280]{1,0:T(8,128)(2,1)S(1)} collective-permute-done((bf16[144,1280]{1,0:T(8,128)(2,1)S(1)}, bf16[144,1280]{1,0:T(8,128)(2,1)S(1)}, u32[]{:S(2)}, u32[]{:S(2)}) %collective-permute-start.27) | collective-permute-done | bytes 368672 | tf_op jit(solution)/shard_map/ppermute | solution.py:779
  242.7 4.8 %collective-permute-done.25.state_ref = bf16[3,1280,128]{2,1,0:T(8,128)(2,1)S(1)} collective-permute-done((bf16[3,1280,128]{2,1,0:T(8,128)(2,1)S(1)}, bf16[3,1280,128]{2,1,0:T(8,128)(2,1)S(1)}, u32[]{:S(2)}, u32[]{:S(2)}) %collective-permute-start.25) | collective-permute-done | bytes 983072 | tf_op jit(solution)/shard_map/ppermute | solution.py:709
  247.5 6.0 %shard_map.152 = (bf16[144,1280]{1,0:T(8,128)(2,1)S(1)}, f32[12,1280,128]{2,1,0:T(8,128)}) custom-call(s32[3]{0:T(128)S(1)} %collective-permute-done.6.slots_ref, f32[576,2944]{1,0:T(8,128)} %shard_map.146.total_ref, bf16[3,1280,128]{2,1,0:T(8,128)(2,1)S(1)} %collective-permute-done.25.state_ref, ...), custom_call_target="tpu_custom_call", output_to_operand_aliasing={{1}: (6, {})} | custom-call | flops 1 | bytes 1 | tf_op jit(solution)/shard_map/pallas_call | solution.py:482
  253.5 6.5 %shard_map.153 = bf16[144,5120]{1,0:T(8,128)(2,1)S(1)} custom-call(bf16[144,1280]{1,0:T(8,128)(2,1)S(1)} %get-tuple-element.87.normed_ref, bf16[4,1280,1280]{2,1,0:T(8,128)(2,1)} %get-tuple-element.83.dense_ref), custom_call_target="tpu_custom_call" | custom-call | flops 1 | bytes 1 | tf_op jit(solution)/shard_map/pallas_call | solution.py:604
  265.1 6.0 %shard_map.154 = (bf16[144,1280]{1,0:T(8,128)(2,1)S(1)}, f32[12,1280,128]{2,1,0:T(8,128)}) custom-call(s32[3]{0:T(128)S(1)} %collective-permute-done.slots_ref, f32[576,2944]{1,0:T(8,128)} %shard_map.146.total_ref, bf16[3,1280,128]{2,1,0:T(8,128)(2,1)S(1)} %collective-permute-done.28.state_ref, ...), custom_call_target="tpu_custom_call", output_to_operand_aliasing={{1}: (6, {})} | custom-call | flops 1 | bytes 1 | tf_op jit(solution)/shard_map/pallas_call | solution.py:482
  271.1 6.5 %shard_map.155 = bf16[144,5120]{1,0:T(8,128)(2,1)S(1)} custom-call(bf16[144,1280]{1,0:T(8,128)(2,1)S(1)} %get-tuple-element.91.normed_ref, bf16[4,1280,1280]{2,1,0:T(8,128)(2,1)} %get-tuple-element.83.dense_ref), custom_call_target="tpu_custom_call" | custom-call | flops 1 | bytes 1 | tf_op jit(solution)/shard_map/pallas_call | solution.py:604
  279.7 17.4 %collective-permute-done.29 = bf16[144,1280]{1,0:T(8,128)(2,1)S(1)} collective-permute-done((bf16[144,1280]{1,0:T(8,128)(2,1)S(1)}, bf16[144,1280]{1,0:T(8,128)(2,1)S(1)}, u32[]{:S(2)}, u32[]{:S(2)}) %collective-permute-start.29) | collective-permute-done | bytes 368672 | tf_op jit(solution)/shard_map/ppermute | solution.py:779
  299.4 5.6 %collective-permute-done.33 = bf16[144,1280]{1,0:T(8,128)(2,1)S(1)} collective-permute-done((bf16[144,1280]{1,0:T(8,128)(2,1)S(1)}, bf16[144,1280]{1,0:T(8,128)(2,1)S(1)}, u32[]{:S(2)}, u32[]{:S(2)}) %collective-permute-start.33) | collective-permute-done | bytes 368672 | tf_op jit(solution)/shard_map/ppermute | solution.py:786
  307.1 5.8 %collective-permute-done.30 = bf16[144,1280]{1,0:T(8,128)(2,1)S(1)} collective-permute-done((bf16[144,1280]{1,0:T(8,128)(2,1)S(1)}, bf16[144,1280]{1,0:T(8,128)(2,1)S(1)}, u32[]{:S(2)}, u32[]{:S(2)}) %collective-permute-start.30) | collective-permute-done | bytes 368672 | tf_op jit(solution)/shard_map/ppermute | solution.py:786
  313.1 7.7 %collective-permute-done.34 = bf16[144,1280]{1,0:T(8,128)(2,1)S(1)} collective-permute-done((bf16[144,1280]{1,0:T(8,128)(2,1)S(1)}, bf16[144,1280]{1,0:T(8,128)(2,1)S(1)}, u32[]{:S(2)}, u32[]{:S(2)}) %collective-permute-start.34) | collective-permute-done | bytes 368672 | tf_op jit(solution)/shard_map/ppermute | solution.py:786
  (210 shorter events, 85.0 us)
Async XLA Ops:
  7.2 134.9 %all-gather.10.cloned.1.call-start = ((), (), s32[]{:S(2)}) async-start(), calls=%async_computation.2 | async-start | bytes 7372800 | tf_op jit(solution)/shard_map/all_gather | solution.py:694
  20.0 68.1 %collective-permute-start.3 = (bf16[82,128,128]{2,1,0:T(8,128)(2,1)}, bf16[82,128,128]{2,1,0:T(8,128)(2,1)}, u32[]{:S(2)}, u32[]{:S(2)}) collective-permute-start(bf16[82,128,128]{2,1,0:T(8,128)(2,1)} %shard_map.140.refs_0_), channel_id=1, source_target_pairs={{0,4},{4,0},{8,12},{12,8},{16,20},{20,16},{24,28},{28,24},{1,5},{5... | collective-permute-start | bytes 8060936 | tf_op jit(solution)/shard_map/ppermute | solution.py:651
  20.5 67.7 %collective-permute-start.1 = (bf16[82,128,128]{2,1,0:T(8,128)(2,1)}, bf16[82,128,128]{2,1,0:T(8,128)(2,1)}, u32[]{:S(2)}, u32[]{:S(2)}) collective-permute-start(bf16[82,128,128]{2,1,0:T(8,128)(2,1)} %shard_map.140.refs_0_), channel_id=1, source_target_pairs={{0,8},{4,12},{8,0},{12,4},{16,24},{20,28},{24,16},{28,20},{1,9},{5... | collective-permute-start | bytes 8060936 | tf_op jit(solution)/shard_map/ppermute | solution.py:651
  23.0 65.2 %collective-permute-start.2 = (bf16[82,128,128]{2,1,0:T(8,128)(2,1)}, bf16[82,128,128]{2,1,0:T(8,128)(2,1)}, u32[]{:S(2)}, u32[]{:S(2)}) collective-permute-start(bf16[82,128,128]{2,1,0:T(8,128)(2,1)} %shard_map.140.refs_0_), channel_id=1, source_target_pairs={{0,16},{4,20},{8,24},{12,28},{16,0},{20,4},{24,8},{28,12},{1,17},{... | collective-permute-start | bytes 8060936 | tf_op jit(solution)/shard_map/ppermute | solution.py:651
  25.3 58.4 %collective-permute-start = (s32[3]{0:T(128)S(1)}, s32[3]{0:T(128)S(1)}, u32[]{:S(2)}, u32[]{:S(2)}) collective-permute-start(s32[3]{0:T(128)S(1)} %get-tuple-element.98), channel_id=1, source_target_pairs={{0,16},{4,20},{8,24},{12,28},{16,0},{20,4},{24,8},{28,12},{1,17},{... | collective-permute-start | bytes 44 | tf_op jit(solution)/shard_map/ppermute | solution.py:709
  25.9 58.2 %collective-permute-start.4 = (s32[3]{0:T(128)S(1)}, s32[3]{0:T(128)S(1)}, u32[]{:S(2)}, u32[]{:S(2)}) collective-permute-start(s32[3]{0:T(128)S(1)} %get-tuple-element.97), channel_id=1, source_target_pairs={{0,4},{4,8},{8,12},{12,16},{16,20},{20,24},{24,28},{28,0},{1,5},{5... | collective-permute-start | bytes 44 | tf_op jit(solution)/shard_map/ppermute | solution.py:709
  89.6 31.7 %collective-permute-start.7 = (bf16[41,128,128]{2,1,0:T(8,128)(2,1)S(1)}, bf16[41,128,128]{2,1,0:T(8,128)(2,1)S(1)}, u32[]{:S(2)}, u32[]{:S(2)}) collective-permute-start(bf16[41,128,128]{2,1,0:T(8,128)(2,1)S(1)} %slice.44), channel_id=1, source_target_pairs={{0,8},{4,12},{8,0},{12,4},{16,24},{20,28},{24,16},{28,20},{1,9},{5... | collective-permute-start | bytes 4030472 | tf_op jit(solution)/shard_map/ppermute | solution.py:651
  92.6 30.7 %collective-permute-start.8 = (bf16[41,128,128]{2,1,0:T(8,128)(2,1)S(1)}, bf16[41,128,128]{2,1,0:T(8,128)(2,1)S(1)}, u32[]{:S(2)}, u32[]{:S(2)}) collective-permute-start(bf16[41,128,128]{2,1,0:T(8,128)(2,1)S(1)} %slice.45), channel_id=1, source_target_pairs={{0,16},{4,20},{8,24},{12,28},{16,0},{20,4},{24,8},{28,12},{1,17},{... | collective-permute-start | bytes 4030472 | tf_op jit(solution)/shard_map/ppermute | solution.py:651
  93.1 49.7 %collective-permute-start.13 = (bf16[82,128,128]{2,1,0:T(8,128)(2,1)}, bf16[82,128,128]{2,1,0:T(8,128)(2,1)}, u32[]{:S(2)}, u32[]{:S(2)}) collective-permute-start(bf16[82,128,128]{2,1,0:T(8,128)(2,1)} %collective-permute-done.1.refs_2_), channel_id=1, source_target_pairs={{0,4},{4,0},{8,12},{12,8},{16,20},{20,16},{24,28},{28,24},{1,5},{5... | collective-permute-start | bytes 8060936 | tf_op jit(solution)/shard_map/ppermute | solution.py:651
  93.2 49.7 %collective-permute-start.14 = (bf16[82,128,128]{2,1,0:T(8,128)(2,1)}, bf16[82,128,128]{2,1,0:T(8,128)(2,1)}, u32[]{:S(2)}, u32[]{:S(2)}) collective-permute-start(bf16[82,128,128]{2,1,0:T(8,128)(2,1)} %collective-permute-done.2.refs_4_), channel_id=1, source_target_pairs={{0,4},{4,0},{8,12},{12,8},{16,20},{20,16},{24,28},{28,24},{1,5},{5... | collective-permute-start | bytes 8060936 | tf_op jit(solution)/shard_map/ppermute | solution.py:651
  138.7 30.8 %collective-permute-start.10 = (bf16[37,128,128]{2,1,0:T(8,128)(2,1)S(1)}, bf16[37,128,128]{2,1,0:T(8,128)(2,1)}, u32[]{:S(2)}, u32[]{:S(2)}) collective-permute-start(bf16[37,128,128]{2,1,0:T(8,128)(2,1)S(1)} %shard_map.141.refs_0_), channel_id=1, source_target_pairs={{0,4},{4,0},{8,12},{12,8},{16,20},{20,16},{24,28},{28,24},{1,5},{5... | collective-permute-start | bytes 3637256 | tf_op jit(solution)/shard_map/ppermute | solution.py:651
  138.7 30.8 %collective-permute-start.11 = (bf16[37,128,128]{2,1,0:T(8,128)(2,1)S(1)}, bf16[37,128,128]{2,1,0:T(8,128)(2,1)S(1)}, u32[]{:S(2)}, u32[]{:S(2)}) collective-permute-start(bf16[37,128,128]{2,1,0:T(8,128)(2,1)S(1)} %shard_map.141.refs_0_), channel_id=1, source_target_pairs={{0,8},{4,12},{8,0},{12,4},{16,24},{20,28},{24,16},{28,20},{1,9},{5... | collective-permute-start | bytes 3637256 | tf_op jit(solution)/shard_map/ppermute | solution.py:651
  139.1 30.4 %collective-permute-start.12 = (bf16[37,128,128]{2,1,0:T(8,128)(2,1)S(1)}, bf16[37,128,128]{2,1,0:T(8,128)(2,1)}, u32[]{:S(2)}, u32[]{:S(2)}) collective-permute-start(bf16[37,128,128]{2,1,0:T(8,128)(2,1)S(1)} %shard_map.141.refs_0_), channel_id=1, source_target_pairs={{0,16},{4,20},{8,24},{12,28},{16,0},{20,4},{24,8},{28,12},{1,17},{... | collective-permute-start | bytes 3637256 | tf_op jit(solution)/shard_map/ppermute | solution.py:651
  170.2 20.5 %collective-permute-start.18 = (bf16[19,128,128]{2,1,0:T(8,128)(2,1)S(1)}, bf16[19,128,128]{2,1,0:T(8,128)(2,1)}, u32[]{:S(2)}, u32[]{:S(2)}) collective-permute-start(bf16[19,128,128]{2,1,0:T(8,128)(2,1)S(1)} %slice.47), channel_id=1, source_target_pairs={{0,16},{4,20},{8,24},{12,28},{16,0},{20,4},{24,8},{28,12},{1,17},{... | collective-permute-start | bytes 1867784 | tf_op jit(solution)/shard_map/ppermute | solution.py:651
  190.7 25.5 %collective-permute-start.23 = (bf16[3,1280,128]{2,1,0:T(8,128)(2,1)}, bf16[3,1280,128]{2,1,0:T(8,128)(2,1)}, u32[]{:S(2)}, u32[]{:S(2)}) collective-permute-start(bf16[3,1280,128]{2,1,0:T(8,128)(2,1)} %shard_map.143), channel_id=1, source_target_pairs={{0,8},{4,12},{8,16},{12,20},{16,24},{20,28},{24,0},{28,4},{1,9},{5... | collective-permute-start | bytes 2949128 | tf_op jit(solution)/shard_map/ppermute | solution.py:709
  206.2 24.5 %collective-permute-start.24 = (bf16[144,1280]{1,0:T(8,128)(2,1)S(1)}, bf16[144,1280]{1,0:T(8,128)(2,1)}, u32[]{:S(2)}, u32[]{:S(2)}) collective-permute-start(bf16[144,1280]{1,0:T(8,128)(2,1)S(1)} %constant_dynamic-slice_fusion.3), channel_id=1, source_target_pairs={{0,1},{1,2},{2,3},{3,0},{4,5},{5,6},{6,7},{7,4},{8,9},{9,10},{10,1... | collective-permute-start | bytes 1105928 | tf_op jit(solution)/shard_map/ppermute | solution.py:779
  207.8 39.7 %collective-permute-start.25 = (bf16[3,1280,128]{2,1,0:T(8,128)(2,1)S(1)}, bf16[3,1280,128]{2,1,0:T(8,128)(2,1)S(1)}, u32[]{:S(2)}, u32[]{:S(2)}) collective-permute-start(bf16[3,1280,128]{2,1,0:T(8,128)(2,1)S(1)} %copy-done.9), channel_id=1, source_target_pairs={{0,12},{4,16},{8,20},{12,24},{16,28},{20,0},{24,4},{28,8},{1,13},{... | collective-permute-start | bytes 2949128 | tf_op jit(solution)/shard_map/ppermute | solution.py:709
  208.9 56.2 %collective-permute-start.28 = (bf16[3,1280,128]{2,1,0:T(8,128)(2,1)S(1)}, bf16[3,1280,128]{2,1,0:T(8,128)(2,1)S(1)}, u32[]{:S(2)}, u32[]{:S(2)}) collective-permute-start(bf16[3,1280,128]{2,1,0:T(8,128)(2,1)S(1)} %copy-done.7), channel_id=1, source_target_pairs={{0,16},{4,20},{8,24},{12,28},{16,0},{20,4},{24,8},{28,12},{1,17},{... | collective-permute-start | bytes 2949128 | tf_op jit(solution)/shard_map/ppermute | solution.py:709
  231.7 29.9 %collective-permute-start.26 = (bf16[144,1280]{1,0:T(8,128)(2,1)S(1)}, bf16[144,1280]{1,0:T(8,128)(2,1)S(1)}, u32[]{:S(2)}, u32[]{:S(2)}) collective-permute-start(bf16[144,1280]{1,0:T(8,128)(2,1)S(1)} %add_convert_fusion.12), channel_id=1, source_target_pairs={{0,1},{1,2},{2,3},{3,0},{4,5},{5,6},{6,7},{7,4},{8,9},{9,10},{10,1... | collective-permute-start | bytes 1105928 | tf_op jit(solution)/shard_map/ppermute | solution.py:786
  242.4 20.9 %collective-permute-start.35 = (bf16[144,1280]{1,0:T(8,128)(2,1)S(1)}, bf16[144,1280]{1,0:T(8,128)(2,1)S(1)}, u32[]{:S(2)}, u32[]{:S(2)}) collective-permute-start(bf16[144,1280]{1,0:T(8,128)(2,1)S(1)} %add_convert_fusion.10), channel_id=1, source_target_pairs={{0,1},{1,2},{2,3},{3,0},{4,5},{5,6},{6,7},{7,4},{8,9},{9,10},{10,1... | collective-permute-start | bytes 1105928 | tf_op jit(solution)/shard_map/ppermute | solution.py:786
  261.8 35.4 %collective-permute-start.37 = (bf16[144,1280]{1,0:T(8,128)(2,1)S(1)}, bf16[144,1280]{1,0:T(8,128)(2,1)S(1)}, u32[]{:S(2)}, u32[]{:S(2)}) collective-permute-start(bf16[144,1280]{1,0:T(8,128)(2,1)S(1)} %add_convert_fusion.11), channel_id=1, source_target_pairs={{0,1},{1,2},{2,3},{3,0},{4,5},{5,6},{6,7},{7,4},{8,9},{9,10},{10,1... | collective-permute-start | bytes 1105928 | tf_op jit(solution)/shard_map/ppermute | solution.py:786
  263.5 35.8 %collective-permute-start.36 = (bf16[144,1280]{1,0:T(8,128)(2,1)S(1)}, bf16[144,1280]{1,0:T(8,128)(2,1)S(1)}, u32[]{:S(2)}, u32[]{:S(2)}) collective-permute-start(bf16[144,1280]{1,0:T(8,128)(2,1)S(1)} %add_convert_fusion.3), channel_id=1, source_target_pairs={{0,1},{1,2},{2,3},{3,0},{4,5},{5,6},{6,7},{7,4},{8,9},{9,10},{10,1... | collective-permute-start | bytes 1105928 | tf_op jit(solution)/shard_map/ppermute | solution.py:786
  277.7 19.4 %collective-permute-start.29 = (bf16[144,1280]{1,0:T(8,128)(2,1)S(1)}, bf16[144,1280]{1,0:T(8,128)(2,1)S(1)}, u32[]{:S(2)}, u32[]{:S(2)}) collective-permute-start(bf16[144,1280]{1,0:T(8,128)(2,1)S(1)} %constant_dynamic-slice_fusion.1), channel_id=1, source_target_pairs={{0,1},{1,2},{2,3},{3,0},{4,5},{5,6},{6,7},{7,4},{8,9},{9,10},{10,1... | collective-permute-start | bytes 1105928 | tf_op jit(solution)/shard_map/ppermute | solution.py:779
  278.0 27.0 %collective-permute-start.33 = (bf16[144,1280]{1,0:T(8,128)(2,1)S(1)}, bf16[144,1280]{1,0:T(8,128)(2,1)S(1)}, u32[]{:S(2)}, u32[]{:S(2)}) collective-permute-start(bf16[144,1280]{1,0:T(8,128)(2,1)S(1)} %add_convert_fusion.6), channel_id=1, source_target_pairs={{0,1},{1,2},{2,3},{3,0},{4,5},{5,6},{6,7},{7,4},{8,9},{9,10},{10,1... | collective-permute-start | bytes 1105928 | tf_op jit(solution)/shard_map/ppermute | solution.py:786
  (46 other events, 344.7 us)
Sparse Core Ops, SparseCore 0:
  10.9 111.5 all-gather.9

commit v4 on v3

--- a/solution.py
+++ b/solution.py
@@ -730,9 +730,9 @@
     got = [move(sends[0], 0)]
     xz_panels = cube_rest(xz_panels, streams, (2, 4, 6))
 
-    out_packed = after(out_packed, (xz_panels[6], got))
+    out_packed = after(out_packed, xz_panels[6])
     out_panels = cube(out_packed, streams)
-    extra = after((kept_xz > xz_room) | (kept_out > out_room), (xz_panels[6], features))
+    extra = after((kept_xz > xz_room) | (kept_out > out_room), (xz_panels[6], features, got))
     spare_xz, spare_out = 2 * out_blocks - xz_room, out_blocks - out_room
 
     def none(*_):

time: 336 us -> 337 us (level)
  no operation moved by 1% of the time
where the time goes in v4:
time: 337 us; the launch traced here: 336 us
  waiting for transfers between devices  143 us (42%)
  Pallas kernels  114 us (34%)
  starting transfers between devices  29.7 us (9%)
  local copies, waits for them, and re-layouts  26.7 us (8%)
  between operations  16 us (5%)
  other arithmetic  5.95 us (2%)
    ppermute x8, waiting for transfers between devices, move(): lax.ppermute(values, 'stream', [(i, (i + steps[k]) % streams) for i in ra...  61.8 us
    ppermute x18, waiting for transfers between devices, swap(): return lax.ppermute(value, 'stream', [(i, i ^ bit) for i in range(size)])  32.2 us
    pallas_call x1, Pallas kernels, project(): pl.pallas_call(functools.partial(project_kernel, [len(panels[b]) for b in...  26.6 us
    ppermute x4, waiting for transfers between devices, sparse(): moving.append(lax.ppermute(term_for(step, 1), 'shard', ring))  26.5 us
    pallas_call x4, Pallas kernels, scan(): pl.pallas_call(functools.partial(scan_kernel, width // HEADDIM, group_wid...  24.5 us
    ppermute x8, waiting for transfers between devices, sparse(): moving[k] = lax.ppermute(value, 'shard', ring)  22.8 us
    pallas_call x3, Pallas kernels, terms(): pl.pallas_call(terms_kernel, grid=(shards,), in_specs=[pl.BlockSpec((rows...  19.5 us
    unnamed x63, local copies, waits for them, and re-layouts  16.5 us
  transfers between devices with their start and end apart: 39, of which 14 were waited for; matrix products, arithmetic and copies ran while one was open for 5% of the time, Pallas kernels for 33%

profile of v4, /device:TPU:0, one launch (start us, length us, event | category | flops | bytes accessed | tf_op | source)
XLA Modules:
  0.0 336.1 jit_solution(12054461307299317362)
XLA Ops:
  10.9 4.2 %copy.29 = bf16[80,8,2,1280]{3,1,2,0:T(8,128)(2,1)} copy(bf16[80,8,2,1280]{3,2,1,0:T(2,128)(2,1)} %bitcast.27) | data formatting | bytes 6553600
  15.3 4.7 %shard_map.140.refs_0_ = bf16[82,128,128]{2,1,0:T(8,128)(2,1)} custom-call(s32[2]{0:T(128)S(1)} %pad_add_fusion.1.at_ref, s32[3200]{0:T(1024)S(1)} %reshape.133.mask_ref, bf16[640,2560]{1,0:T(8,128)(2,1)} %bitcast.24, bf16[336,640]{1,0:T(8,128)(2,1)S(1)} %bitcast.16), custom_call_target="tpu_custom_call" | custom-call | flops 1 | bytes 1 | tf_op jit(solution)/shard_map/pallas_call | solution.py:210
  33.5 3.8 %shard_map.143 = bf16[3,1280,128]{2,1,0:T(8,128)(2,1)} custom-call(s32[3]{0:T(128)S(1)} %get-tuple-element.108.order_ref, f32[12,1280,128]{2,1,0:T(8,128)} %bitcast.19), custom_call_target="tpu_custom_call" | custom-call | flops 1 | bytes 1 | tf_op jit(solution)/shard_map/pallas_call | solution.py:384
  40.3 4.1 %shard_map.141.refs_0_ = bf16[37,128,128]{2,1,0:T(8,128)(2,1)S(1)} custom-call(s32[2]{0:T(128)S(1)} %pad_add_fusion.1.at_ref, s32[1600]{0:T(1024)S(1)} %reshape.136.mask_ref, bf16[640,1280]{1,0:T(8,128)(2,1)} %x_ref.1), custom_call_target="tpu_custom_call" | custom-call | flops 1 | bytes 1 | tf_op jit(solution)/shard_map/pallas_call | solution.py:210
  49.6 34.1 %collective-permute-done.slots_ref = s32[3]{0:T(128)S(1)} collective-permute-done((s32[3]{0:T(128)S(1)}, s32[3]{0:T(128)S(1)}, u32[]{:S(2)}, u32[]{:S(2)}) %collective-permute-start) | collective-permute-done | bytes 44 | tf_op jit(solution)/shard_map/ppermute | solution.py:709
  93.7 27.6 %collective-permute-done.7.refs_6_ = bf16[41,128,128]{2,1,0:T(8,128)(2,1)S(1)} collective-permute-done((bf16[41,128,128]{2,1,0:T(8,128)(2,1)S(1)}, bf16[41,128,128]{2,1,0:T(8,128)(2,1)S(1)}, u32[]{:S(2)}, u32[]{:S(2)}) %collective-permute-start.7) | collective-permute-done | bytes 1343520 | tf_op jit(solution)/shard_map/ppermute | solution.py:651
  123.8 13.9 %collective-permute-done.12.state_ref = bf16[3,1280,128]{2,1,0:T(8,128)(2,1)S(1)} collective-permute-done((bf16[3,1280,128]{2,1,0:T(8,128)(2,1)S(1)}, bf16[3,1280,128]{2,1,0:T(8,128)(2,1)S(1)}, u32[]{:S(2)}, u32[]{:S(2)}) %collective-permute-start.12) | collective-permute-done | bytes 983072 | tf_op jit(solution)/shard_map/ppermute | solution.py:709
  143.8 26.6 %shard_map.146.total_ref = f32[576,2944]{1,0:T(8,128)} custom-call(s32[3]{0:T(128)} %pad_add_fusion.2.at_ref, s32[920]{0:T(1024)} %reshape.139.table_ref, bf16[576,5120]{1,0:T(8,128)(2,1)} %all-gather.10.cloned.1.call-done.x_ref, bf16[8,34,128,128]{3,2,1,0:T(8,128)(2,1)} %get-tuple-element.66.over_ref, bf16[82,128,128]{2,1,0:T(8,128)(2,1)} %shard_map.140.refs_0_, ...), custom_call_target="tpu_custom_call" | custom-call | flops 1 | bytes 1 | tf_op jit(solution)/shard_map/pallas_call | solution.py:358
  174.6 6.3 %shard_map.147 = (bf16[144,1280]{1,0:T(8,128)(2,1)S(1)}, f32[12,1280,128]{2,1,0:T(8,128)}) custom-call(s32[3]{0:T(128)S(1)} %collective-permute-done.4.slots_ref, f32[576,2944]{1,0:T(8,128)} %shard_map.146.total_ref, bf16[3,1280,128]{2,1,0:T(8,128)(2,1)S(1)} %copy-done.11, f32[8,1280]{1,0:T(8,128)S(1)} %maximum_maximum_fusion.rows_ref, ...), custom_call_target="tpu_custom_call" | custom-call | flops 1 | bytes 1 | tf_op jit(solution)/shard_map/pallas_call | solution.py:482
  181.9 9.6 %shard_map.148 = (bf16[144,5120]{1,0:T(8,128)(2,1)}, bf16[4,1280,1280]{2,1,0:T(8,128)(2,1)}) custom-call(s32[3]{0:T(128)S(1)} %copy-done.17, s32[400]{0:T(512)S(1)} %reshape_reshape.8.table_ref, bf16[144,1280]{1,0:T(8,128)(2,1)S(1)} %get-tuple-element.68.normed_ref, bf16[8,14,128,128]{3,2,1,0:T(8,128)(2,1)S(1)} %copy-done.18, ...), custom_call_target="tpu_custom_call" | custom-call | flops 1 | bytes 1 | tf_op jit(solution)/shard_map/pallas_call | solution.py:571
  200.9 5.0 %shard_map.149 = (bf16[144,5120]{1,0:T(8,128)(2,1)S(1)}, bf16[4,1280,1280]{2,1,0:T(8,128)(2,1)}) custom-call(s32[3]{0:T(128)S(1)} %copy-done.17, s32[400]{0:T(512)S(1)} %reshape_reshape.8.table_ref, bf16[144,1280]{1,0:T(8,128)(2,1)S(1)} %copy-done.5, ...), custom_call_target="tpu_custom_call", output_to_operand_aliasing={{0}: (8, {}), {1}: (9, {})} | custom-call | flops 1 | bytes 1 | tf_op jit(solution)/shard_map/pallas_call | solution.py:571
  210.9 6.2 %collective-permute-done.23.state_ref = bf16[3,1280,128]{2,1,0:T(8,128)(2,1)} collective-permute-done((bf16[3,1280,128]{2,1,0:T(8,128)(2,1)}, bf16[3,1280,128]{2,1,0:T(8,128)(2,1)}, u32[]{:S(2)}, u32[]{:S(2)}) %collective-permute-start.23) | collective-permute-done | bytes 983072 | tf_op jit(solution)/shard_map/ppermute | solution.py:709
  217.1 6.2 %shard_map.150 = (bf16[144,1280]{1,0:T(8,128)(2,1)S(1)}, f32[12,1280,128]{2,1,0:T(8,128)}) custom-call(s32[3]{0:T(128)S(1)} %collective-permute-done.5.slots_ref, f32[576,2944]{1,0:T(8,128)} %shard_map.146.total_ref, bf16[3,1280,128]{2,1,0:T(8,128)(2,1)} %collective-permute-done.23.state_ref, ...), custom_call_target="tpu_custom_call", output_to_operand_aliasing={{1}: (6, {})} | custom-call | flops 1 | bytes 1 | tf_op jit(solution)/shard_map/pallas_call | solution.py:482
  223.3 6.6 %shard_map.151 = bf16[144,5120]{1,0:T(8,128)(2,1)S(1)} custom-call(bf16[144,1280]{1,0:T(8,128)(2,1)S(1)} %get-tuple-element.82.normed_ref, bf16[4,1280,1280]{2,1,0:T(8,128)(2,1)} %get-tuple-element.83.dense_ref), custom_call_target="tpu_custom_call" | custom-call | flops 1 | bytes 1 | tf_op jit(solution)/shard_map/pallas_call | solution.py:604
  234.2 9.0 %collective-permute-done.27 = bf16[144,1280]{1,0:T(8,128)(2,1)S(1)} collective-permute-done((bf16[144,1280]{1,0:T(8,128)(2,1)S(1)}, bf16[144,1280]{1,0:T(8,128)(2,1)S(1)}, u32[]{:S(2)}, u32[]{:S(2)}) %collective-permute-start.27) | collective-permute-done | bytes 368672 | tf_op jit(solution)/shard_map/ppermute | solution.py:779
  243.6 4.8 %collective-permute-done.25.state_ref = bf16[3,1280,128]{2,1,0:T(8,128)(2,1)S(1)} collective-permute-done((bf16[3,1280,128]{2,1,0:T(8,128)(2,1)S(1)}, bf16[3,1280,128]{2,1,0:T(8,128)(2,1)S(1)}, u32[]{:S(2)}, u32[]{:S(2)}) %collective-permute-start.25) | collective-permute-done | bytes 983072 | tf_op jit(solution)/shard_map/ppermute | solution.py:709
  248.4 6.0 %shard_map.152 = (bf16[144,1280]{1,0:T(8,128)(2,1)S(1)}, f32[12,1280,128]{2,1,0:T(8,128)}) custom-call(s32[3]{0:T(128)S(1)} %collective-permute-done.6.slots_ref, f32[576,2944]{1,0:T(8,128)} %shard_map.146.total_ref, bf16[3,1280,128]{2,1,0:T(8,128)(2,1)S(1)} %collective-permute-done.25.state_ref, ...), custom_call_target="tpu_custom_call", output_to_operand_aliasing={{1}: (6, {})} | custom-call | flops 1 | bytes 1 | tf_op jit(solution)/shard_map/pallas_call | solution.py:482
  254.4 6.5 %shard_map.153 = bf16[144,5120]{1,0:T(8,128)(2,1)S(1)} custom-call(bf16[144,1280]{1,0:T(8,128)(2,1)S(1)} %get-tuple-element.87.normed_ref, bf16[4,1280,1280]{2,1,0:T(8,128)(2,1)} %get-tuple-element.83.dense_ref), custom_call_target="tpu_custom_call" | custom-call | flops 1 | bytes 1 | tf_op jit(solution)/shard_map/pallas_call | solution.py:604
  266.0 6.0 %shard_map.154 = (bf16[144,1280]{1,0:T(8,128)(2,1)S(1)}, f32[12,1280,128]{2,1,0:T(8,128)}) custom-call(s32[3]{0:T(128)S(1)} %collective-permute-done.slots_ref, f32[576,2944]{1,0:T(8,128)} %shard_map.146.total_ref, bf16[3,1280,128]{2,1,0:T(8,128)(2,1)S(1)} %collective-permute-done.28.state_ref, ...), custom_call_target="tpu_custom_call", output_to_operand_aliasing={{1}: (6, {})} | custom-call | flops 1 | bytes 1 | tf_op jit(solution)/shard_map/pallas_call | solution.py:482
  272.0 6.5 %shard_map.155 = bf16[144,5120]{1,0:T(8,128)(2,1)S(1)} custom-call(bf16[144,1280]{1,0:T(8,128)(2,1)S(1)} %get-tuple-element.91.normed_ref, bf16[4,1280,1280]{2,1,0:T(8,128)(2,1)} %get-tuple-element.83.dense_ref), custom_call_target="tpu_custom_call" | custom-call | flops 1 | bytes 1 | tf_op jit(solution)/shard_map/pallas_call | solution.py:604
  280.5 17.5 %collective-permute-done.29 = bf16[144,1280]{1,0:T(8,128)(2,1)S(1)} collective-permute-done((bf16[144,1280]{1,0:T(8,128)(2,1)S(1)}, bf16[144,1280]{1,0:T(8,128)(2,1)S(1)}, u32[]{:S(2)}, u32[]{:S(2)}) %collective-permute-start.29) | collective-permute-done | bytes 368672 | tf_op jit(solution)/shard_map/ppermute | solution.py:779
  300.3 5.6 %collective-permute-done.33 = bf16[144,1280]{1,0:T(8,128)(2,1)S(1)} collective-permute-done((bf16[144,1280]{1,0:T(8,128)(2,1)S(1)}, bf16[144,1280]{1,0:T(8,128)(2,1)S(1)}, u32[]{:S(2)}, u32[]{:S(2)}) %collective-permute-start.33) | collective-permute-done | bytes 368672 | tf_op jit(solution)/shard_map/ppermute | solution.py:786
  308.0 5.8 %collective-permute-done.30 = bf16[144,1280]{1,0:T(8,128)(2,1)S(1)} collective-permute-done((bf16[144,1280]{1,0:T(8,128)(2,1)S(1)}, bf16[144,1280]{1,0:T(8,128)(2,1)S(1)}, u32[]{:S(2)}, u32[]{:S(2)}) %collective-permute-start.30) | collective-permute-done | bytes 368672 | tf_op jit(solution)/shard_map/ppermute | solution.py:786
  314.0 7.7 %collective-permute-done.34 = bf16[144,1280]{1,0:T(8,128)(2,1)S(1)} collective-permute-done((bf16[144,1280]{1,0:T(8,128)(2,1)S(1)}, bf16[144,1280]{1,0:T(8,128)(2,1)S(1)}, u32[]{:S(2)}, u32[]{:S(2)}) %collective-permute-start.34) | collective-permute-done | bytes 368672 | tf_op jit(solution)/shard_map/ppermute | solution.py:786
  (210 shorter events, 85.8 us)
Async XLA Ops:
  7.2 135.8 %all-gather.10.cloned.1.call-start = ((), (), s32[]{:S(2)}) async-start(), calls=%async_computation.2 | async-start | bytes 7372800 | tf_op jit(solution)/shard_map/all_gather | solution.py:694
  20.0 68.1 %collective-permute-start.3 = (bf16[82,128,128]{2,1,0:T(8,128)(2,1)}, bf16[82,128,128]{2,1,0:T(8,128)(2,1)}, u32[]{:S(2)}, u32[]{:S(2)}) collective-permute-start(bf16[82,128,128]{2,1,0:T(8,128)(2,1)} %shard_map.140.refs_0_), channel_id=1, source_target_pairs={{0,4},{4,0},{8,12},{12,8},{16,20},{20,16},{24,28},{28,24},{1,5},{5... | collective-permute-start | bytes 8060936 | tf_op jit(solution)/shard_map/ppermute | solution.py:651
  20.5 67.7 %collective-permute-start.1 = (bf16[82,128,128]{2,1,0:T(8,128)(2,1)}, bf16[82,128,128]{2,1,0:T(8,128)(2,1)}, u32[]{:S(2)}, u32[]{:S(2)}) collective-permute-start(bf16[82,128,128]{2,1,0:T(8,128)(2,1)} %shard_map.140.refs_0_), channel_id=1, source_target_pairs={{0,8},{4,12},{8,0},{12,4},{16,24},{20,28},{24,16},{28,20},{1,9},{5... | collective-permute-start | bytes 8060936 | tf_op jit(solution)/shard_map/ppermute | solution.py:651
  23.0 65.2 %collective-permute-start.2 = (bf16[82,128,128]{2,1,0:T(8,128)(2,1)}, bf16[82,128,128]{2,1,0:T(8,128)(2,1)}, u32[]{:S(2)}, u32[]{:S(2)}) collective-permute-start(bf16[82,128,128]{2,1,0:T(8,128)(2,1)} %shard_map.140.refs_0_), channel_id=1, source_target_pairs={{0,16},{4,20},{8,24},{12,28},{16,0},{20,4},{24,8},{28,12},{1,17},{... | collective-permute-start | bytes 8060936 | tf_op jit(solution)/shard_map/ppermute | solution.py:651
  25.3 58.4 %collective-permute-start = (s32[3]{0:T(128)S(1)}, s32[3]{0:T(128)S(1)}, u32[]{:S(2)}, u32[]{:S(2)}) collective-permute-start(s32[3]{0:T(128)S(1)} %get-tuple-element.98), channel_id=1, source_target_pairs={{0,16},{4,20},{8,24},{12,28},{16,0},{20,4},{24,8},{28,12},{1,17},{... | collective-permute-start | bytes 44 | tf_op jit(solution)/shard_map/ppermute | solution.py:709
  25.9 58.2 %collective-permute-start.4 = (s32[3]{0:T(128)S(1)}, s32[3]{0:T(128)S(1)}, u32[]{:S(2)}, u32[]{:S(2)}) collective-permute-start(s32[3]{0:T(128)S(1)} %get-tuple-element.97), channel_id=1, source_target_pairs={{0,4},{4,8},{8,12},{12,16},{16,20},{20,24},{24,28},{28,0},{1,5},{5... | collective-permute-start | bytes 44 | tf_op jit(solution)/shard_map/ppermute | solution.py:709
  89.6 31.7 %collective-permute-start.7 = (bf16[41,128,128]{2,1,0:T(8,128)(2,1)S(1)}, bf16[41,128,128]{2,1,0:T(8,128)(2,1)S(1)}, u32[]{:S(2)}, u32[]{:S(2)}) collective-permute-start(bf16[41,128,128]{2,1,0:T(8,128)(2,1)S(1)} %slice.44), channel_id=1, source_target_pairs={{0,8},{4,12},{8,0},{12,4},{16,24},{20,28},{24,16},{28,20},{1,9},{5... | collective-permute-start | bytes 4030472 | tf_op jit(solution)/shard_map/ppermute | solution.py:651
  92.6 30.7 %collective-permute-start.8 = (bf16[41,128,128]{2,1,0:T(8,128)(2,1)S(1)}, bf16[41,128,128]{2,1,0:T(8,128)(2,1)S(1)}, u32[]{:S(2)}, u32[]{:S(2)}) collective-permute-start(bf16[41,128,128]{2,1,0:T(8,128)(2,1)S(1)} %slice.45), channel_id=1, source_target_pairs={{0,16},{4,20},{8,24},{12,28},{16,0},{20,4},{24,8},{28,12},{1,17},{... | collective-permute-start | bytes 4030472 | tf_op jit(solution)/shard_map/ppermute | solution.py:651
  93.2 50.6 %collective-permute-start.13 = (bf16[82,128,128]{2,1,0:T(8,128)(2,1)}, bf16[82,128,128]{2,1,0:T(8,128)(2,1)}, u32[]{:S(2)}, u32[]{:S(2)}) collective-permute-start(bf16[82,128,128]{2,1,0:T(8,128)(2,1)} %collective-permute-done.1.refs_2_), channel_id=1, source_target_pairs={{0,4},{4,0},{8,12},{12,8},{16,20},{20,16},{24,28},{28,24},{1,5},{5... | collective-permute-start | bytes 8060936 | tf_op jit(solution)/shard_map/ppermute | solution.py:651
  93.2 50.6 %collective-permute-start.14 = (bf16[82,128,128]{2,1,0:T(8,128)(2,1)}, bf16[82,128,128]{2,1,0:T(8,128)(2,1)}, u32[]{:S(2)}, u32[]{:S(2)}) collective-permute-start(bf16[82,128,128]{2,1,0:T(8,128)(2,1)} %collective-permute-done.2.refs_4_), channel_id=1, source_target_pairs={{0,4},{4,0},{8,12},{12,8},{16,20},{20,16},{24,28},{28,24},{1,5},{5... | collective-permute-start | bytes 8060936 | tf_op jit(solution)/shard_map/ppermute | solution.py:651
  138.7 31.7 %collective-permute-start.10 = (bf16[37,128,128]{2,1,0:T(8,128)(2,1)S(1)}, bf16[37,128,128]{2,1,0:T(8,128)(2,1)S(1)}, u32[]{:S(2)}, u32[]{:S(2)}) collective-permute-start(bf16[37,128,128]{2,1,0:T(8,128)(2,1)S(1)} %shard_map.141.refs_0_), channel_id=1, source_target_pairs={{0,8},{4,12},{8,0},{12,4},{16,24},{20,28},{24,16},{28,20},{1,9},{5... | collective-permute-start | bytes 3637256 | tf_op jit(solution)/shard_map/ppermute | solution.py:651
  139.0 31.4 %collective-permute-start.11 = (bf16[37,128,128]{2,1,0:T(8,128)(2,1)S(1)}, bf16[37,128,128]{2,1,0:T(8,128)(2,1)}, u32[]{:S(2)}, u32[]{:S(2)}) collective-permute-start(bf16[37,128,128]{2,1,0:T(8,128)(2,1)S(1)} %shard_map.141.refs_0_), channel_id=1, source_target_pairs={{0,16},{4,20},{8,24},{12,28},{16,0},{20,4},{24,8},{28,12},{1,17},{... | collective-permute-start | bytes 3637256 | tf_op jit(solution)/shard_map/ppermute | solution.py:651
  140.6 29.9 %collective-permute-start.9 = (bf16[37,128,128]{2,1,0:T(8,128)(2,1)S(1)}, bf16[37,128,128]{2,1,0:T(8,128)(2,1)}, u32[]{:S(2)}, u32[]{:S(2)}) collective-permute-start(bf16[37,128,128]{2,1,0:T(8,128)(2,1)S(1)} %shard_map.141.refs_0_), channel_id=1, source_target_pairs={{0,4},{4,0},{8,12},{12,8},{16,20},{20,16},{24,28},{28,24},{1,5},{5... | collective-permute-start | bytes 3637256 | tf_op jit(solution)/shard_map/ppermute | solution.py:651
  171.1 20.5 %collective-permute-start.18 = (bf16[19,128,128]{2,1,0:T(8,128)(2,1)S(1)}, bf16[19,128,128]{2,1,0:T(8,128)(2,1)}, u32[]{:S(2)}, u32[]{:S(2)}) collective-permute-start(bf16[19,128,128]{2,1,0:T(8,128)(2,1)S(1)} %slice.47), channel_id=1, source_target_pairs={{0,16},{4,20},{8,24},{12,28},{16,0},{20,4},{24,8},{28,12},{1,17},{... | collective-permute-start | bytes 1867784 | tf_op jit(solution)/shard_map/ppermute | solution.py:651
  191.6 25.5 %collective-permute-start.23 = (bf16[3,1280,128]{2,1,0:T(8,128)(2,1)}, bf16[3,1280,128]{2,1,0:T(8,128)(2,1)}, u32[]{:S(2)}, u32[]{:S(2)}) collective-permute-start(bf16[3,1280,128]{2,1,0:T(8,128)(2,1)} %shard_map.143), channel_id=1, source_target_pairs={{0,8},{4,12},{8,16},{12,20},{16,24},{20,28},{24,0},{28,4},{1,9},{5... | collective-permute-start | bytes 2949128 | tf_op jit(solution)/shard_map/ppermute | solution.py:709
  207.0 24.5 %collective-permute-start.24 = (bf16[144,1280]{1,0:T(8,128)(2,1)S(1)}, bf16[144,1280]{1,0:T(8,128)(2,1)}, u32[]{:S(2)}, u32[]{:S(2)}) collective-permute-start(bf16[144,1280]{1,0:T(8,128)(2,1)S(1)} %constant_dynamic-slice_fusion.3), channel_id=1, source_target_pairs={{0,1},{1,2},{2,3},{3,0},{4,5},{5,6},{6,7},{7,4},{8,9},{9,10},{10,1... | collective-permute-start | bytes 1105928 | tf_op jit(solution)/shard_map/ppermute | solution.py:779
  208.7 39.7 %collective-permute-start.25 = (bf16[3,1280,128]{2,1,0:T(8,128)(2,1)S(1)}, bf16[3,1280,128]{2,1,0:T(8,128)(2,1)S(1)}, u32[]{:S(2)}, u32[]{:S(2)}) collective-permute-start(bf16[3,1280,128]{2,1,0:T(8,128)(2,1)S(1)} %copy-done.9), channel_id=1, source_target_pairs={{0,12},{4,16},{8,20},{12,24},{16,28},{20,0},{24,4},{28,8},{1,13},{... | collective-permute-start | bytes 2949128 | tf_op jit(solution)/shard_map/ppermute | solution.py:709
  209.5 56.5 %collective-permute-start.28 = (bf16[3,1280,128]{2,1,0:T(8,128)(2,1)S(1)}, bf16[3,1280,128]{2,1,0:T(8,128)(2,1)S(1)}, u32[]{:S(2)}, u32[]{:S(2)}) collective-permute-start(bf16[3,1280,128]{2,1,0:T(8,128)(2,1)S(1)} %copy-done.7), channel_id=1, source_target_pairs={{0,16},{4,20},{8,24},{12,28},{16,0},{20,4},{24,8},{28,12},{1,17},{... | collective-permute-start | bytes 2949128 | tf_op jit(solution)/shard_map/ppermute | solution.py:709
  232.6 29.9 %collective-permute-start.26 = (bf16[144,1280]{1,0:T(8,128)(2,1)S(1)}, bf16[144,1280]{1,0:T(8,128)(2,1)S(1)}, u32[]{:S(2)}, u32[]{:S(2)}) collective-permute-start(bf16[144,1280]{1,0:T(8,128)(2,1)S(1)} %add_convert_fusion.12), channel_id=1, source_target_pairs={{0,1},{1,2},{2,3},{3,0},{4,5},{5,6},{6,7},{7,4},{8,9},{9,10},{10,1... | collective-permute-start | bytes 1105928 | tf_op jit(solution)/shard_map/ppermute | solution.py:786
  243.4 20.9 %collective-permute-start.35 = (bf16[144,1280]{1,0:T(8,128)(2,1)S(1)}, bf16[144,1280]{1,0:T(8,128)(2,1)S(1)}, u32[]{:S(2)}, u32[]{:S(2)}) collective-permute-start(bf16[144,1280]{1,0:T(8,128)(2,1)S(1)} %add_convert_fusion.10), channel_id=1, source_target_pairs={{0,1},{1,2},{2,3},{3,0},{4,5},{5,6},{6,7},{7,4},{8,9},{9,10},{10,1... | collective-permute-start | bytes 1105928 | tf_op jit(solution)/shard_map/ppermute | solution.py:786
  262.6 35.5 %collective-permute-start.37 = (bf16[144,1280]{1,0:T(8,128)(2,1)S(1)}, bf16[144,1280]{1,0:T(8,128)(2,1)S(1)}, u32[]{:S(2)}, u32[]{:S(2)}) collective-permute-start(bf16[144,1280]{1,0:T(8,128)(2,1)S(1)} %add_convert_fusion.11), channel_id=1, source_target_pairs={{0,1},{1,2},{2,3},{3,0},{4,5},{5,6},{6,7},{7,4},{8,9},{9,10},{10,1... | collective-permute-start | bytes 1105928 | tf_op jit(solution)/shard_map/ppermute | solution.py:786
  264.4 35.8 %collective-permute-start.36 = (bf16[144,1280]{1,0:T(8,128)(2,1)S(1)}, bf16[144,1280]{1,0:T(8,128)(2,1)S(1)}, u32[]{:S(2)}, u32[]{:S(2)}) collective-permute-start(bf16[144,1280]{1,0:T(8,128)(2,1)S(1)} %add_convert_fusion.3), channel_id=1, source_target_pairs={{0,1},{1,2},{2,3},{3,0},{4,5},{5,6},{6,7},{7,4},{8,9},{9,10},{10,1... | collective-permute-start | bytes 1105928 | tf_op jit(solution)/shard_map/ppermute | solution.py:786
  278.5 19.5 %collective-permute-start.29 = (bf16[144,1280]{1,0:T(8,128)(2,1)S(1)}, bf16[144,1280]{1,0:T(8,128)(2,1)S(1)}, u32[]{:S(2)}, u32[]{:S(2)}) collective-permute-start(bf16[144,1280]{1,0:T(8,128)(2,1)S(1)} %constant_dynamic-slice_fusion.1), channel_id=1, source_target_pairs={{0,1},{1,2},{2,3},{3,0},{4,5},{5,6},{6,7},{7,4},{8,9},{9,10},{10,1... | collective-permute-start | bytes 1105928 | tf_op jit(solution)/shard_map/ppermute | solution.py:779
  278.9 27.0 %collective-permute-start.33 = (bf16[144,1280]{1,0:T(8,128)(2,1)S(1)}, bf16[144,1280]{1,0:T(8,128)(2,1)S(1)}, u32[]{:S(2)}, u32[]{:S(2)}) collective-permute-start(bf16[144,1280]{1,0:T(8,128)(2,1)S(1)} %add_convert_fusion.6), channel_id=1, source_target_pairs={{0,1},{1,2},{2,3},{3,0},{4,5},{5,6},{6,7},{7,4},{8,9},{9,10},{10,1... | collective-permute-start | bytes 1105928 | tf_op jit(solution)/shard_map/ppermute | solution.py:786
  (46 other events, 350.4 us)
Sparse Core Ops, SparseCore 0:
  10.9 111.5 all-gather.9
